TPU v7x, 32 devices: a whole 2x2x4 slice. The times are simulated.
32 devices in a mesh: dp: 8 (over y, x, core), tensor: 4 (over z).
Axes of the slice: x: 2, y: 2, z: 4, core: 2. Of those that a mesh axis runs over, the one named last changes fastest.
Arguments:
- tokens: bfloat16 [16384, 512], P(('dp', 'tensor')), may hold values from -6 to 6
- cotangent: bfloat16 [16384, 512], P(('dp', 'tensor')), may hold values from -6 to 6
- clip_lengths: int32 [8, 4], P('dp'), may hold values from 0 to 2048, as said below
- w_qkv: bfloat16 [2, 3, 512, 512], P(None, None, None, 'tensor'), may hold values from -0.25 to 0.25
- b_qv: bfloat16 [2, 2, 512], P(None, None, 'tensor'), may hold values from -1.5 to 1.5
- w_out: bfloat16 [2, 512, 512], P(None, 'tensor'), may hold values from -2 to 2
- b_out: bfloat16 [2, 512], replicated, may hold values from -1.5 to 1.5
- w_up: bfloat16 [2, 512, 2048], P(None, None, 'tensor'), may hold values from -0.25 to 0.25
- b_up: bfloat16 [2, 2048], P(None, 'tensor'), may hold values from -1.5 to 1.5
- w_down: bfloat16 [2, 2048, 512], P(None, 'tensor'), may hold values from -0.25 to 0.25
- b_down: bfloat16 [2, 512], replicated, may hold values from -1.5 to 1.5
- ln_gain: bfloat16 [2, 2, 512], replicated, may hold values from 0.5 to 1.5
- ln_bias: bfloat16 [2, 2, 512], replicated, may hold values from -1.5 to 1.5
Outputs:
- output: bfloat16 [16384, 512], P(('dp', 'tensor'))
- grad_tokens: bfloat16 [16384, 512], P(('dp', 'tensor'))
- grad_w_qkv: float32 [2, 3, 512, 512], P(None, None, None, 'tensor')
- grad_b_qv: float32 [2, 2, 512], P(None, None, 'tensor')
- grad_w_out: float32 [2, 512, 512], P(None, 'tensor')
- grad_b_out: float32 [2, 512], replicated
- grad_w_up: float32 [2, 512, 2048], P(None, None, 'tensor')
- grad_b_up: float32 [2, 2048], P(None, 'tensor')
- grad_w_down: float32 [2, 2048, 512], P(None, 'tensor')
- grad_b_down: float32 [2, 512], replicated
- grad_ln_gain: float32 [2, 2, 512], replicated
- grad_ln_bias: float32 [2, 2, 512], replicated
Inputs may be any that keep to these rules, and one draw needn't show every extreme that they name: `clip_lengths`: each row lists the clips of one slot of 2048 tokens in order: either one clip of 2048 tokens and three zeros, or four clips of 512 tokens each; every draw has rows of both kinds.
All inputs are finite; a program needn't handle non-finite values.
Results may differ from a plain program's by a relative error of at most 0.02.
Values may be sent and summed in bfloat16 or wider, within the bound.
A program may use at most 192 MiB of HBM per device.

v0:
```python
import jax
import jax.numpy as jnp
from jax import lax
from jax.sharding import PartitionSpec as P

HEAD_DIM = 64


EPSILON = 1e-05


def layer_norm(values, gain_row, bias_row):
    average = jnp.mean(values, axis=-1, keepdims=True)
    centered = values - average
    variance = jnp.mean(centered * centered, axis=-1, keepdims=True)
    return centered * lax.rsqrt(variance + EPSILON) * gain_row + bias_row


def gelu_act(values):
    return jax.nn.gelu(values, approximate=False)


def clip_ids(clip_lengths, slot_len):
    positions = jnp.arange(slot_len, dtype=jnp.int32)
    clip_ends = jnp.cumsum(clip_lengths, axis=-1)
    return jnp.sum((positions[None, :, None] >= clip_ends[:, None, :]).astype(jnp.int32), axis=-1)


def spread_rows(values):
    return lax.all_gather(values, "tensor", axis=0, tiled=True)


def spread_grads(values):
    return lax.all_gather(values, "tensor", axis=0, tiled=True)


def branch_total(left_side, right_side):
    return lax.psum_scatter(
        jnp.dot(left_side, right_side, preferred_element_type=jnp.float32).astype(jnp.bfloat16),
        "tensor",
        scatter_dimension=0,
        tiled=True,
    ).astype(jnp.float32)


def input_total(left_side, right_side):
    return lax.psum_scatter(
        jnp.einsum("se,de->sd", left_side, right_side, preferred_element_type=jnp.float32).astype(
            jnp.bfloat16
        ),
        "tensor",
        scatter_dimension=0,
        tiled=True,
    ).astype(jnp.float32)


def reduce_grads(local_grads, shared_grads):
    summed_local = lax.psum(
        (
            local_grads[0],
            local_grads[1],
            local_grads[2],
            local_grads[3],
            local_grads[4],
            local_grads[5],
        ),
        "dp",
    )
    summed_shared = lax.psum(
        (shared_grads[0], shared_grads[1], shared_grads[2], shared_grads[3]), ("dp", "tensor")
    )
    return (summed_local, summed_shared)


def stack_layers(*pieces):
    return jnp.stack(pieces)


def shards(
    tokens,
    cotangent,
    clip_lengths,
    w_qkv,
    b_qv,
    w_out,
    b_out,
    w_up,
    b_up,
    w_down,
    b_down,
    ln_gain,
    ln_bias,
):
    row_total = tokens.shape[0]
    model_width = tokens.shape[1]
    slot_len = row_total * lax.axis_size("tensor")
    block_rows = min(512, slot_len)
    block_count = slot_len // block_rows
    positions = jnp.arange(slot_len, dtype=jnp.int32)
    segment = clip_ids(clip_lengths, slot_len)[0]
    local_dim = w_qkv.shape[3]
    heads_here = local_dim // HEAD_DIM
    score_scale = HEAD_DIM ** (-0.5)
    layer_count = w_qkv.shape[0]

    def block_scores(query_rows, key_rows, blk_index):
        row_first = blk_index * block_rows
        key_end = row_first + block_rows
        query_blk = query_rows[row_first:key_end]
        scores = (
            jnp.einsum(
                "qhd,khd->hqk", query_blk, key_rows[:key_end], preferred_element_type=jnp.float32
            )
            * score_scale
        )
        allowed = (segment[row_first:key_end][:, None] == segment[None, :key_end]) & (
            positions[None, :key_end] <= positions[row_first:key_end][:, None]
        )
        return (jnp.where(allowed[None], scores, -1e30), query_blk)

    def joined_qkv(layer_at):
        return jnp.transpose(w_qkv[layer_at], (1, 0, 2)).reshape(model_width, 3 * local_dim)

    stream = tokens.astype(jnp.float32)
    stored = []
    for layer_at in range(layer_count):
        stream_in = stream
        gains = ln_gain[layer_at].astype(jnp.float32)
        shifts = ln_bias[layer_at].astype(jnp.float32)
        attn_in = layer_norm(stream, gains[0], shifts[0]).astype(jnp.bfloat16)
        gathered = spread_rows(attn_in)
        projected = jnp.dot(gathered, joined_qkv(layer_at), preferred_element_type=jnp.float32)
        proj_bias = b_qv[layer_at].astype(jnp.float32)
        head_shape = (slot_len, heads_here, HEAD_DIM)
        query_rows = (
            (projected[:, :local_dim] + proj_bias[0]).astype(jnp.bfloat16).reshape(head_shape)
        )
        key_rows = projected[:, local_dim : 2 * local_dim].astype(jnp.bfloat16).reshape(head_shape)
        value_rows = (
            (projected[:, 2 * local_dim :] + proj_bias[1]).astype(jnp.bfloat16).reshape(head_shape)
        )
        peak_list, total_list, attended_list = ([], [], [])
        for blk_index in range(block_count):
            key_end = (blk_index + 1) * block_rows
            scores, query_blk = block_scores(query_rows, key_rows, blk_index)
            row_peak = jnp.max(scores, axis=-1, keepdims=True)
            exponent = jnp.exp(scores - row_peak)
            exp_total = jnp.sum(exponent, axis=-1, keepdims=True)
            probability = (exponent / exp_total).astype(jnp.bfloat16)
            attended_list.append(
                jnp.einsum(
                    "hqk,khd->qhd",
                    probability,
                    value_rows[:key_end],
                    preferred_element_type=jnp.float32,
                )
            )
            peak_list.append(row_peak)
            total_list.append(exp_total)
        attended = (
            jnp.concatenate(attended_list, axis=0).astype(jnp.bfloat16).reshape(slot_len, local_dim)
        )
        branch = branch_total(attended, w_out[layer_at])
        mid_stream = stream + branch + b_out[layer_at].astype(jnp.float32)
        mlp_in = layer_norm(mid_stream, gains[1], shifts[1]).astype(jnp.bfloat16)
        gathered_mlp = spread_rows(mlp_in)
        pre_act = jnp.dot(gathered_mlp, w_up[layer_at], preferred_element_type=jnp.float32) + b_up[
            layer_at
        ].astype(jnp.float32)
        hidden = gelu_act(pre_act).astype(jnp.bfloat16)
        mlp_out = branch_total(hidden, w_down[layer_at])
        mlp_keep = (gathered_mlp, w_up[layer_at], w_down[layer_at])
        stream = mid_stream + mlp_out + b_down[layer_at].astype(jnp.float32)
        stored.append(
            (
                stream_in,
                gathered,
                query_rows,
                key_rows,
                value_rows,
                peak_list,
                total_list,
                attended,
                mid_stream,
                mlp_keep,
                pre_act,
                hidden,
            )
        )
    output = stream.astype(jnp.bfloat16)
    grad_stream = cotangent.astype(jnp.float32)
    local_list = []
    shared_list = []
    for layer_at in reversed(range(layer_count)):
        (
            stream_in,
            gathered,
            query_rows,
            key_rows,
            value_rows,
            peak_list,
            total_list,
            attended,
            mid_stream,
            mlp_keep,
            pre_act,
            hidden,
        ) = stored[layer_at]
        mlp_rows, up_used, down_used = mlp_keep
        gains = ln_gain[layer_at].astype(jnp.float32)
        shifts = ln_bias[layer_at].astype(jnp.float32)
        gelu_pull = jax.vjp(gelu_act, pre_act)[1]
        grad_bdown = jnp.sum(grad_stream, axis=0)
        grad_out_all = spread_grads(grad_stream.astype(jnp.bfloat16))
        grad_wdown = jnp.einsum(
            "sf,sd->fd", hidden, grad_out_all, preferred_element_type=jnp.float32
        )
        grad_hidden = jnp.einsum(
            "sd,fd->sf", grad_out_all, down_used, preferred_element_type=jnp.float32
        )
        grad_pre = gelu_pull(grad_hidden)[0].astype(jnp.bfloat16)
        grad_wup = jnp.einsum("sd,sf->df", mlp_rows, grad_pre, preferred_element_type=jnp.float32)
        grad_bup = jnp.sum(grad_pre.astype(jnp.float32), axis=0)
        grad_mlp_in = input_total(grad_pre, up_used)
        second_pull = jax.vjp(layer_norm, mid_stream, gains[1], shifts[1])[1]
        grad_mid, grad_gain_two, grad_bias_two = second_pull(grad_mlp_in)
        grad_mid = grad_mid + grad_stream
        grad_bout = jnp.sum(grad_mid, axis=0)
        grad_branch_all = spread_grads(grad_mid.astype(jnp.bfloat16))
        grad_wout = jnp.einsum(
            "se,sd->ed", attended, grad_branch_all, preferred_element_type=jnp.float32
        )
        grad_att = jnp.einsum(
            "sd,ed->se", grad_branch_all, w_out[layer_at], preferred_element_type=jnp.float32
        )
        grad_att = grad_att.astype(jnp.bfloat16).reshape(slot_len, heads_here, HEAD_DIM)
        grad_keys = jnp.zeros((slot_len, heads_here, HEAD_DIM), jnp.float32)
        grad_values = jnp.zeros((slot_len, heads_here, HEAD_DIM), jnp.float32)
        grad_query_list = []
        for blk_index in range(block_count):
            row_first = blk_index * block_rows
            key_end = row_first + block_rows
            scores, query_blk = block_scores(query_rows, key_rows, blk_index)
            probability = jnp.exp(scores - peak_list[blk_index]) / total_list[blk_index]
            grad_blk = grad_att[row_first:key_end]
            grad_probs = jnp.einsum(
                "qhd,khd->hqk", grad_blk, value_rows[:key_end], preferred_element_type=jnp.float32
            )
            inner_sum = jnp.sum(probability * grad_probs, axis=-1, keepdims=True)
            grad_scores = (probability * (grad_probs - inner_sum)).astype(jnp.bfloat16)
            grad_query_list.append(
                jnp.einsum(
                    "hqk,khd->qhd",
                    grad_scores,
                    key_rows[:key_end],
                    preferred_element_type=jnp.float32,
                )
                * score_scale
            )
            grad_keys = grad_keys.at[:key_end].add(
                jnp.einsum(
                    "hqk,qhd->khd", grad_scores, query_blk, preferred_element_type=jnp.float32
                )
                * score_scale
            )
            grad_values = grad_values.at[:key_end].add(
                jnp.einsum(
                    "hqk,qhd->khd",
                    probability.astype(jnp.bfloat16),
                    grad_blk,
                    preferred_element_type=jnp.float32,
                )
            )
        grad_queries = jnp.concatenate(grad_query_list, axis=0).reshape(slot_len, local_dim)
        grad_qkv = jnp.concatenate(
            [
                grad_queries,
                grad_keys.reshape(slot_len, local_dim),
                grad_values.reshape(slot_len, local_dim),
            ],
            axis=1,
        ).astype(jnp.bfloat16)
        grad_wqkv = jnp.einsum("sd,se->de", gathered, grad_qkv, preferred_element_type=jnp.float32)
        grad_wqkv = jnp.transpose(grad_wqkv.reshape(model_width, 3, local_dim), (1, 0, 2))
        grad_bqv = jnp.stack(
            [
                jnp.sum(grad_qkv[:, :local_dim].astype(jnp.float32), axis=0),
                jnp.sum(grad_qkv[:, 2 * local_dim :].astype(jnp.float32), axis=0),
            ]
        )
        grad_attn_in = input_total(grad_qkv, joined_qkv(layer_at))
        first_pull = jax.vjp(layer_norm, stream_in, gains[0], shifts[0])[1]
        grad_in, grad_gain_one, grad_bias_one = first_pull(grad_attn_in)
        grad_stream = grad_in + grad_mid
        local_grads = (grad_wqkv, grad_bqv, grad_wout, grad_wup, grad_bup, grad_wdown)
        shared_grads = (
            grad_bout,
            grad_bdown,
            jnp.stack([grad_gain_one, grad_gain_two]),
            jnp.stack([grad_bias_one, grad_bias_two]),
        )
        local_grads, shared_grads = reduce_grads(local_grads, shared_grads)
        local_list.append(local_grads)
        shared_list.append(shared_grads)
    local_list = local_list[::-1]
    shared_list = shared_list[::-1]
    local_stack = jax.tree.map(stack_layers, *local_list)
    shared_stack = jax.tree.map(stack_layers, *shared_list)
    return (
        output,
        grad_stream.astype(jnp.bfloat16),
        local_stack[0],
        local_stack[1],
        local_stack[2],
        shared_stack[0],
        local_stack[3],
        local_stack[4],
        local_stack[5],
        shared_stack[1],
        shared_stack[2],
        shared_stack[3],
    )


def solution(mesh):
    in_specs = (
        P(("dp", "tensor"), None),
        P(("dp", "tensor"), None),
        P("dp", None),
        P(None, None, None, "tensor"),
        P(None, None, "tensor"),
        P(None, "tensor", None),
        P(),
        P(None, None, "tensor"),
        P(None, "tensor"),
        P(None, "tensor", None),
        P(),
        P(),
        P(),
    )
    out_specs = (
        P(("dp", "tensor"), None),
        P(("dp", "tensor"), None),
        P(None, None, None, "tensor"),
        P(None, None, "tensor"),
        P(None, "tensor", None),
        P(),
        P(None, None, "tensor"),
        P(None, "tensor"),
        P(None, "tensor", None),
        P(),
        P(),
        P(),
    )
    return jax.shard_map(shards, mesh=mesh, in_specs=in_specs, out_specs=out_specs, check_vma=False)
```

profile of v0, /device:TPU:0, one launch (start us, length us, event | category | flops | bytes accessed | tf_op | source)
XLA Modules:
  0.0 1157.4 jit_solution(4523890381655496849)
XLA Ops:
  22.1 40.7 %all-gather.9.cloned.1.call-done = bf16[2048,512]{1,0:T(8,128)(2,1)} async-done(((bf16[512,512]{1,0:T(8,128)(2,1)}), bf16[2048,512]{1,0:T(8,128)(2,1)}) %all-gather.9.cloned.1.call-update) | async-done | bytes 2097168 | tf_op jit(solution)/shard_map/all_gather | solution.py:30
  106.9 42.6 %reduce-scatter.9.cloned.1.call-done = bf16[512,512]{1,0:T(8,128)(2,1)} async-done(((bf16[2048,512]{1,0:T(8,128)(2,1)}), bf16[512,512]{1,0:T(8,128)(2,1)}) %reduce-scatter.9.cloned.1.call-update) | async-done | bytes 524304 | tf_op jit(solution)/shard_map/reduce_scatter | solution.py:38
  155.0 44.8 %all-gather.11.cloned.1.call-done = bf16[2048,512]{1,0:T(8,128)(2,1)} async-done(((bf16[512,512]{1,0:T(8,128)(2,1)}), bf16[2048,512]{1,0:T(8,128)(2,1)}) %all-gather.11.cloned.1.call-update) | async-done | bytes 2097168 | tf_op jit(solution)/shard_map/all_gather | solution.py:30
  199.8 12.9 %multiply_convert_fusion.7 = (bf16[2048,512]{1,0:T(8,128)(2,1)S(1)}, f32[2048,512]{1,0:T(8,128)}, f32[2048,512]{1,0:T(8,128)}) fusion(f32[512]{0:T(512)S(1)} %bitcast.612, bf16[2048,512]{1,0:T(8,128)(2,1)} %all-gather.11.cloned.1.call-done, bf16[2,512,512]{2,1,0:T(8,128)(2,1)S(1)} %copy-done.167), kind=kOutput, calls=%fused_computation.56 | convolution fusion | flops 1142947840 | bytes 13109248 | tf_op jit(solution)/shard_map/dot_general | solution.py:167
  217.2 42.1 %reduce-scatter.11.cloned.1.call-done = bf16[512,512]{1,0:T(8,128)(2,1)} async-done(((bf16[2048,512]{1,0:T(8,128)(2,1)}), bf16[512,512]{1,0:T(8,128)(2,1)}) %reduce-scatter.11.cloned.1.call-update) | async-done | bytes 524304 | tf_op jit(solution)/shard_map/reduce_scatter | solution.py:38
  262.8 44.7 %all-gather.13.cloned.1.call-done = bf16[2048,512]{1,0:T(8,128)(2,1)} async-done(((bf16[512,512]{1,0:T(8,128)(2,1)}), bf16[2048,512]{1,0:T(8,128)(2,1)}) %all-gather.13.cloned.1.call-update) | async-done | bytes 2097168 | tf_op jit(solution)/shard_map/all_gather | solution.py:30
  335.3 7.4 fusion.269
  351.1 42.7 %reduce-scatter.13.cloned.1.call-done = bf16[512,512]{1,0:T(8,128)(2,1)} async-done(((bf16[2048,512]{1,0:T(8,128)(2,1)}), bf16[512,512]{1,0:T(8,128)(2,1)}) %reduce-scatter.13.cloned.1.call-update) | async-done | bytes 524304 | tf_op jit(solution)/shard_map/reduce_scatter | solution.py:38
  397.1 44.6 %all-gather.15.cloned.1.call-done = bf16[2048,512]{1,0:T(8,128)(2,1)} async-done(((bf16[512,512]{1,0:T(8,128)(2,1)}), bf16[2048,512]{1,0:T(8,128)(2,1)}) %all-gather.15.cloned.1.call-update) | async-done | bytes 2097168 | tf_op jit(solution)/shard_map/all_gather | solution.py:30
  441.8 13.2 %multiply_convert_fusion.6 = (bf16[2048,512]{1,0:T(8,128)(2,1)}, f32[2048,512]{1,0:T(8,128)}, f32[2048,512]{1,0:T(8,128)}) fusion(f32[512]{0:T(512)S(1)} %bitcast.614, bf16[2048,512]{1,0:T(8,128)(2,1)} %all-gather.15.cloned.1.call-done, bf16[2,512,512]{2,1,0:T(8,128)(2,1)} %param.60), kind=kOutput, calls=%fused_computation.40 | convolution fusion | flops 1142947840 | bytes 13109248 | tf_op jit(solution)/shard_map/dot_general | solution.py:167
  455.0 33.1 %all-gather.17.cloned.1.call-done = bf16[2048,512]{1,0:T(8,128)(2,1)} async-done(((bf16[512,512]{1,0:T(8,128)(2,1)}), bf16[2048,512]{1,0:T(8,128)(2,1)}) %all-gather.17.cloned.1.call-update) | async-done | bytes 2097168 | tf_op jit(solution)/shard_map/all_gather | solution.py:34
  488.0 7.6 convert_reduce_fusion
  504.4 38.0 %reduce-scatter.17.cloned.1.call-done = bf16[512,512]{1,0:T(8,128)(2,1)} async-done(((bf16[2048,512]{1,0:T(8,128)(2,1)}), bf16[512,512]{1,0:T(8,128)(2,1)}) %reduce-scatter.17.cloned.1.call-update) | async-done | bytes 524304 | tf_op jit(solution)/shard_map/reduce_scatter | solution.py:47
  545.0 42.7 %reduce-scatter.15.cloned.1.call-done = bf16[512,512]{1,0:T(8,128)(2,1)} async-done(((bf16[2048,512]{1,0:T(8,128)(2,1)}), bf16[512,512]{1,0:T(8,128)(2,1)}) %reduce-scatter.15.cloned.1.call-update) | async-done | bytes 524304 | tf_op jit(solution)/shard_map/reduce_scatter | solution.py:38
  592.3 45.4 %all-gather.19.cloned.1.call-done = bf16[2048,512]{1,0:T(8,128)(2,1)} async-done(((bf16[512,512]{1,0:T(8,128)(2,1)}), bf16[2048,512]{1,0:T(8,128)(2,1)}) %all-gather.19.cloned.1.call-update) | async-done | bytes 2097168 | tf_op jit(solution)/shard_map/all_gather | solution.py:34
  692.5 42.5 %reduce-scatter.19.cloned.1.call-done = bf16[512,512]{1,0:T(8,128)(2,1)} async-done(((bf16[2048,512]{1,0:T(8,128)(2,1)}), bf16[512,512]{1,0:T(8,128)(2,1)}) %reduce-scatter.19.cloned.1.call-update) | async-done | bytes 524304 | tf_op jit(solution)/shard_map/reduce_scatter | solution.py:47
  742.7 45.4 %all-gather.21.cloned.1.call-done = bf16[2048,512]{1,0:T(8,128)(2,1)} async-done(((bf16[512,512]{1,0:T(8,128)(2,1)}), bf16[2048,512]{1,0:T(8,128)(2,1)}) %all-gather.21.cloned.1.call-update) | async-done | bytes 2097168 | tf_op jit(solution)/shard_map/all_gather | solution.py:34
  788.1 7.6 convert_reduce_fusion.1
  799.8 42.7 %reduce-scatter.21.cloned.1.call-done = bf16[512,512]{1,0:T(8,128)(2,1)} async-done(((bf16[2048,512]{1,0:T(8,128)(2,1)}), bf16[512,512]{1,0:T(8,128)(2,1)}) %reduce-scatter.21.cloned.1.call-update) | async-done | bytes 524304 | tf_op jit(solution)/shard_map/reduce_scatter | solution.py:47
  868.6 26.2 %all-gather.23.cloned.1.call-done = bf16[2048,512]{1,0:T(8,128)(2,1)} async-done(((bf16[512,512]{1,0:T(8,128)(2,1)}), bf16[2048,512]{1,0:T(8,128)(2,1)}) %all-gather.23.cloned.1.call-update) | async-done | bytes 2097168 | tf_op jit(solution)/shard_map/all_gather | solution.py:34
  959.7 15.1 %all-reduce.5 = (f32[1,2,128]{2,1,0:T(2,128)S(1)}, f32[1,2,128]{2,1,0:T(2,128)S(1)}, f32[1,512]{1,0:T(1,128)S(1)}, f32[1,512]{1,0:T(1,128)S(1)}) all-reduce(f32[1,2,128]{2,1,0:T(2,128)S(1)} %maximum_bitcast_fusion.5, f32[1,2,128]{2,1,0:T(2,128)S(1)} %maximum_bitcast_fusion.4, ...), channel_id=1, replica_groups=mesh['dp'=8,'tensor'=4] {'dp'}, use_global_device_ids=true, to_apply=%region_57.58 | all-reduce | flops 1536 | bytes 12288 | tf_op jit(solution)/shard_map/psum | solution.py:58
  976.1 80.3 %all-reduce.9.cloned.1.call-done = (f32[1,3,512,128]{3,2,1,0:T(8,128)}, f32[1,3,512,128]{3,2,1,0:T(8,128)}, f32[1,128,512]{2,1,0:T(8,128)}, f32[1,128,512]{2,1,0...) async-done(((f32[1,3,512,128]{3,2,1,0:T(8,128)}, f32[1,3,512,128]{3,2,1,0:T(8,128)}, ...) | async-done | bytes 6291472 | tf_op jit(solution)/shard_map/psum | solution.py:58
  1064.0 38.5 %reduce-scatter.23.cloned.1.call-done = bf16[512,512]{1,0:T(8,128)(2,1)} async-done(((bf16[2048,512]{1,0:T(8,128)(2,1)}), bf16[512,512]{1,0:T(8,128)(2,1)}) %reduce-scatter.23.cloned.1.call-update) | async-done | bytes 524304 | tf_op jit(solution)/shard_map/reduce_scatter | solution.py:47
  1105.7 40.0 %all-reduce.4 = (f32[1,512]{1,0:T(1,128)S(1)}, f32[1,512]{1,0:T(1,128)S(1)}, f32[1,512]{1,0:T(1,128)S(1)}, f32[1,512]{1,0:T(1,128)S(1)}, f32[1,2,512]{2,1,0:T(2,...) all-reduce(f32[1,512]{1,0:T(1,128)S(1)} %bitcast.585, ...), channel_id=1, replica_groups=mesh['dp'=8,'tensor'=4] {'dp','tensor'}, use_global_device_ids=true, to_apply=%region_63.64 | all-reduce | flops 6144 | bytes 49152 | tf_op jit(solution)/shard_map/psum | solution.py:69
  (617 shorter events, 300.1 us)
Async XLA Ops:
  7.2 55.6 %all-gather.9.cloned.1.call-start = ((), (), s32[]{:S(2)}) async-start(), calls=%async_computation.8 | async-start | bytes 2621440 | tf_op jit(solution)/shard_map/all_gather | solution.py:30
  11.2 140.9 %copy-start.110 = (f32[1,1,512]{2,1,0:T(1,128)}, f32[1,1,512]{2,1,0:T(1,128)S(1)}, u32[]{:S(2)}) copy-start(f32[1,1,512]{2,1,0:T(1,128)S(1)} %get-tuple-element.384) | copy-start | bytes 6148
  11.2 249.7 %copy-start.112 = (f32[1,1,512]{2,1,0:T(1,128)}, f32[1,1,512]{2,1,0:T(1,128)S(1)}, u32[]{:S(2)}) copy-start(f32[1,1,512]{2,1,0:T(1,128)S(1)} %get-tuple-element.317) | copy-start | bytes 6148
  14.0 135.5 %reduce-scatter.9.cloned.1.call-start = ((), (), s32[]{:S(2)}) async-start(), calls=%async_computation.9 | async-start | bytes 2621440 | tf_op jit(solution)/shard_map/reduce_scatter | solution.py:38
  20.5 73.5 %copy-start.38 = (pred[512,2048]{1,0:T(8,128)(4,1)}, pred[512,2048]{1,0:T(8,128)(4,1)S(1)}, u32[]{:S(2)}) copy-start(pred[512,2048]{1,0:T(8,128)(4,1)S(1)} %fusion.28) | copy-start | bytes 3145732
  106.8 93.0 %copy-start.167 = (bf16[2,512,512]{2,1,0:T(8,128)(2,1)S(1)}, bf16[2,512,512]{2,1,0:T(8,128)(2,1)}, u32[]{:S(2)}) copy-start(bf16[2,512,512]{2,1,0:T(8,128)(2,1)} %param.60) | copy-start | bytes 3145732
  106.8 93.0 %all-gather.11.cloned.1.call-start = ((), (), s32[]{:S(2)}) async-start(), calls=%async_computation.10 | async-start | bytes 2621440 | tf_op jit(solution)/shard_map/all_gather | solution.py:30
  106.9 152.4 %copy-start.102 = (f32[1,512]{1,0:T(1,128)}, f32[1,512]{1,0:T(1,128)S(1)}, u32[]{:S(2)}) copy-start(f32[1,512]{1,0:T(1,128)S(1)} %get-tuple-element.332) | copy-start | bytes 6148
  154.3 105.0 %reduce-scatter.11.cloned.1.call-start = ((), (), s32[]{:S(2)}) async-start(), calls=%async_computation.11 | async-start | bytes 2621440 | tf_op jit(solution)/shard_map/reduce_scatter | solution.py:38
  216.6 90.9 %all-gather.13.cloned.1.call-start = ((), (), s32[]{:S(2)}) async-start(), calls=%async_computation.12 | async-start | bytes 2621440 | tf_op jit(solution)/shard_map/all_gather | solution.py:30
  262.1 131.7 %reduce-scatter.13.cloned.1.call-start = ((), (), s32[]{:S(2)}) async-start(), calls=%async_computation.13 | async-start | bytes 2621440 | tf_op jit(solution)/shard_map/reduce_scatter | solution.py:38
  351.0 90.8 %copy-start.162 = (f32[1,512]{1,0:T(1,128)S(1)}, f32[1,512]{1,0:T(1,128)}, u32[]{:S(2)}) copy-start(f32[1,512]{1,0:T(1,128)} %get-tuple-element.330) | copy-start | bytes 6148
  351.0 90.7 %all-gather.15.cloned.1.call-start = ((), (), s32[]{:S(2)}) async-start(), calls=%async_computation.14 | async-start | bytes 2621440 | tf_op jit(solution)/shard_map/all_gather | solution.py:30
  396.3 91.7 %all-gather.17.cloned.1.call-start = ((), (), s32[]{:S(2)}) async-start(), calls=%async_computation.16 | async-start | bytes 2621440 | tf_op jit(solution)/shard_map/all_gather | solution.py:34
  397.1 145.3 %reduce-scatter.17.cloned.1.call-start = ((), (), s32[]{:S(2)}) async-start(), calls=%async_computation.17 | async-start | bytes 2621440 | tf_op jit(solution)/shard_map/reduce_scatter | solution.py:47
  499.6 88.1 %reduce-scatter.15.cloned.1.call-start = ((), (), s32[]{:S(2)}) async-start(), calls=%async_computation.15 | async-start | bytes 2621440 | tf_op jit(solution)/shard_map/reduce_scatter | solution.py:38
  503.9 87.3 %copy-start.9 = (bf16[512,512]{1,0:T(8,128)(2,1)S(1)}, bf16[512,512]{1,0:T(8,128)(2,1)}, u32[]{:S(2)}) copy-start(bf16[512,512]{1,0:T(8,128)(2,1)} %param.54) | copy-start | bytes 1572868
  504.0 133.7 %all-gather.19.cloned.1.call-start = ((), (), s32[]{:S(2)}) async-start(), calls=%async_computation.18 | async-start | bytes 2621440 | tf_op jit(solution)/shard_map/all_gather | solution.py:34
  592.2 142.8 %reduce-scatter.19.cloned.1.call-start = ((), (), s32[]{:S(2)}) async-start(), calls=%async_computation.19 | async-start | bytes 2621440 | tf_op jit(solution)/shard_map/reduce_scatter | solution.py:47
  692.2 95.8 %all-gather.21.cloned.1.call-start = ((), (), s32[]{:S(2)}) async-start(), calls=%async_computation.20 | async-start | bytes 2621440 | tf_op jit(solution)/shard_map/all_gather | solution.py:34
  742.7 99.8 %reduce-scatter.21.cloned.1.call-start = ((), (), s32[]{:S(2)}) async-start(), calls=%async_computation.21 | async-start | bytes 2621440 | tf_op jit(solution)/shard_map/reduce_scatter | solution.py:47
  799.7 95.1 %all-gather.23.cloned.1.call-start = ((), (), s32[]{:S(2)}) async-start(), calls=%async_computation.22 | async-start | bytes 2621440 | tf_op jit(solution)/shard_map/all_gather | solution.py:34
  849.4 206.9 %all-reduce.9.cloned.1.call-start = ((), (), s32[]{:S(2)}) async-start(), calls=%async_computation.24 | async-start | bytes 12582912 | tf_op jit(solution)/shard_map/psum | solution.py:58
  951.4 151.1 %reduce-scatter.23.cloned.1.call-start = ((), (), s32[]{:S(2)}) async-start(), calls=%async_computation.23 | async-start | bytes 2621440 | tf_op jit(solution)/shard_map/reduce_scatter | solution.py:47
  (184 other events, 2653.9 us)
Sparse Core Ops, SparseCore 0:
  14.1 48.6 all-gather.8
  106.9 42.4 reduce-scatter.8
  154.5 45.2 all-gather.10
  216.7 42.5 reduce-scatter.10
  262.2 45.2 all-gather.12
  351.1 42.5 reduce-scatter.12
  396.5 45.2 all-gather.14
  443.4 44.5 all-gather.16
  499.8 42.5 reduce-scatter.16
  544.5 43.1 reduce-scatter.14
  592.3 45.2 all-gather.18
  692.4 42.5 reduce-scatter.18
  742.8 45.2 all-gather.20
  799.8 42.5 reduce-scatter.20
  849.5 45.2 all-gather.22
  951.5 104.7 all-reduce.8
  1058.5 43.9 reduce-scatter.22
where the time goes:
time: 1170 us; the launch traced here: 1160 us
  waiting for transfers between devices  738 us (63%)
  matrix products  237 us (20%)
  other arithmetic  77.1 us (7%)
  blocking collectives  55.1 us (5%)
  local copies, waits for them, and re-layouts  32 us (3%)
  between operations  16.7 us (1%)
    all_gather x4, waiting for transfers between devices, spread_rows(): return lax.all_gather(values, 'tensor', axis=0, tiled=True)  175 us
    reduce_scatter x4, waiting for transfers between devices, branch_total(): lax.psum_scatter(jnp.dot(left_side, right_side, preferred_element_type=jn...  170 us
    reduce_scatter x4, waiting for transfers between devices, input_total(): lax.psum_scatter(jnp.einsum('se,de->sd', left_side, right_side, preferred...  162 us
    all_gather x4, waiting for transfers between devices, spread_grads(): return lax.all_gather(values, 'tensor', axis=0, tiled=True)  150 us
    psum x1, waiting for transfers between devices, reduce_grads(): lax.psum((local_grads[0], local_grads[1], local_grads[2], local_grads[3],...  80.3 us
    sub x8, matrix products, shards(): exponent = jnp.exp(scores - row_peak)  40.9 us
    psum x1, blocking collectives, reduce_grads(): lax.psum((shared_grads[0], shared_grads[1], shared_grads[2], shared_grads...  40 us
    dot_general x8, matrix products, shards(): jnp.einsum('qhd,khd->hqk', grad_blk, value_rows[:key_end], preferred_elem...  34.2 us
  transfers between devices with their start and end apart: 17, of which 17 were waited for; matrix products, arithmetic and copies ran while one was open for 6% of the time, Pallas kernels for 0%

commit v1 on v0

v1 whole, which is shorter than its diff:
```python
import functools

import jax
import jax.numpy as jnp
from jax import lax
from jax.experimental import pallas as pl
from jax.experimental.pallas import tpu as pltpu
from jax.sharding import Mesh
from jax.sharding import PartitionSpec as P

HEAD_DIM = 64
EPSILON = 1e-05
LOG2E = 1.4426950408889634
SCALE2 = HEAD_DIM ** (-0.5) * LOG2E
SCALE = HEAD_DIM ** (-0.5)
MESH = pl.DeviceIdType.MESH
AXES = ("o", "k", "c", "h", "b")
BF = jnp.bfloat16
F32 = jnp.float32
VMEM_LIMIT = 56 * 2**20


def nt(a, b):
    return lax.dot_general(a, b, (((1,), (1,)), ((), ())), preferred_element_type=F32)


def nn(a, b):
    return jnp.dot(a, b, preferred_element_type=F32)


def ln_parts(x):
    mean = jnp.mean(x, axis=-1, keepdims=True)
    cen = x - mean
    var = jnp.mean(cen * cen, axis=-1, keepdims=True)
    rstd = lax.rsqrt(var + EPSILON)
    return cen * rstd, rstd


def group_barrier(c, b):
    bar = pltpu.get_barrier_semaphore()
    for cc, bb in ((c, 1 - b), (1 - c, b), (1 - c, 1 - b)):
        pl.semaphore_signal(bar, inc=1, device_id={"c": cc, "b": bb}, device_id_type=MESH)
    pl.semaphore_wait(bar, 3)


def pad_heads_lanes(t):
    row = lax.broadcasted_iota(jnp.int32, t.shape, 0)
    low = jnp.where(row < HEAD_DIM, t, 0.0)
    high = jnp.where(row >= HEAD_DIM, t, 0.0)
    return jnp.concatenate([low, high], axis=1)


def pad_heads_rows(t):
    col = lax.broadcasted_iota(jnp.int32, t.shape, 1)
    low = jnp.where(col < HEAD_DIM, t, 0.0)
    high = jnp.where(col >= HEAD_DIM, t, 0.0)
    return jnp.concatenate([low, high], axis=0)


def causal_mask(rows):
    key = lax.broadcasted_iota(jnp.int32, (rows, 2 * rows), 0)
    qry = lax.broadcasted_iota(jnp.int32, (rows, 2 * rows), 1)
    qry = jnp.where(qry >= rows, qry - rows, qry)
    return key <= qry


def attn_fwd_kernel(
    x_ref,
    gain_ref,
    shift_ref,
    w_ref,
    bias_ref,
    neg_ref,
    ag_ref,
    qkv_ref,
    ot_ref,
    lse_ref,
    att_ref,
    qt_s,
    vt_s,
    ob_s,
    acc_s,
    ag_send,
    ag_recv,
    a2a_send,
    a2a_recv,
):
    c = lax.axis_index("c")
    b = lax.axis_index("b")
    me = 2 * c + b
    core_peer = 2 * (1 - c) + b
    z_peer = 2 * c + 1 - b
    far_peer = 2 * (1 - c) + 1 - b
    rows = x_ref.shape[0]
    width = x_ref.shape[1]
    group = ag_ref.shape[0]
    ld = w_ref.shape[1] // 3
    step = 64

    def norm(it, carry):
        at = pl.ds(pl.multiple_of(it * step, step), step)
        n, _ = ln_parts(x_ref[at, :].astype(F32))
        ag_ref[me, at, :] = (n * gain_ref[...] + shift_ref[...]).astype(BF)
        return carry

    lax.fori_loop(0, rows // step, norm, 0)
    group_barrier(c, b)

    def send(src_slot, dev, slot):
        return pltpu.make_async_remote_copy(
            src_ref=ag_ref.at[src_slot],
            dst_ref=ag_ref.at[src_slot],
            send_sem=ag_send.at[slot],
            recv_sem=ag_recv.at[slot],
            device_id=dev,
            device_id_type=MESH,
        )

    to_z = send(me, {"c": c, "b": 1 - b}, 0)
    to_core = send(me, {"c": 1 - c, "b": b}, 1)
    fwd = send(z_peer, {"c": 1 - c, "b": b}, 2)
    to_z.start()
    to_core.start()

    def project(slot):
        r = nn(ag_ref[slot], w_ref[...]) + bias_ref[...]
        qkv_ref[slot] = r.astype(BF)
        qt_s[slot] = pad_heads_lanes(r[:, :ld].T).astype(BF)
        vt_s[slot] = r[:, 2 * ld :].T.astype(BF)

    project(me)
    to_core.wait_recv()
    project(core_peer)
    to_z.wait_recv()
    fwd.start()
    project(z_peer)
    fwd.wait_recv()
    project(far_peer)

    neg = neg_ref[0:1, 0:1]

    def block(i, j, m, l, diag):
        s = nn(qkv_ref[j, :, ld : 2 * ld], qt_s[i])
        if diag:
            s = jnp.where(causal_mask(rows), s, -1e30)
            m_new = jnp.max(s, axis=0, keepdims=True)
            base = m_new * SCALE2
        else:
            m_new = jnp.maximum(m, jnp.max(s, axis=0, keepdims=True) + neg)
            base = (m_new - neg) * SCALE2
        p = jnp.exp2(s * SCALE2 - base)
        l_new = jnp.sum(p, axis=0, keepdims=True)
        pb = p.astype(BF)
        o0 = nn(vt_s[j, :HEAD_DIM, :], pb[:, :rows])
        o1 = nn(vt_s[j, HEAD_DIM:, :], pb[:, rows:])
        if diag:
            acc_s[:HEAD_DIM, :] = o0
            acc_s[HEAD_DIM:, :] = o1
        else:
            alpha = jnp.exp2((m - m_new) * SCALE2)
            l_new = l * alpha + l_new
            acc_s[:HEAD_DIM, :] = acc_s[:HEAD_DIM, :] * alpha[:, :rows] + o0
            acc_s[HEAD_DIM:, :] = acc_s[HEAD_DIM:, :] * alpha[:, rows:] + o1
        return m_new, l_new

    def a2a(i):
        ic, ib = i // 2, i % 2
        slot = 2 * (ic - c) * (ic - c) + (ib - b) * (ib - b)
        return pltpu.make_async_remote_copy(
            src_ref=ob_s.at[i],
            dst_ref=att_ref.at[:, pl.ds(pl.multiple_of(me * ld, ld), ld)],
            send_sem=a2a_send.at[slot],
            recv_sem=a2a_recv.at[slot],
            device_id={"c": ic, "b": ib},
            device_id_type=MESH,
        )

    def row(it, carry):
        i = group - 1 - it
        m, l = block(i, i, None, None, True)
        m, l = lax.fori_loop(0, i, lambda j, ml: block(i, j, ml[0], ml[1], False), (m, l))
        inv = 1.0 / l
        ot = jnp.concatenate(
            [acc_s[:HEAD_DIM, :] * inv[:, :rows], acc_s[HEAD_DIM:, :] * inv[:, rows:]], axis=0
        )
        ot_ref[i] = ot
        lse_ref[i] = jnp.broadcast_to(m * SCALE2 + jnp.log(l) * LOG2E, lse_ref.shape[1:])
        ob_s[i] = ot.T.astype(BF)

        @pl.when(i == me)
        def _():
            att_ref[:, pl.ds(pl.multiple_of(me * ld, ld), ld)] = ob_s[i]

        @pl.when(i != me)
        def _():
            a2a(i).start()

        return carry

    lax.fori_loop(0, group, row, 0)
    to_z.wait_send()
    to_core.wait_send()
    fwd.wait_send()
    for slot in range(1, group):
        cp = pltpu.make_async_remote_copy(
            src_ref=ob_s.at[0],
            dst_ref=ob_s.at[0],
            send_sem=a2a_send.at[slot],
            recv_sem=a2a_recv.at[slot],
            device_id={"c": 1 - c, "b": b},
            device_id_type=MESH,
        )
        cp.wait_send()
        cp.wait_recv()


def vm(n):
    return [pl.BlockSpec(memory_space=pltpu.VMEM)] * n


def attn_fwd(x, gain, shift, w, bias, neg, cid):
    rows, width = x.shape
    ld = w.shape[1] // 3
    g = 4
    return pl.pallas_call(
        attn_fwd_kernel,
        name="attn_fwd",
        out_shape=(
            jax.ShapeDtypeStruct((g, rows, width), BF),
            jax.ShapeDtypeStruct((g, rows, 3 * ld), BF),
            jax.ShapeDtypeStruct((g, ld, rows), F32),
            jax.ShapeDtypeStruct((g, 8, 2 * rows), F32),
            jax.ShapeDtypeStruct((rows, width), BF),
        ),
        in_specs=vm(6),
        out_specs=tuple(vm(5)),
        scratch_shapes=[
            pltpu.VMEM((g, ld, 2 * rows), BF),
            pltpu.VMEM((g, ld, rows), BF),
            pltpu.VMEM((g, rows, ld), BF),
            pltpu.VMEM((ld, rows), F32),
            pltpu.SemaphoreType.DMA((3,)),
            pltpu.SemaphoreType.DMA((3,)),
            pltpu.SemaphoreType.DMA((4,)),
            pltpu.SemaphoreType.DMA((4,)),
        ],
        compiler_params=pltpu.CompilerParams(
            collective_id=cid, has_side_effects=True, vmem_limit_bytes=VMEM_LIMIT
        ),
    )(x, gain, shift, w, bias, neg)


def attn_bwd_kernel(
    ga_ref,
    x_ref,
    gain_ref,
    gmid_ref,
    ag_ref,
    qkv_ref,
    ot_ref,
    lse_ref,
    w_ref,
    neg_ref,
    gx_ref,
    gwt_ref,
    gb_ref,
    gln_ref,
    do_s,
    qt_s,
    qp_s,
    dot_s,
    dop_s,
    kt_s,
    delta_s,
    dk_s,
    dv_s,
    dqt_s,
    part_s,
    core_in,
    zsend_s,
    z_in,
    own_s,
    a2a_send,
    a2a_recv,
    cs_sem,
    cr_sem,
    zs_sem,
    zr_sem,
):
    c = lax.axis_index("c")
    b = lax.axis_index("b")
    me = 2 * c + b
    rows = x_ref.shape[0]
    group = ag_ref.shape[0]
    ld = w_ref.shape[1] // 3
    group_barrier(c, b)
    peers = [(1, c, 1 - b), (2, 1 - c, b), (3, 1 - c, 1 - b)]
    sends = []
    for slot, cc, bb in peers:
        cp = pltpu.make_async_remote_copy(
            src_ref=ga_ref.at[:, pl.ds(pl.multiple_of((2 * cc + bb) * ld, ld), ld)],
            dst_ref=do_s.at[me],
            send_sem=a2a_send.at[slot],
            recv_sem=a2a_recv.at[slot],
            device_id={"c": cc, "b": bb},
            device_id_type=MESH,
        )
        cp.start()
        sends.append(cp)
    do_s[me] = ga_ref[:, pl.ds(pl.multiple_of(me * ld, ld), ld)]

    def prep_q(i, carry):
        q = qkv_ref[i, :, :ld].astype(F32)
        qt_s[i] = pad_heads_lanes(q.T).astype(BF)
        qp_s[i] = pad_heads_rows(q).astype(BF)
        kt_s[i] = qkv_ref[i, :, ld : 2 * ld].astype(F32).T.astype(BF)
        dk_s[i] = jnp.zeros(dk_s.shape[1:], F32)
        dv_s[i] = jnp.zeros(dv_s.shape[1:], F32)
        return carry

    lax.fori_loop(0, group, prep_q, 0)
    for cp in sends:
        cp.wait_recv()

    def prep_do(i, carry):
        do = do_s[i].astype(F32)
        dot = do.T
        dot_s[i] = pad_heads_lanes(dot).astype(BF)
        dop_s[i] = pad_heads_rows(do).astype(BF)
        prod = ot_ref[i] * dot
        d0 = jnp.sum(prod[:HEAD_DIM], axis=0, keepdims=True)
        d1 = jnp.sum(prod[HEAD_DIM:], axis=0, keepdims=True)
        delta_s[i] = jnp.broadcast_to(jnp.concatenate([d0, d1], axis=1), delta_s.shape[1:])
        return carry

    lax.fori_loop(0, group, prep_do, 0)
    neg = neg_ref[0:1, 0:1]
    gwt_ref[...] = jnp.zeros(gwt_ref.shape, F32)
    gb_ref[...] = jnp.zeros(gb_ref.shape, F32)

    def block(i, j, diag):
        s = nn(qkv_ref[j, :, ld : 2 * ld], qt_s[i])
        lse = lse_ref[i, 0:1, :]
        if diag:
            s = jnp.where(causal_mask(rows), s, -1e30)
            p = jnp.exp2(s * SCALE2 - lse)
        else:
            p = jnp.exp2(s * SCALE2 - (lse - neg))
        dp = nn(qkv_ref[j, :, 2 * ld :], dot_s[i])
        ds = (p * (dp - delta_s[i, 0:1, :])).astype(BF)
        pb = p.astype(BF)
        dv_s[j] += nn(pb, dop_s[i])
        dk_s[j] += nn(ds, qp_s[i])
        q0 = nn(kt_s[j, :HEAD_DIM, :], ds[:, :rows])
        q1 = nn(kt_s[j, HEAD_DIM:, :], ds[:, rows:])
        if diag:
            dqt_s[:HEAD_DIM, :] = q0
            dqt_s[HEAD_DIM:, :] = q1
        else:
            dqt_s[:HEAD_DIM, :] += q0
            dqt_s[HEAD_DIM:, :] += q1

    def core_copy(i, kind):
        return pltpu.make_async_remote_copy(
            src_ref=part_s.at[i],
            dst_ref=core_in.at[kind],
            send_sem=cs_sem.at[kind],
            recv_sem=cr_sem.at[kind],
            device_id={"c": 1 - c, "b": b},
            device_id_type=MESH,
        )

    z_copy = pltpu.make_async_remote_copy(
        src_ref=zsend_s,
        dst_ref=z_in,
        send_sem=zs_sem,
        recv_sem=zr_sem,
        device_id={"c": c, "b": 1 - b},
        device_id_type=MESH,
    )

    def relay(i):
        ic, ib = i // 2, i % 2

        @pl.when((ic == c) & (ib != b))
        def _():
            core_copy(0, 1).wait_recv()
            zsend_s[...] = (part_s[i].astype(F32) + core_in[1].astype(F32)).astype(BF)
            z_copy.start()

    def row(it, carry):
        i = group - 1 - it
        ic, ib = i // 2, i % 2
        block(i, i, True)

        def off(j, cc):
            block(i, j, False)
            return cc

        lax.fori_loop(0, i, off, 0)
        dq = (dqt_s[...] * SCALE).astype(BF)
        dk = (dk_s[i] * SCALE).astype(BF)
        dv = dv_s[i].astype(BF)
        dq_n = dq.astype(F32).T.astype(BF)
        dqkv = jnp.concatenate([dq_n, dk, dv], axis=1)
        part = nt(dqkv, w_ref[...])
        part_s[i] = part.astype(BF)

        @pl.when(i == me)
        def _():
            own_s[...] = part

        @pl.when(ic != c)
        def _():
            core_copy(i, (ib - b) * (ib - b)).start()

        dqkv_t = jnp.concatenate(
            [dq, dk.astype(F32).T.astype(BF), dv.astype(F32).T.astype(BF)], axis=0
        )
        gwt_ref[...] += nn(dqkv_t, ag_ref[i])
        gb_ref[...] += jnp.broadcast_to(
            jnp.sum(dqkv.astype(F32), axis=0, keepdims=True), gb_ref.shape
        )

        @pl.when(it > 0)
        def _():
            relay(i + 1)

        return carry

    lax.fori_loop(0, group, row, 0)
    relay(jnp.int32(0))
    core_copy(0, 0).wait_recv()
    z_copy.wait_recv()

    step = 64
    gln_ref[...] = jnp.zeros(gln_ref.shape, F32)

    def norm(it, carry):
        at = pl.ds(pl.multiple_of(it * step, step), step)
        g = own_s[at, :] + core_in[0, at, :].astype(F32) + z_in[at, :].astype(F32)
        n, rstd = ln_parts(x_ref[at, :].astype(F32))
        u = g * gain_ref[...]
        mu = jnp.mean(u, axis=-1, keepdims=True)
        mun = jnp.mean(u * n, axis=-1, keepdims=True)
        gx_ref[at, :] = gmid_ref[at, :] + rstd * (u - mu - n * mun)
        gln_ref[0:1, :] += jnp.sum(g * n, axis=0, keepdims=True)
        gln_ref[1:2, :] += jnp.sum(g, axis=0, keepdims=True)
        return carry

    lax.fori_loop(0, rows // step, norm, 0)
    for cp in sends:
        cp.wait_send()
    core_copy(0, 0).wait_send()
    core_copy(0, 1).wait_send()
    z_copy.wait_send()


def attn_bwd(ga, x, gain, gmid, ag, qkv, ot, lse, w, neg, cid):
    rows, width = x.shape
    ld = w.shape[1] // 3
    g = 4
    return pl.pallas_call(
        attn_bwd_kernel,
        name="attn_bwd",
        out_shape=(
            jax.ShapeDtypeStruct((rows, width), F32),
            jax.ShapeDtypeStruct((3 * ld, width), F32),
            jax.ShapeDtypeStruct((8, 3 * ld), F32),
            jax.ShapeDtypeStruct((8, width), F32),
        ),
        in_specs=vm(10),
        out_specs=tuple(vm(4)),
        scratch_shapes=[
            pltpu.VMEM((g, rows, ld), BF),
            pltpu.VMEM((g, ld, 2 * rows), BF),
            pltpu.VMEM((g, 2 * rows, ld), BF),
            pltpu.VMEM((g, ld, 2 * rows), BF),
            pltpu.VMEM((g, 2 * rows, ld), BF),
            pltpu.VMEM((g, ld, rows), BF),
            pltpu.VMEM((g, 8, 2 * rows), F32),
            pltpu.VMEM((g, rows, ld), F32),
            pltpu.VMEM((g, rows, ld), F32),
            pltpu.VMEM((ld, rows), F32),
            pltpu.VMEM((g, rows, width), BF),
            pltpu.VMEM((2, rows, width), BF),
            pltpu.VMEM((rows, width), BF),
            pltpu.VMEM((rows, width), BF),
            pltpu.VMEM((rows, width), F32),
            pltpu.SemaphoreType.DMA((4,)),
            pltpu.SemaphoreType.DMA((4,)),
            pltpu.SemaphoreType.DMA((2,)),
            pltpu.SemaphoreType.DMA((2,)),
            pltpu.SemaphoreType.DMA,
            pltpu.SemaphoreType.DMA,
        ],
        compiler_params=pltpu.CompilerParams(
            collective_id=cid, has_side_effects=True, vmem_limit_bytes=VMEM_LIMIT
        ),
    )(ga, x, gain, gmid, ag, qkv, ot, lse, w, neg)


def gelu_act(values):
    return jax.nn.gelu(values, approximate=False)


def layer_norm(values, gain_row, bias_row):
    n, _ = ln_parts(values)
    return n * gain_row + bias_row


def shards(
    tokens,
    cotangent,
    clip_lengths,
    w_qkv,
    b_qv,
    w_out,
    b_out,
    w_up,
    b_up,
    w_down,
    b_down,
    ln_gain,
    ln_bias,
):
    rows, width = tokens.shape
    layers = w_qkv.shape[0]
    ld = w_qkv.shape[3]
    n_outer = lax.axis_size("o")
    quarter = w_up.shape[2]

    perm = []
    for lead in range(4 * n_outer):
        for cc in range(2):
            for hh in range(2):
                for bb in range(2):
                    perm.append((lead * 8 + cc * 4 + hh * 2 + bb, lead * 8 + hh * 4 + cc * 2 + bb))

    def swap(v):
        return lax.ppermute(v, AXES, perm)

    piece = lax.axis_index("k") * 2 + lax.axis_index("c")

    def gather_weights(l):
        def cut(v):
            n = v.shape[0] // 8
            return lax.dynamic_slice_in_dim(v, piece * n, n, 0)

        rows_b = jnp.broadcast_to(b_up[l][None], (16, quarter))
        own = jnp.concatenate([cut(w_out[l]), cut(w_up[l]), cut(w_down[l]), rows_b], axis=0)
        g1 = lax.all_gather(own, ("h", "b"), axis=0, tiled=False)
        g2 = lax.all_gather(g1[:, :-16], ("k", "c"), axis=0, tiled=False)
        return g2, g1[:, -16, :]

    weights = [gather_weights(l) for l in range(layers)]
    n_out = ld // 8
    n_up = width // 8

    def unpack(l):
        g2, bu = weights[l]
        wo = g2[:, :, :n_out].transpose(1, 0, 2, 3).reshape(4 * ld, width)
        wu = g2[:, :, n_out : n_out + n_up].transpose(0, 2, 1, 3).reshape(width, 4 * quarter)
        wd = g2[:, :, n_out + n_up :].transpose(1, 0, 2, 3).reshape(4 * quarter, width)
        return wo, wu, wd, bu.reshape(1, 4 * quarter).astype(F32)

    x = swap(tokens)
    wq = swap(jnp.transpose(w_qkv, (0, 2, 1, 3)).reshape(layers, width, 3 * ld))
    small = swap(b_qv)
    lengths = swap(clip_lengths)
    slot_len = rows * 4
    neg = jnp.where(lengths[0, 0] == slot_len, 0.0, -1e30).astype(F32)
    neg = jnp.broadcast_to(neg, (8, 128))
    gains = ln_gain.astype(F32)
    shifts = ln_bias.astype(F32)
    g_in = swap(cotangent)

    stream = x.astype(F32)
    stored = []
    for l in range(layers):
        bias = jnp.concatenate(
            [small[l, 0], jnp.zeros((ld,), BF), small[l, 1]]
        ).astype(F32)[None]
        ag, qkv, ot, lse, att = attn_fwd(
            stream, gains[l, 0][None], shifts[l, 0][None], wq[l], bias, neg, 2 * l
        )
        wo, wu, wd, bu = unpack(l)
        mid = stream + nn(att, wo) + b_out[l].astype(F32)
        mlp_in = layer_norm(mid, gains[l, 1], shifts[l, 1]).astype(BF)
        pre = nn(mlp_in, wu) + bu
        hidden = gelu_act(pre).astype(BF)
        nxt = mid + nn(hidden, wd) + b_down[l].astype(F32)
        stored.append((stream, ag, qkv, ot, lse, att, mid, mlp_in, pre, hidden, wo, wu, wd))
        stream = nxt
    output = swap(stream.astype(BF))

    def reduce_big(g):
        r1 = lax.psum_scatter(g, ("k", "c"), scatter_dimension=0, tiled=False)
        r2 = lax.psum_scatter(r1, ("h", "b"), scatter_dimension=0, tiled=False)
        if n_outer > 1:
            r2 = lax.psum(r2, "o")
        return lax.all_gather(r2, ("k", "c"), axis=0, tiled=False)

    grad = g_in.astype(F32)
    outs = {k: [None] * layers for k in ("wqkv", "bqv", "wout", "wup", "bup", "wdown", "shared")}
    for l in reversed(range(layers)):
        stream_in, ag, qkv, ot, lse, att, mid, mlp_in, pre, hidden, wo, wu, wd = stored[l]
        g_bdown = jnp.sum(grad, axis=0)
        low = grad.astype(BF)
        g_wd = lax.dot_general(hidden, low, (((0,), (0,)), ((), ())), preferred_element_type=F32)
        g_hid = nt(low, wd)
        g_pre = jax.vjp(gelu_act, pre)[1](g_hid)[0].astype(BF)
        g_wu = lax.dot_general(mlp_in, g_pre, (((0,), (0,)), ((), ())), preferred_element_type=F32)
        g_bup = jnp.sum(g_pre.astype(F32), axis=0)
        g_mlp = nt(g_pre, wu)
        n, rstd = ln_parts(mid)
        u = g_mlp * gains[l, 1]
        mu = jnp.mean(u, axis=-1, keepdims=True)
        mun = jnp.mean(u * n, axis=-1, keepdims=True)
        g_mid = grad + rstd * (u - mu - n * mun)
        g_gain2 = jnp.sum(g_mlp * n, axis=0)
        g_shift2 = jnp.sum(g_mlp, axis=0)
        g_bout = jnp.sum(g_mid, axis=0)
        mid_low = g_mid.astype(BF)
        g_wo = lax.dot_general(att, mid_low, (((0,), (0,)), ((), ())), preferred_element_type=F32)
        ga = nt(mid_low, wo).astype(BF)
        grad, gwt, gb, gln = attn_bwd(
            ga, stream_in, gains[l, 0][None], g_mid, ag, qkv, ot, lse, wq[l], neg, 2 * l + 1
        )
        packed = jnp.concatenate(
            [
                g_wo.astype(BF).reshape(4, 8, n_out, width).transpose(1, 0, 2, 3),
                g_wu.astype(BF).reshape(8, n_up, 4, quarter).transpose(0, 2, 1, 3),
                g_wd.astype(BF).reshape(4, 8, quarter // 8, width).transpose(1, 0, 2, 3),
            ],
            axis=2,
        )
        red = reduce_big(packed).astype(F32)
        outs["wout"][l] = red[:, :n_out].reshape(ld, width)
        outs["wup"][l] = red[:, n_out : n_out + n_up].reshape(width, quarter)
        outs["wdown"][l] = red[:, n_out + n_up :].reshape(quarter, width)
        outs["wqkv"][l] = gwt.astype(BF)
        outs["bqv"][l] = gb[0]
        outs["bup"][l] = g_bup
        outs["shared"][l] = jnp.stack([g_bout, g_bdown, gln[0], g_gain2, gln[1], g_shift2])
    gq = lax.psum(jnp.stack(outs["wqkv"]), ("o", "k", "h"))
    gbq = lax.psum(jnp.stack(outs["bqv"]), ("o", "k", "h"))
    gq = swap(gq).astype(F32)
    gbq = swap(gbq)
    gq = gq.reshape(layers, 3, ld, width).transpose(0, 1, 3, 2)
    gbq = jnp.stack([gbq[:, :ld], gbq[:, 2 * ld :]], axis=1)
    flat = jnp.concatenate(
        [jnp.stack(outs["bup"]).reshape(-1), jnp.stack(outs["shared"]).reshape(-1)]
    )
    flat = lax.psum(flat, AXES)
    nb = layers * 4 * quarter
    t = lax.axis_index("h") * 2 + lax.axis_index("b")
    g_bup = lax.dynamic_slice_in_dim(flat[:nb].reshape(layers, 4 * quarter), t * quarter, quarter, 1)
    sh = flat[nb:].reshape(layers, 6, width)
    return (
        output,
        swap(grad.astype(BF)),
        gq,
        gbq,
        jnp.stack(outs["wout"]),
        sh[:, 0],
        jnp.stack(outs["wup"]),
        g_bup,
        jnp.stack(outs["wdown"]),
        sh[:, 1],
        sh[:, 2:4],
        sh[:, 4:6],
    )


def solution(mesh):
    n_dp = mesh.shape["dp"]
    inner = Mesh(mesh.devices.reshape(n_dp // 8, 4, 2, 2, 2), AXES)
    dp = ("o", "k", "c")
    tensor = ("h", "b")
    both = dp + tensor
    in_specs = (
        P(both, None),
        P(both, None),
        P(dp, None),
        P(None, None, None, tensor),
        P(None, None, tensor),
        P(None, tensor, None),
        P(),
        P(None, None, tensor),
        P(None, tensor),
        P(None, tensor, None),
        P(),
        P(),
        P(),
    )
    out_specs = (
        P(both, None),
        P(both, None),
        P(None, None, None, tensor),
        P(None, None, tensor),
        P(None, tensor, None),
        P(),
        P(None, None, tensor),
        P(None, tensor),
        P(None, tensor, None),
        P(),
        P(),
        P(),
    )
    return jax.shard_map(shards, mesh=inner, in_specs=in_specs, out_specs=out_specs, check_vma=False)
```

time: 1170 us -> 656 us (0.56)
  waiting for transfers between devices: 738 us -> 152 us
  Pallas kernels: 0 us -> 210 us
  matrix products: 237 us -> 70.4 us
  other arithmetic: 77.1 us -> 17.4 us
  blocking collectives: 55.1 us -> 108 us
  local copies, waits for them, and re-layouts: 32 us -> 58.6 us
  starting transfers between devices: 2.19 us -> 20.3 us
    all_gather x8 -> x4, waiting for transfers between devices: 325 us -> 15.3 us  [the longest x2 15.3 us: reduce_big(): return lax.all_gather(r2, ('k', 'c'), axis=0, tiled=False)]
    reduce_scatter x8 -> x4, waiting for transfers between devices: 332 us -> 94.6 us  [the longest x2 94.5 us: reduce_big(): r1 = lax.psum_scatter(g, ('k', 'c'), scatter_dimension=0, tiled=False)]
    pallas_call x0 -> x4, Pallas kernels: none -> 210 us  [the longest x2 108 us: attn_fwd(): pl.pallas_call(attn_fwd_kernel, name='attn_fwd', out_shape=(jax.ShapeDtyp...]
    dot_general x64 -> x18, matrix products: 196 us -> 70.4 us  [the longest x6 43.8 us: nn(): return jnp.dot(a, b, preferred_element_type=F32)]
    sub x8 -> x0, matrix products: 40.9 us -> none  [shards(): exponent = jnp.exp(scores - row_peak)]
    psum x1, waiting for transfers between devices: 80.3 us -> 41.5 us  [shards(): gq = lax.psum(jnp.stack(outs['wqkv']), ('o', 'k', 'h'))]
    all_gather x0 -> x2, blocking collectives: none -> 35.7 us  [gather_weights(): g1 = lax.all_gather(own, ('h', 'b'), axis=0, tiled=False)]
    reduce_sum x23 -> x4, other arithmetic: 30.8 us -> 2.48 us  [the longest x2 1.96 us: shards(): g_bout = jnp.sum(g_mid, axis=0)]
  transfers between devices with their start and end apart: 17 -> 18, of which waited for: 17 -> 4; matrix products, arithmetic and copies ran while one was open for 6% -> 15% of each run, Pallas kernels for 0% -> 25%
where the time goes in v1:
time: 656 us; the launch traced here: 652 us
  Pallas kernels  210 us (32%)
  waiting for transfers between devices  152 us (23%)
  blocking collectives  108 us (16%)
  matrix products  70.4 us (11%)
  local copies, waits for them, and re-layouts  58.6 us (9%)
  starting transfers between devices  20.3 us (3%)
  other arithmetic  17.4 us (3%)
  between operations  15 us (2%)
    pallas_call x2, Pallas kernels, attn_fwd(): pl.pallas_call(attn_fwd_kernel, name='attn_fwd', out_shape=(jax.ShapeDtyp...  108 us
    pallas_call x2, Pallas kernels, attn_bwd(): pl.pallas_call(attn_bwd_kernel, name='attn_bwd', out_shape=(jax.ShapeDtyp...  103 us
    reduce_scatter x2, waiting for transfers between devices, reduce_big(): r1 = lax.psum_scatter(g, ('k', 'c'), scatter_dimension=0, tiled=False)  94.5 us
    dot_general x6, matrix products, nn(): return jnp.dot(a, b, preferred_element_type=F32)  43.8 us
    psum x1, blocking collectives, shards(): flat = lax.psum(flat, AXES)  42.6 us
    psum x1, waiting for transfers between devices, shards(): gq = lax.psum(jnp.stack(outs['wqkv']), ('o', 'k', 'h'))  41.5 us
    all_gather x2, blocking collectives, gather_weights(): g1 = lax.all_gather(own, ('h', 'b'), axis=0, tiled=False)  35.7 us
    psum x1, blocking collectives, shards(): gbq = lax.psum(jnp.stack(outs['bqv']), ('o', 'k', 'h'))  29.2 us
  transfers between devices with their start and end apart: 18, of which 4 were waited for; matrix products, arithmetic and copies ran while one was open for 15% of the time, Pallas kernels for 25%

profile of v1, /device:TPU:0, one launch (start us, length us, event | category | flops | bytes accessed | tf_op | source)
XLA Modules:
  0.0 651.9 jit_solution(11850832160608909057)
XLA Ops:
  12.3 19.6 %all-gather.2 = bf16[640,512]{1,0:T(8,128)(2,1)S(1)} all-gather(bf16[160,512]{1,0:T(8,128)(2,1)S(1)} %pad_maximum_fusion.7), channel_id=4, replica_groups=mesh['o'=1,'k'=4,'c'=2,'h'=2,'b'=2] {'h','b'}, dimensions={0}, use_global_device_ids=true | all-gather | bytes 819200 | tf_op jit(solution)/shard_map/all_gather | solution.py:552
  33.6 16.1 %all-gather = bf16[640,512]{1,0:T(8,128)(2,1)S(1)} all-gather(bf16[160,512]{1,0:T(8,128)(2,1)S(1)} %pad_maximum_fusion.6), channel_id=2, replica_groups=mesh['o'=1,'k'=4,'c'=2,'h'=2,'b'=2] {'h','b'}, dimensions={0}, use_global_device_ids=true | all-gather | bytes 819200 | tf_op jit(solution)/shard_map/all_gather | solution.py:552
  55.0 5.4 collective-permute-start.5
  66.4 71.5 %attn_fwd.2 = (bf16[4,512,512]{2,1,0:T(8,128)(2,1)}, bf16[4,512,384]{2,1,0:T(8,128)(2,1)}, f32[4,128,512]{2,1,0:T(8,128)}, f32[4,8,1024]{2,1,0:T(8,128)}, bf16[512,512]{1,0:T(8,128)(2,1)}) custom-call(f32[512,512]{1,0:T(8,128)} %convert_element_type.139.x_ref, f32[1,512]{1,0:T(1,128)} %get-tuple-element.143.gain_ref, f32[1,512]{1,0:T(1,128)} %get-tuple-element.141.shift_ref, ...), custom_call_target="tpu_custom_call" | custom-call | tf_op jit(solution)/shard_map/attn_fwd/pallas_call | solution.py:225
  139.1 4.0 slice_bitcast_fusion
  153.9 24.1 %multiply_convert_fusion.1 = (bf16[512,2048]{1,0:T(8,128)(2,1)S(1)}, f32[512,2048]{1,0:T(8,128)}, f32[512,2048]{1,0:T(8,128)}) fusion(f32[2048]{0:T(1024)S(1)} %bitcast.240, bf16[512,2048]{1,0:T(8,128)(2,1)S(1)} %bitcast.207, f32[512,512]{1,0:T(8,128)S(1)} %get-tuple-element.161, f32[512]{0:T(512)S(1)} %bitcast.255, f32[512]{0:T(512)S(1)} %bitcast.234, ...), kind=kOutput, calls=%fused_computation.31 | convolution fusion | flops 1144258560 | bytes 13647872 | tf_op jit(solution)/shard_map/dot_general | solution.py:28
  180.3 36.1 %attn_fwd.3 = (bf16[4,512,512]{2,1,0:T(8,128)(2,1)}, bf16[4,512,384]{2,1,0:T(8,128)(2,1)}, f32[4,128,512]{2,1,0:T(8,128)}, f32[4,8,1024]{2,1,0:T(8,128)}, bf16[512,512]{1,0:T(8,128)(2,1)}) custom-call(f32[512,512]{1,0:T(8,128)} %fusion.22.x_ref, f32[1,512]{1,0:T(1,128)} %get-tuple-element.142.gain_ref, f32[1,512]{1,0:T(1,128)} %get-tuple-element.140.shift_ref, ...), custom_call_target="tpu_custom_call" | custom-call | tf_op jit(solution)/shard_map/attn_fwd/pallas_call | solution.py:225
  218.5 11.3 %multiply_convert_fusion = (bf16[512,2048]{1,0:T(8,128)(2,1)}, f32[512,2048]{1,0:T(8,128)S(1)}, f32[512,2048]{1,0:T(8,128)S(1)}) fusion(f32[2048]{0:T(1024)S(1)} %bitcast.242, bf16[512,2048]{1,0:T(8,128)(2,1)S(1)} %bitcast.211, f32[512,512]{1,0:T(8,128)S(1)} %get-tuple-element.164, f32[512]{0:T(512)S(1)} %bitcast.253, f32[512]{0:T(512)S(1)} %bitcast.230, ...), kind=kOutput, calls=%fused_computation.18 | convolution fusion | flops 1144258560 | bytes 13647872 | tf_op jit(solution)/shard_map/dot_general | solution.py:28
  230.1 4.3 convert_reduce_fusion
  238.8 44.6 %attn_bwd.2 = (f32[512,512]{1,0:T(8,128)}, f32[384,512]{1,0:T(8,128)}, f32[8,384]{1,0:T(8,128)}, f32[8,512]{1,0:T(8,128)}) custom-call(bf16[512,512]{1,0:T(8,128)(2,1)} %convolution_convert_fusion.7.ga_ref, f32[512,512]{1,0:T(8,128)} %fusion.22.x_ref, f32[1,512]{1,0:T(1,128)} %get-tuple-element.142.gain_ref, f32[512,512]{1,0:T(8,128)} %copy-done.1, ...), custom_call_target="tpu_custom_call" | custom-call | tf_op jit(solution)/shard_map/attn_bwd/pallas_call | solution.py:463
  287.0 4.6 convert_reduce_fusion.1
  298.4 4.5 reshape.243
  307.7 3.0 convolution_convert_fusion
  313.5 2.8 convolution_convert_fusion.1
  316.3 4.7 reshape.246
  326.1 37.0 %reduce-scatter.5.cloned.1.call-done = bf16[1,4,144,512]{3,2,1,0:T(8,128)(2,1)} async-done(((bf16[8,4,144,512]{3,2,1,0:T(8,128)(2,1)}), bf16[1,4,144,512]{3,2,1,0:T(8,128)(2,1)}) %reduce-scatter.5.cloned.1.call-update) | async-done | bytes 589840 | tf_op jit(solution)/shard_map/reduce_scatter | solution.py:598
  363.1 57.5 %reduce-scatter.9.cloned.1.call-done = bf16[1,4,144,512]{3,2,1,0:T(8,128)(2,1)} async-done(((bf16[8,4,144,512]{3,2,1,0:T(8,128)(2,1)}), bf16[1,4,144,512]{3,2,1,0:T(8,128)(2,1)}) %reduce-scatter.9.cloned.1.call-update) | async-done | bytes 589840 | tf_op jit(solution)/shard_map/reduce_scatter | solution.py:598
  422.0 58.2 %attn_bwd.3 = (f32[512,512]{1,0:T(8,128)}, f32[384,512]{1,0:T(8,128)}, f32[8,384]{1,0:T(8,128)}, f32[8,512]{1,0:T(8,128)}) custom-call(bf16[512,512]{1,0:T(8,128)(2,1)} %convolution_convert_fusion.6.ga_ref, f32[512,512]{1,0:T(8,128)} %convert_element_type.139.x_ref, f32[1,512]{1,0:T(1,128)} %get-tuple-element.143.gain_ref, f32[512,512]{1,0:T(8,128)} %copy-done, ...), custom_call_target="tpu_custom_call" | custom-call | tf_op jit(solution)/shard_map/attn_bwd/pallas_call | solution.py:463
  485.2 42.6 %psum.23 = f32[10240]{0:T(1024)S(1)} all-reduce(f32[10240]{0:T(1024)S(1)} %pad_maximum_fusion.8), channel_id=1, replica_groups=mesh['o'=1,'k'=4,'c'=2,'h'=2,'b'=2] {'o','k','c','h','b'}, use_global_device_ids=true, to_apply=%region_24.25 | all-reduce | flops 10240 | bytes 81920 | tf_op jit(solution)/shard_map/psum | solution.py:655
  531.3 5.4 collective-permute-start.6
  536.6 3.6 fusion.23
  542.6 41.5 %all-reduce.2.cloned.1.call-done = bf16[2,384,512]{2,1,0:T(8,128)(2,1)} async-done(((bf16[2,384,512]{2,1,0:T(8,128)(2,1)}), bf16[2,384,512]{2,1,0:T(8,128)(2,1)}) %all-reduce.2.cloned.1.call-update) | async-done | bytes 786448 | tf_op jit(solution)/shard_map/psum | solution.py:646
  585.9 29.2 %psum.22 = f32[2,384]{1,0:T(2,128)S(1)} all-reduce(f32[2,384]{1,0:T(2,128)S(1)} %pad_maximum_fusion.10), channel_id=1, replica_groups=mesh['o'=1,'k'=4,'c'=2,'h'=2,'b'=2] {'o','k','h'}, use_global_device_ids=true, to_apply=%region_9.10 | all-reduce | flops 768 | bytes 6144 | tf_op jit(solution)/shard_map/psum | solution.py:647
  620.7 15.3 %all-gather.11.cloned.1.call-done = bf16[8,144,512]{2,1,0:T(8,128)(2,1)} async-done(((bf16[1,144,512]{2,1,0:T(8,128)(2,1)}), bf16[8,144,512]{2,1,0:T(8,128)(2,1)}) %all-gather.11.cloned.1.call-update) | async-done | bytes 1179664 | tf_op jit(solution)/shard_map/all_gather | solution.py:602
  (220 shorter events, 90.0 us)
Async XLA Ops:
  7.2 130.8 %all-gather.15.cloned.1.call-start = ((), (), s32[]{:S(2)}) async-start(), calls=%async_computation.12 | async-start | bytes 5308416 | tf_op jit(solution)/shard_map/all_gather | solution.py:553
  10.8 49.5 %copy-start.23 = (bf16[2,3,512,128]{3,2,1,0:T(8,128)(2,1)S(1)}, bf16[2,3,512,128]{3,2,1,0:T(8,128)(2,1)}, u32[]{:S(2)}) copy-start(bf16[2,3,512,128]{3,2,1,0:T(8,128)(2,1)} %param.16) | copy-start | bytes 2359300
  32.8 110.3 %all-gather.13.cloned.1.call-start = ((), (), s32[]{:S(2)}) async-start(), calls=%async_computation.11 | async-start | bytes 5308416 | tf_op jit(solution)/shard_map/all_gather | solution.py:553
  50.6 312.5 %reduce-scatter.5.cloned.1.call-start = ((), (), s32[]{:S(2)}) async-start(), calls=%async_computation.5 | async-start | bytes 5308416 | tf_op jit(solution)/shard_map/reduce_scatter | solution.py:598
  50.7 12.4 %collective-permute-start.3 = (s32[1,4]{1,0:T(1,128)}, s32[1,4]{1,0:T(1,128)S(1)}, u32[]{:S(2)}, u32[]{:S(2)}) collective-permute-start(s32[1,4]{1,0:T(1,128)} %param.15), channel_id=1, source_target_pairs={{0,0},{1,1},{2,4},{3,5},{4,2},{5,3},{6,6},{7,7},{8,8},{9,9},{10,12... | collective-permute-start | bytes 56 | tf_op jit(solution)/shard_map/ppermute | solution.py:541
  52.0 11.2 %collective-permute-start.2 = (bf16[2,2,128]{2,1,0:T(2,128)(2,1)}, bf16[2,2,128]{2,1,0:T(2,128)(2,1)S(1)}, u32[]{:S(2)}, u32[]{:S(2)}) collective-permute-start(bf16[2,2,128]{2,1,0:T(2,128)(2,1)} %param.17), channel_id=1, source_target_pairs={{0,0},{1,1},{2,4},{3,5},{4,2},{5,3},{6,6},{7,7},{8,8},{9,9},{10,12... | collective-permute-start | bytes 3080 | tf_op jit(solution)/shard_map/ppermute | solution.py:541
  53.3 10.4 %collective-permute-start = (bf16[512,512]{1,0:T(8,128)(2,1)}, bf16[512,512]{1,0:T(8,128)(2,1)S(1)}, u32[]{:S(2)}, u32[]{:S(2)}) collective-permute-start(bf16[512,512]{1,0:T(8,128)(2,1)} %param.13), channel_id=1, source_target_pairs={{0,0},{1,1},{2,4},{3,5},{4,2},{5,3},{6,6},{7,7},{8,8},{9,9},{10,12... | collective-permute-start | bytes 1572872 | tf_op jit(solution)/shard_map/ppermute | solution.py:541
  55.0 175.1 %collective-permute-start.5 = (bf16[512,512]{1,0:T(8,128)(2,1)}, bf16[512,512]{1,0:T(8,128)(2,1)}, u32[]{:S(2)}, u32[]{:S(2)}) collective-permute-start(bf16[512,512]{1,0:T(8,128)(2,1)} %param.14), channel_id=1, source_target_pairs={{0,0},{1,1},{2,4},{3,5},{4,2},{5,3},{6,6},{7,7},{8,8},{9,9},{10,12... | collective-permute-start | bytes 1572872 | tf_op jit(solution)/shard_map/ppermute | solution.py:541
  61.0 3.9 collective-permute-start.1
  63.7 74.3 %copy-start.9 = (bf16[512,512]{1,0:T(8,128)(2,1)}, bf16[512,512]{1,0:T(8,128)(2,1)S(1)}, u32[]{:S(2)}) copy-start(bf16[512,512]{1,0:T(8,128)(2,1)S(1)} %collective-permute-done) | copy-start | bytes 1572868
  297.9 122.9 %copy-start = (f32[512,512]{1,0:T(8,128)}, f32[512,512]{1,0:T(8,128)S(1)}, u32[]{:S(2)}) copy-start(f32[512,512]{1,0:T(8,128)S(1)} %get-tuple-element.107.gmid_ref) | copy-start | bytes 3145732
  307.6 113.0 %reduce-scatter.9.cloned.1.call-start = ((), (), s32[]{:S(2)}) async-start(), calls=%async_computation.8 | async-start | bytes 5308416 | tf_op jit(solution)/shard_map/reduce_scatter | solution.py:598
  326.0 94.8 %copy-start.8 = (bf16[4,8,16,512]{3,2,1,0:T(8,128)(2,1)S(1)}, bf16[4,8,16,512]{3,2,1,0:T(8,128)(2,1)}, u32[]{:S(2)}) copy-start(bf16[4,8,16,512]{3,2,1,0:T(8,128)(2,1)} %copy-done.7) | copy-start | bytes 1572868
  326.0 156.7 %reduce-scatter.7.cloned.1.call-start = ((), (), s32[]{:S(2)}) async-start(), calls=%async_computation.6 | async-start | bytes 737280 | tf_op jit(solution)/shard_map/reduce_scatter | solution.py:599
  363.1 121.1 %reduce-scatter.11.cloned.1.call-start = ((), (), s32[]{:S(2)}) async-start(), calls=%async_computation.9 | async-start | bytes 737280 | tf_op jit(solution)/shard_map/reduce_scatter | solution.py:599
  420.7 163.4 %all-reduce.2.cloned.1.call-start = ((), (), s32[]{:S(2)}) async-start(), calls=%async_computation.4 | async-start | bytes 1572864 | tf_op jit(solution)/shard_map/psum | solution.py:646
  422.0 58.2 %copy-start.24 = (f32[384,512]{1,0:T(8,128)S(1)}, f32[384,512]{1,0:T(8,128)}, u32[]{:S(2)}) copy-start(f32[384,512]{1,0:T(8,128)} %get-tuple-element.43) | copy-start | bytes 2359300
  480.2 56.4 %copy-start.12 = (bf16[4,8,64,512]{3,2,1,0:T(8,128)(2,1)S(1)}, bf16[4,8,64,512]{3,2,1,0:T(8,128)(2,1)}, u32[]{:S(2)}) copy-start(bf16[4,8,64,512]{3,2,1,0:T(8,128)(2,1)} %copy-done.11) | copy-start | bytes 6291460
  482.6 137.1 %all-gather.9.cloned.1.call-start = ((), (), s32[]{:S(2)}) async-start(), calls=%async_computation.7 | async-start | bytes 1327104 | tf_op jit(solution)/shard_map/all_gather | solution.py:602
  483.4 152.6 %all-gather.11.cloned.1.call-start = ((), (), s32[]{:S(2)}) async-start(), calls=%async_computation.10 | async-start | bytes 1327104 | tf_op jit(solution)/shard_map/all_gather | solution.py:602
  531.3 87.0 %collective-permute-start.6 = (bf16[512,512]{1,0:T(8,128)(2,1)}, bf16[512,512]{1,0:T(8,128)(2,1)}, u32[]{:S(2)}, u32[]{:S(2)}) collective-permute-start(bf16[512,512]{1,0:T(8,128)(2,1)} %convert_element_type.161), channel_id=1, source_target_pairs={{0,0},{1,1},{2,4},{3,5},{4,2},{5,3},{6,6},{7,7},{8,8},{9,9},{10,12... | collective-permute-start | bytes 1572872 | tf_op jit(solution)/shard_map/ppermute | solution.py:541
  540.3 78.0 %collective-permute-start.4 = (bf16[512,512]{1,0:T(8,128)(2,1)}, bf16[512,512]{1,0:T(8,128)(2,1)S(1)}, u32[]{:S(2)}, u32[]{:S(2)}) collective-permute-start(bf16[512,512]{1,0:T(8,128)(2,1)} %fusion.23), channel_id=1, source_target_pairs={{0,0},{1,1},{2,4},{3,5},{4,2},{5,3},{6,6},{7,7},{8,8},{9,9},{10,12... | collective-permute-start | bytes 1572872 | tf_op jit(solution)/shard_map/ppermute | solution.py:541
  584.1 34.1 %collective-permute-start.7 = (bf16[2,384,512]{2,1,0:T(8,128)(2,1)}, bf16[2,384,512]{2,1,0:T(8,128)(2,1)S(1)}, u32[]{:S(2)}, u32[]{:S(2)}) collective-permute-start(bf16[2,384,512]{2,1,0:T(8,128)(2,1)} %all-reduce.2.cloned.1.call-done), channel_id=1, source_target_pairs={{0,0},{1,1},{2,4},{3,5},{4,2},{5,3},{6,6},{7,7},{8,8},{9,9},{10,12... | collective-permute-start | bytes 2359304 | tf_op jit(solution)/shard_map/ppermute | solution.py:541
  615.2 2.5 collective-permute-start.8
  (28 other events, 315.1 us)
Sparse Core Ops, SparseCore 0:
  32.9 39.1 all-gather.14
  74.6 38.9 all-gather.12
  307.7 55.2 reduce-scatter.4
  366.8 53.8 reduce-scatter.8
  422.8 24.1 reduce-scatter.6
  449.1 24.5 reduce-scatter.10
  482.7 101.3 all-reduce.1
  586.2 23.6 all-gather.8
  612.0 24.0 all-gather.10

commit v2 on v1

--- a/solution.py
+++ b/solution.py
@@ -261,10 +261,12 @@
     lse_ref,
     w_ref,
     neg_ref,
+    p_ref,
     gx_ref,
     gwt_ref,
     gb_ref,
     gln_ref,
+    e_ref,
     do_s,
     qt_s,
     qp_s,
@@ -286,14 +288,19 @@
     cr_sem,
     zs_sem,
     zr_sem,
+    *red_refs,
 ):
-    c = lax.axis_index("c")
-    b = lax.axis_index("b")
+    py, px, c, h, b = place()
     me = 2 * c + b
     rows = x_ref.shape[0]
     group = ag_ref.shape[0]
     ld = w_ref.shape[1] // 3
-    group_barrier(c, b)
+    red = Reducer(p_ref, e_ref, *red_refs)
+    meet(
+        [dev for _, dev in plane_peers(py, px, c)]
+        + [{"h": hh, "b": bb} for _, hh, bb in depth_peers(h, b)]
+        + [{"c": 1 - c, "b": 1 - b}]
+    )
     peers = [(1, c, 1 - b), (2, 1 - c, b), (3, 1 - c, 1 - b)]
     sends = []
     for slot, cc, bb in peers:
@@ -307,6 +314,7 @@
         )
         cp.start()
         sends.append(cp)
+    red.stage_a()
     do_s[me] = ga_ref[:, pl.ds(pl.multiple_of(me * ld, ld), ld)]
 
     def prep_q(i, carry):
@@ -334,6 +342,7 @@
         return carry
 
     lax.fori_loop(0, group, prep_do, 0)
+    red.stage_b()
     neg = neg_ref[0:1, 0:1]
     gwt_ref[...] = jnp.zeros(gwt_ref.shape, F32)
     gb_ref[...] = jnp.zeros(gb_ref.shape, F32)
@@ -426,6 +435,9 @@
         def _():
             relay(i + 1)
 
+        for n, stage in ((0, red.stage_c), (1, red.stage_d), (2, red.stage_e)):
+            pl.when(it == n)(stage)
+
         return carry
 
     lax.fori_loop(0, group, row, 0)
@@ -454,10 +466,12 @@
     core_copy(0, 0).wait_send()
     core_copy(0, 1).wait_send()
     z_copy.wait_send()
-
-
-def attn_bwd(ga, x, gain, gmid, ag, qkv, ot, lse, w, neg, cid):
+    red.finish()
+
+
+def attn_bwd(ga, x, gain, gmid, ag, qkv, ot, lse, w, neg, p, cid):
     rows, width = x.shape
+    p = p.reshape((2, 2, 2) + p.shape[1:])
     ld = w.shape[1] // 3
     g = 4
     return pl.pallas_call(
@@ -468,9 +482,10 @@
             jax.ShapeDtypeStruct((3 * ld, width), F32),
             jax.ShapeDtypeStruct((8, 3 * ld), F32),
             jax.ShapeDtypeStruct((8, width), F32),
+            jax.ShapeDtypeStruct((8,) + p.shape[4:], BF),
         ),
-        in_specs=vm(10),
-        out_specs=tuple(vm(4)),
+        in_specs=vm(11),
+        out_specs=tuple(vm(5)),
         scratch_shapes=[
             pltpu.VMEM((g, rows, ld), BF),
             pltpu.VMEM((g, ld, 2 * rows), BF),
@@ -493,20 +508,475 @@
             pltpu.SemaphoreType.DMA((2,)),
             pltpu.SemaphoreType.DMA,
             pltpu.SemaphoreType.DMA,
+        ]
+        + reducer_scratch(*p.shape[4:]),
+        compiler_params=pltpu.CompilerParams(
+            collective_id=cid, has_side_effects=True, vmem_limit_bytes=VMEM_LIMIT
+        ),
+    )(ga, x, gain, gmid, ag, qkv, ot, lse, w, neg, p)
+
+
+def gelu_both(x):
+    ax = jnp.abs(x)
+    e = jnp.exp2(x * x * (-0.5 * LOG2E))
+    t = 1.0 / (1.0 + ax * (0.3275911 * 0.7071067811865476))
+    poly = t * (
+        0.127414796
+        + t * (-0.142248368 + t * (0.7107068705 + t * (-0.7265760135 + t * 0.5307027145)))
+    )
+    tail = poly * e
+    cdf = jnp.where(x >= 0.0, 1.0 - tail, tail)
+    return x * cdf, cdf + x * e * 0.3989422804014327
+
+
+def mlp_fwd_kernel(
+    att_ref, x_ref, w_ref, bu_ref, vec_ref, mid_ref, hid_ref, dg_ref, out_ref, in_s
+):
+    n_out = att_ref.shape[1] // 32
+    n_up = (w_ref.shape[2] - n_out) // 2
+    quarter = w_ref.shape[3]
+    att_w = 8 * n_out
+    width = x_ref.shape[1]
+    acc = x_ref[...].astype(F32) + vec_ref[0:1, :]
+    for q in range(4):
+        wo = w_ref[:, q, :n_out, :].reshape(att_w, width)
+        acc = acc + nn(att_ref[:, q * att_w : (q + 1) * att_w], wo)
+    mid_ref[...] = acc
+    step = 64
+
+    def norm(it, carry):
+        at = pl.ds(pl.multiple_of(it * step, step), step)
+        n, _ = ln_parts(mid_ref[at, :])
+        in_s[at, :] = (n * vec_ref[2:3, :] + vec_ref[3:4, :]).astype(BF)
+        return carry
+
+    lax.fori_loop(0, x_ref.shape[0] // step, norm, 0)
+    out_ref[...] = mid_ref[...] + vec_ref[1:2, :]
+
+    def part(q, carry):
+        wu = w_ref[:, q, n_out : n_out + n_up, :].reshape(8 * n_up, quarter)
+        wd = w_ref[:, q, n_out + n_up :, :].reshape(8 * n_up, width)
+        half = 128
+
+        def chunk(r, cc):
+            at = pl.ds(pl.multiple_of(r * half, half), half)
+            pre = nn(in_s[at, :], wu) + bu_ref[q, 0:1, :]
+            act, der = gelu_both(pre)
+            act = act.astype(BF)
+            hid_ref[q, at, :] = act
+            dg_ref[q, at, :] = der.astype(BF)
+            out_ref[at, :] += nn(act, wd)
+            return cc
+
+        lax.fori_loop(0, x_ref.shape[0] // half, chunk, 0)
+        return carry
+
+    lax.fori_loop(0, 4, part, 0)
+
+
+def mlp_fwd(att, x, w, bu, vec):
+    rows, width = x.shape
+    quarter = w.shape[3]
+    return pl.pallas_call(
+        mlp_fwd_kernel,
+        name="mlp_fwd",
+        out_shape=(
+            jax.ShapeDtypeStruct((rows, width), F32),
+            jax.ShapeDtypeStruct((4, rows, quarter), BF),
+            jax.ShapeDtypeStruct((4, rows, quarter), BF),
+            jax.ShapeDtypeStruct((rows, width), F32),
+        ),
+        in_specs=vm(5),
+        out_specs=tuple(vm(4)),
+        scratch_shapes=[pltpu.VMEM((rows, width), BF)],
+        compiler_params=pltpu.CompilerParams(vmem_limit_bytes=VMEM_LIMIT),
+    )(att, x, w, bu, vec)
+
+
+def mlp_bwd_kernel(
+    g_ref,
+    mid_ref,
+    att_ref,
+    hid_ref,
+    dg_ref,
+    w_ref,
+    vec_ref,
+    p_ref,
+    gmid_ref,
+    ga_ref,
+    small_ref,
+    low_s,
+    lowt_s,
+    int_s,
+    gm_s,
+):
+    n_out = att_ref.shape[1] // 32
+    n_up = (w_ref.shape[2] - n_out) // 2
+    quarter = w_ref.shape[3]
+    att_w = 8 * n_out
+    rows, width = g_ref.shape
+    step = 64
+    small_ref[...] = jnp.zeros(small_ref.shape, F32)
+
+    def prep(it, carry):
+        at = pl.ds(pl.multiple_of(it * step, step), step)
+        g = g_ref[at, :]
+        low_s[at, :] = g.astype(BF)
+        small_ref[0:1, :] += jnp.sum(g, axis=0, keepdims=True)
+        return carry
+
+    lax.fori_loop(0, rows // step, prep, 0)
+
+    def flip(it, carry):
+        at = pl.ds(pl.multiple_of(it * 128, 128), 128)
+        lowt_s[:, at] = g_ref[at, :].T.astype(BF)
+        n, _ = ln_parts(mid_ref[at, :])
+        int_s[:, at] = (n * vec_ref[2:3, :] + vec_ref[3:4, :]).astype(BF).astype(F32).T.astype(BF)
+        return carry
+
+    for it in range(rows // 128):
+        flip(it, 0)
+    gm_s[...] = jnp.zeros(gm_s.shape, F32)
+
+    def put(q, first, count, val):
+        for r in range(8):
+            p_ref[r, q, first : first + count, :] = val[r * count : (r + 1) * count]
+
+    def part(q, carry):
+        wu = w_ref[:, q, n_out : n_out + n_up, :].reshape(8 * n_up, quarter)
+        wd = w_ref[:, q, n_out + n_up :, :].reshape(8 * n_up, width)
+        gh = nt(low_s[...], wd)
+        gp = (gh * dg_ref[q].astype(F32)).astype(BF)
+        small_ref[pl.ds(4 + q, 1), :] = jnp.sum(gp.astype(F32), axis=0, keepdims=True)
+        gm_s[...] += nt(gp, wu)
+        put(q, n_out, n_up, nn(int_s[...], gp).astype(BF))
+        put(q, n_out + n_up, n_up, nn(lowt_s[...], hid_ref[q]).astype(BF))
+        return carry
+
+    lax.fori_loop(0, 4, part, 0)
+
+    def norm(it, carry):
+        at = pl.ds(pl.multiple_of(it * step, step), step)
+        gm = gm_s[at, :]
+        n, rstd = ln_parts(mid_ref[at, :])
+        u = gm * vec_ref[2:3, :]
+        mu = jnp.mean(u, axis=-1, keepdims=True)
+        mun = jnp.mean(u * n, axis=-1, keepdims=True)
+        g = g_ref[at, :] + rstd * (u - mu - n * mun)
+        gmid_ref[at, :] = g
+        low_s[at, :] = g.astype(BF)
+        small_ref[1:2, :] += jnp.sum(g, axis=0, keepdims=True)
+        small_ref[2:3, :] += jnp.sum(gm * n, axis=0, keepdims=True)
+        small_ref[3:4, :] += jnp.sum(gm, axis=0, keepdims=True)
+        return carry
+
+    lax.fori_loop(0, rows // step, norm, 0)
+    for q in range(4):
+        wo = w_ref[:, q, :n_out, :].reshape(att_w, width)
+        cols = slice(q * att_w, (q + 1) * att_w)
+        ga_ref[:, cols] = nt(low_s[...], wo).astype(BF)
+        att_t = att_ref[:, cols].astype(F32).T.astype(BF)
+        put(q, 0, n_out, nn(att_t, low_s[...]).astype(BF))
+
+
+def mlp_bwd(g, mid, att, hid, dg, w, vec):
+    rows, width = g.shape
+    return pl.pallas_call(
+        mlp_bwd_kernel,
+        name="mlp_bwd",
+        out_shape=(
+            jax.ShapeDtypeStruct(w.shape, BF),
+            jax.ShapeDtypeStruct((rows, width), F32),
+            jax.ShapeDtypeStruct((rows, width), BF),
+            jax.ShapeDtypeStruct((8, width), F32),
+        ),
+        in_specs=vm(7),
+        out_specs=tuple(vm(4)),
+        scratch_shapes=[
+            pltpu.VMEM((rows, width), BF),
+            pltpu.VMEM((width, rows), BF),
+            pltpu.VMEM((width, rows), BF),
+            pltpu.VMEM((rows, width), F32),
+        ],
+        compiler_params=pltpu.CompilerParams(vmem_limit_bytes=VMEM_LIMIT),
+    )(g, mid, att, hid, dg, w, vec)
+
+
+def place():
+    k = lax.axis_index("k")
+    return lax.div(k, 2), lax.rem(k, 2), lax.axis_index("c"), lax.axis_index("h"), lax.axis_index("b")
+
+
+def plane_peers(y, x, c):
+    found = []
+    for dy in range(2):
+        for dx in range(2):
+            for dc in range(2):
+                if dy + dx + dc:
+                    yy = 1 - y if dy else y
+                    xx = 1 - x if dx else x
+                    cc = 1 - c if dc else c
+                    found.append((dy * 4 + dx * 2 + dc, {"k": 2 * yy + xx, "c": cc}))
+    return found
+
+
+def depth_peers(h, b):
+    return [(1, h, 1 - b), (2, 1 - h, b), (3, 1 - h, 1 - b)]
+
+
+def meet(devices):
+    bar = pltpu.get_barrier_semaphore()
+    for dev in devices:
+        pl.semaphore_signal(bar, inc=1, device_id=dev, device_id_type=MESH)
+    pl.semaphore_wait(bar, len(devices))
+
+
+def remote(src, dst, send, recv, dev):
+    return pltpu.make_async_remote_copy(
+        src_ref=src, dst_ref=dst, send_sem=send, recv_sem=recv, device_id=dev, device_id_type=MESH
+    )
+
+
+class Reducer:
+    def __init__(self, p_ref, e_ref, ra, rb1, rb2, rc, rd, s_sem, r_sem):
+        y, x, c, h, b = place()
+        self.at = (y, x, c, h, b)
+        self.bufs = (p_ref, e_ref, ra, rb1, rb2, rc, rd)
+        self.piece = c * 4 + y * 2 + x
+        core = {"c": 1 - c}
+        xp = {"k": 2 * y + 1 - x}
+        yp = {"k": 2 * (1 - y) + x}
+        n = iter(range(32))
+
+        def cp(src, dst, dev):
+            i = next(n)
+            return remote(src, dst, s_sem.at[i], r_sem.at[i], dev)
+
+        self.a = [cp(p_ref.at[1 - c], ra, core)]
+        self.b = [cp(ra.at[j, 1 - x, 0:2], rb1.at[j], xp) for j in range(2)]
+        self.b += [cp(ra.at[1 - y, j, 2:4], rb2.at[j], yp) for j in range(2)]
+        self.c = [cp(rb1.at[1 - y], rc.at[0:2], yp), cp(rb2.at[1 - x], rc.at[2:4], xp)]
+        self.d = [
+            cp(rc.at[2 * hh + bb], rd.at[i - 1], {"h": hh, "b": bb})
+            for i, hh, bb in depth_peers(h, b)
+        ]
+        self.e = [cp(e_ref.at[self.piece], e_ref.at[self.piece], dev) for _, dev in plane_peers(y, x, c)]
+
+    @staticmethod
+    def start(copies):
+        for one in copies:
+            one.start()
+
+    @staticmethod
+    def landed(copies):
+        for one in copies:
+            one.wait_recv()
+
+    def stage_a(self):
+        self.start(self.a)
+
+    def stage_b(self):
+        p_ref, e_ref, ra, rb1, rb2, rc, rd = self.bufs
+        c = self.at[2]
+        self.landed(self.a)
+
+        def add(i, carry):
+            yy, xx = lax.div(i, 2), lax.rem(i, 2)
+            for q in range(4):
+                ra[yy, xx, q] = (ra[yy, xx, q].astype(F32) + p_ref[c, yy, xx, q].astype(F32)).astype(BF)
+            return carry
+
+        lax.fori_loop(0, 4, add, 0)
+        self.start(self.b)
+
+    def stage_c(self):
+        p_ref, e_ref, ra, rb1, rb2, rc, rd = self.bufs
+        y, x = self.at[0], self.at[1]
+        self.landed(self.b)
+        for j in range(2):
+            for q in range(2):
+                rb1[j, q] = (rb1[j, q].astype(F32) + ra[j, x, q].astype(F32)).astype(BF)
+                rb2[j, q] = (rb2[j, q].astype(F32) + ra[y, j, 2 + q].astype(F32)).astype(BF)
+        self.start(self.c)
+
+    def stage_d(self):
+        p_ref, e_ref, ra, rb1, rb2, rc, rd = self.bufs
+        y, x = self.at[0], self.at[1]
+        self.landed(self.c)
+        for q in range(2):
+            rc[q] = (rc[q].astype(F32) + rb1[y, q].astype(F32)).astype(BF)
+            rc[2 + q] = (rc[2 + q].astype(F32) + rb2[x, q].astype(F32)).astype(BF)
+        self.start(self.d)
+
+    def stage_e(self):
+        p_ref, e_ref, ra, rb1, rb2, rc, rd = self.bufs
+        h, b = self.at[3], self.at[4]
+        self.landed(self.d)
+        tot = rc[2 * h + b].astype(F32) + rd[0].astype(F32) + rd[1].astype(F32) + rd[2].astype(F32)
+        e_ref[self.piece] = tot.astype(BF)
+        self.start(self.e)
+
+    def finish(self):
+        self.landed(self.e)
+        for group in (self.a, self.b, self.c, self.d, self.e):
+            for one in group:
+                one.wait_send()
+
+
+def reducer_scratch(rows, width):
+    return [
+        pltpu.VMEM((2, 2, 4, rows, width), BF),
+        pltpu.VMEM((2, 2, rows, width), BF),
+        pltpu.VMEM((2, 2, rows, width), BF),
+        pltpu.VMEM((4, rows, width), BF),
+        pltpu.VMEM((3, rows, width), BF),
+        pltpu.SemaphoreType.DMA((17,)),
+        pltpu.SemaphoreType.DMA((17,)),
+    ]
+
+
+def tail_kernel(
+    gw_ref, small_ref, gt_ref, gwo_ref, tot_ref, gto_ref, gw_s, rt, sm_in, sz, s_sem, r_sem, own_sem
+):
+    y, x, c, h, b = place()
+    k = 2 * y + x
+    pieces = gwo_ref.shape[0]
+    devs = [dev for _, dev in plane_peers(y, x, c)]
+    for dy in range(2):
+        for dx in range(2):
+            for dc in range(2):
+                yy = 1 - y if dy else y
+                xx = 1 - x if dx else x
+                devs.append({"k": 2 * yy + xx, "c": 1 - c if dc else c, "h": 1 - h})
+    devs += [{"h": h, "b": 1 - b}, {"h": 1 - h, "b": 1 - b}]
+    meet(devs)
+    gt_copy = remote(
+        gt_ref, gto_ref, s_sem.at[0], r_sem.at[0], {"c": 1 - c, "h": 1 - h}
+    )
+    gt_own = pltpu.make_async_copy(gt_ref, gto_ref, own_sem)
+    stays = c == h
+
+    small_copies = []
+    for i, dev in plane_peers(y, x, c):
+        one = remote(small_ref, sm_in.at[i - 1], s_sem.at[i], r_sem.at[i], dev)
+        one.start()
+        small_copies.append(one)
+
+    def pack(l, carry):
+        for p in range(8):
+            rows = gw_s.shape[2]
+            gw_s[p, l] = gw_ref[l, p * rows : (p + 1) * rows, :].astype(BF)
+        return carry
+
+    lax.fori_loop(0, gw_ref.shape[0], pack, 0)
+
+    def gw_copy(p):
+        dev = {"k": p // 2, "c": p % 2, "h": c}
+        return remote(
+            gw_s.at[p], rt.at[2 * k + h], s_sem.at[8 + p], r_sem.at[8 + 2 * k + h], dev
+        )
+
+    def at_home(p):
+        return (k == p // 2) & (c == p % 2) & stays
+
+    for p in range(8):
+        @pl.when(jnp.logical_not(at_home(p)))
+        def _():
+            gw_copy(p).start()
+
+        @pl.when(at_home(p))
+        def _():
+            rt[p // 2 * 2 + h] = gw_s[p]
+
+    @pl.when(jnp.logical_not(stays))
+    def _():
+        gt_copy.start()
+
+    @pl.when(stays)
+    def _():
+        gt_own.start()
+
+    acc = small_ref[...]
+    for i, one in enumerate(small_copies):
+        one.wait_recv()
+        acc = acc + sm_in[i]
+    sz[0] = acc
+    depth = []
+    for i, hh, bb in depth_peers(h, b):
+        one = remote(sz.at[0], sz.at[i], s_sem.at[15 + i], r_sem.at[15 + i], {"h": hh, "b": bb})
+        one.start()
+        depth.append(one)
+
+    def gw_landed(j):
+        one = remote(gw_s.at[0], rt.at[j], s_sem.at[8], r_sem.at[8 + j], {"c": 1 - c})
+        one.wait_recv()
+
+    for j in range(8):
+        @pl.when(jnp.logical_not(stays & (k == j // 2) & (h == j % 2)))
+        def _():
+            gw_landed(j)
+
+    me = 2 * k + c
+    for l in range(gw_ref.shape[0]):
+        tot = rt[0, l].astype(F32)
+        for j in range(1, 8):
+            tot = tot + rt[j, l].astype(F32)
+        gwo_ref[me, l] = tot.astype(BF)
+    plane = []
+    for i, dev in plane_peers(y, x, c):
+        one = remote(gwo_ref.at[me], gwo_ref.at[me], s_sem.at[18 + i], r_sem.at[18 + i], dev)
+        one.start()
+        plane.append(one)
+    acc = sz[0]
+    for i, one in enumerate(depth):
+        one.wait_recv()
+        acc = acc + sz[i + 1]
+    tot_ref[...] = acc
+    for one in plane:
+        one.wait_recv()
+
+    @pl.when(jnp.logical_not(stays))
+    def _():
+        gt_copy.wait()
+
+    @pl.when(stays)
+    def _():
+        gt_own.wait()
+
+    for one in small_copies + depth + plane:
+        one.wait_send()
+    for p in range(8):
+        @pl.when(jnp.logical_not(at_home(p)))
+        def _():
+            gw_copy(p).wait_send()
+
+
+def tail(gw, small, gt, cid):
+    layers, rows3, width = gw.shape
+    n = rows3 // 8
+    return pl.pallas_call(
+        tail_kernel,
+        name="tail_sums",
+        out_shape=(
+            jax.ShapeDtypeStruct((8, layers, n, width), BF),
+            jax.ShapeDtypeStruct(small.shape, F32),
+            jax.ShapeDtypeStruct(gt.shape, BF),
+        ),
+        in_specs=vm(3),
+        out_specs=tuple(vm(3)),
+        scratch_shapes=[
+            pltpu.VMEM((8, layers, n, width), BF),
+            pltpu.VMEM((8, layers, n, width), BF),
+            pltpu.VMEM((7,) + small.shape, F32),
+            pltpu.VMEM((4,) + small.shape, F32),
+            pltpu.SemaphoreType.DMA((26,)),
+            pltpu.SemaphoreType.DMA((26,)),
+            pltpu.SemaphoreType.DMA,
         ],
         compiler_params=pltpu.CompilerParams(
             collective_id=cid, has_side_effects=True, vmem_limit_bytes=VMEM_LIMIT
         ),
-    )(ga, x, gain, gmid, ag, qkv, ot, lse, w, neg)
-
-
-def gelu_act(values):
-    return jax.nn.gelu(values, approximate=False)
-
-
-def layer_norm(values, gain_row, bias_row):
-    n, _ = ln_parts(values)
-    return n * gain_row + bias_row
+    )(gw, small, gt)
 
 
 def shards(
@@ -557,12 +1027,9 @@
     n_out = ld // 8
     n_up = width // 8
 
-    def unpack(l):
-        g2, bu = weights[l]
-        wo = g2[:, :, :n_out].transpose(1, 0, 2, 3).reshape(4 * ld, width)
-        wu = g2[:, :, n_out : n_out + n_up].transpose(0, 2, 1, 3).reshape(width, 4 * quarter)
-        wd = g2[:, :, n_out + n_up :].transpose(1, 0, 2, 3).reshape(4 * quarter, width)
-        return wo, wu, wd, bu.reshape(1, 4 * quarter).astype(F32)
+    def vectors(l):
+        rows4 = [b_out[l].astype(F32), b_down[l].astype(F32), gains[l, 1], shifts[l, 1]]
+        return jnp.concatenate([jnp.stack(rows4), jnp.zeros((4, width), F32)])
 
     x = swap(tokens)
     wq = swap(jnp.transpose(w_qkv, (0, 2, 1, 3)).reshape(layers, width, 3 * ld))
@@ -584,92 +1051,63 @@
         ag, qkv, ot, lse, att = attn_fwd(
             stream, gains[l, 0][None], shifts[l, 0][None], wq[l], bias, neg, 2 * l
         )
-        wo, wu, wd, bu = unpack(l)
-        mid = stream + nn(att, wo) + b_out[l].astype(F32)
-        mlp_in = layer_norm(mid, gains[l, 1], shifts[l, 1]).astype(BF)
-        pre = nn(mlp_in, wu) + bu
-        hidden = gelu_act(pre).astype(BF)
-        nxt = mid + nn(hidden, wd) + b_down[l].astype(F32)
-        stored.append((stream, ag, qkv, ot, lse, att, mid, mlp_in, pre, hidden, wo, wu, wd))
+        w, bu = weights[l]
+        bu = jnp.broadcast_to(bu.astype(F32)[:, None], (4, 8, quarter))
+        vec = vectors(l)
+        mid, hid, dg, nxt = mlp_fwd(att, stream, w, bu, vec)
+        stored.append((stream, ag, qkv, ot, lse, att, mid, hid, dg, w, vec))
         stream = nxt
     output = swap(stream.astype(BF))
 
-    def reduce_big(g):
-        r1 = lax.psum_scatter(g, ("k", "c"), scatter_dimension=0, tiled=False)
-        r2 = lax.psum_scatter(r1, ("h", "b"), scatter_dimension=0, tiled=False)
-        if n_outer > 1:
-            r2 = lax.psum(r2, "o")
-        return lax.all_gather(r2, ("k", "c"), axis=0, tiled=False)
-
     grad = g_in.astype(F32)
-    outs = {k: [None] * layers for k in ("wqkv", "bqv", "wout", "wup", "bup", "wdown", "shared")}
+    keys = ("wqkv", "bqv", "small", "big")
+    outs = {k: [None] * layers for k in keys}
     for l in reversed(range(layers)):
-        stream_in, ag, qkv, ot, lse, att, mid, mlp_in, pre, hidden, wo, wu, wd = stored[l]
-        g_bdown = jnp.sum(grad, axis=0)
-        low = grad.astype(BF)
-        g_wd = lax.dot_general(hidden, low, (((0,), (0,)), ((), ())), preferred_element_type=F32)
-        g_hid = nt(low, wd)
-        g_pre = jax.vjp(gelu_act, pre)[1](g_hid)[0].astype(BF)
-        g_wu = lax.dot_general(mlp_in, g_pre, (((0,), (0,)), ((), ())), preferred_element_type=F32)
-        g_bup = jnp.sum(g_pre.astype(F32), axis=0)
-        g_mlp = nt(g_pre, wu)
-        n, rstd = ln_parts(mid)
-        u = g_mlp * gains[l, 1]
-        mu = jnp.mean(u, axis=-1, keepdims=True)
-        mun = jnp.mean(u * n, axis=-1, keepdims=True)
-        g_mid = grad + rstd * (u - mu - n * mun)
-        g_gain2 = jnp.sum(g_mlp * n, axis=0)
-        g_shift2 = jnp.sum(g_mlp, axis=0)
-        g_bout = jnp.sum(g_mid, axis=0)
-        mid_low = g_mid.astype(BF)
-        g_wo = lax.dot_general(att, mid_low, (((0,), (0,)), ((), ())), preferred_element_type=F32)
-        ga = nt(mid_low, wo).astype(BF)
-        grad, gwt, gb, gln = attn_bwd(
-            ga, stream_in, gains[l, 0][None], g_mid, ag, qkv, ot, lse, wq[l], neg, 2 * l + 1
+        stream_in, ag, qkv, ot, lse, att, mid, hid, dg, w, vec = stored[l]
+        p, g_mid, ga, small_l = mlp_bwd(grad, mid, att, hid, dg, w, vec)
+        grad, gwt, gb, gln, big = attn_bwd(
+            ga, stream_in, gains[l, 0][None], g_mid, ag, qkv, ot, lse, wq[l], neg, p, 2 * l + 1
         )
-        packed = jnp.concatenate(
-            [
-                g_wo.astype(BF).reshape(4, 8, n_out, width).transpose(1, 0, 2, 3),
-                g_wu.astype(BF).reshape(8, n_up, 4, quarter).transpose(0, 2, 1, 3),
-                g_wd.astype(BF).reshape(4, 8, quarter // 8, width).transpose(1, 0, 2, 3),
-            ],
-            axis=2,
-        )
-        red = reduce_big(packed).astype(F32)
-        outs["wout"][l] = red[:, :n_out].reshape(ld, width)
-        outs["wup"][l] = red[:, n_out : n_out + n_up].reshape(width, quarter)
-        outs["wdown"][l] = red[:, n_out + n_up :].reshape(quarter, width)
-        outs["wqkv"][l] = gwt.astype(BF)
-        outs["bqv"][l] = gb[0]
-        outs["bup"][l] = g_bup
-        outs["shared"][l] = jnp.stack([g_bout, g_bdown, gln[0], g_gain2, gln[1], g_shift2])
-    gq = lax.psum(jnp.stack(outs["wqkv"]), ("o", "k", "h"))
-    gbq = lax.psum(jnp.stack(outs["bqv"]), ("o", "k", "h"))
-    gq = swap(gq).astype(F32)
-    gbq = swap(gbq)
-    gq = gq.reshape(layers, 3, ld, width).transpose(0, 1, 3, 2)
-    gbq = jnp.stack([gbq[:, :ld], gbq[:, 2 * ld :]], axis=1)
-    flat = jnp.concatenate(
-        [jnp.stack(outs["bup"]).reshape(-1), jnp.stack(outs["shared"]).reshape(-1)]
-    )
-    flat = lax.psum(flat, AXES)
-    nb = layers * 4 * quarter
-    t = lax.axis_index("h") * 2 + lax.axis_index("b")
-    g_bup = lax.dynamic_slice_in_dim(flat[:nb].reshape(layers, 4 * quarter), t * quarter, quarter, 1)
-    sh = flat[nb:].reshape(layers, 6, width)
+        outs["wqkv"][l] = gwt
+        outs["bqv"][l] = gb[0:1]
+        outs["small"][l] = jnp.concatenate([small_l, gln[:2]])
+        outs["big"][l] = big
+    group_at = lax.axis_index("c") * 2 + lax.axis_index("b")
+    home = lax.axis_index("h") * 2 + lax.axis_index("b")
+    gbq = jnp.pad(jnp.concatenate(outs["bqv"]), ((0, 0), (0, width - 3 * ld)))
+    gbq = jnp.where(jnp.arange(4)[:, None, None] == group_at, gbq[None], 0.0)
+    flat = jnp.concatenate(outs["small"] + [gbq.reshape(4 * layers, width)])
+    n_small = flat.shape[0]
+    flat = jnp.pad(flat, ((0, -n_small % 8), (0, 0)))
+    gq, flat, g_tok = tail(jnp.stack(outs["wqkv"]), flat, grad.astype(BF), 2 * layers)
+    big = jnp.stack(outs["big"])
+    if n_outer > 1:
+        gq, flat, big = lax.psum((gq, flat, big), "o")
+    gq = gq.transpose(1, 0, 2, 3).reshape(layers, 3, ld, width).transpose(0, 1, 3, 2).astype(F32)
+    small = flat[: 10 * layers].reshape(layers, 10, width)
+    gbq = flat[10 * layers : n_small].reshape(4, layers, width)
+    gbq = lax.dynamic_index_in_dim(gbq, home, 0, keepdims=False)[:, : 3 * ld]
+    gbq = gbq.reshape(layers, 3, ld)[:, ::2]
+    n_out = ld // 8
+    n_up = width // 8
+    big = big.astype(F32)
+    g_wout = big[:, :, :n_out].reshape(layers, ld, width)
+    g_wup = big[:, :, n_out : n_out + n_up].reshape(layers, width, quarter)
+    g_wdown = big[:, :, n_out + n_up :].reshape(layers, width, quarter).transpose(0, 2, 1)
+    g_bup = lax.dynamic_index_in_dim(small[:, 4:8], home, 1, keepdims=False)
     return (
         output,
-        swap(grad.astype(BF)),
+        g_tok,
         gq,
         gbq,
-        jnp.stack(outs["wout"]),
-        sh[:, 0],
-        jnp.stack(outs["wup"]),
+        g_wout,
+        small[:, 1],
+        g_wup,
         g_bup,
-        jnp.stack(outs["wdown"]),
-        sh[:, 1],
-        sh[:, 2:4],
-        sh[:, 4:6],
+        g_wdown,
+        small[:, 0],
+        jnp.stack([small[:, 8], small[:, 2]], axis=1),
+        jnp.stack([small[:, 9], small[:, 3]], axis=1),
     )
 
 

time: 656 us -> 467 us (0.71)
  waiting for transfers between devices: 152 us -> 0.09 us
  Pallas kernels: 210 us -> 359 us
  blocking collectives: 108 us -> 35.9 us
  matrix products: 70.4 us -> 0 us
  local copies, waits for them, and re-layouts: 58.6 us -> 26.9 us
    pallas_call x0 -> x5, Pallas kernels: none -> 118 us  [the longest x1 50.7 us: tail(): pl.pallas_call(tail_kernel, name='tail_sums', out_shape=(jax.ShapeDtypeSt...]
    reduce_scatter x4 -> x0, waiting for transfers between devices: 94.6 us -> none  [the longest x2 94.5 us: reduce_big(): r1 = lax.psum_scatter(g, ('k', 'c'), scatter_dimension=0, tiled=False)]
    psum x2 -> x0, blocking collectives: 71.8 us -> none  [the longest x1 42.6 us: shards(): flat = lax.psum(flat, AXES)]
    dot_general x18 -> x0, matrix products: 70.4 us -> none  [the longest x6 43.8 us: nn(): return jnp.dot(a, b, preferred_element_type=F32)]
    psum x1 -> x0, waiting for transfers between devices: 41.5 us -> none  [shards(): gq = lax.psum(jnp.stack(outs['wqkv']), ('o', 'k', 'h'))]
    pallas_call x2, Pallas kernels: 103 us -> 136 us  [attn_bwd(): pl.pallas_call(attn_bwd_kernel, name='attn_bwd', out_shape=(jax.ShapeDtyp...]
    all_gather x2 -> x0, waiting for transfers between devices: 15.3 us -> none  [reduce_big(): return lax.all_gather(r2, ('k', 'c'), axis=0, tiled=False)]
    reshape x10 -> x4, local copies, waits for them, and re-layouts: 17.1 us -> 1.84 us  [the longest x1 1.8 us: shards(): big[:, :, n_out + n_up:].reshape(layers, width, quarter).transpose(0, 2, 1)]
  transfers between devices with their start and end apart: 18 -> 8, of which waited for: 4 -> 0; matrix products, arithmetic and copies ran while one was open for 15% -> 4% of each run, Pallas kernels for 25% -> 26%
where the time goes in v2:
time: 467 us; the launch traced here: 466 us
  Pallas kernels  359 us (77%)
  blocking collectives  35.9 us (8%)
  local copies, waits for them, and re-layouts  26.9 us (6%)
  starting transfers between devices  14.7 us (3%)
  other arithmetic  14.5 us (3%)
  between operations  14.5 us (3%)
    pallas_call x2, Pallas kernels, attn_bwd(): pl.pallas_call(attn_bwd_kernel, name='attn_bwd', out_shape=(jax.ShapeDtyp...  136 us
    pallas_call x2, Pallas kernels, attn_fwd(): pl.pallas_call(attn_fwd_kernel, name='attn_fwd', out_shape=(jax.ShapeDtyp...  105 us
    pallas_call x1, Pallas kernels, tail(): pl.pallas_call(tail_kernel, name='tail_sums', out_shape=(jax.ShapeDtypeSt...  50.7 us
    all_gather x2, blocking collectives, gather_weights(): g1 = lax.all_gather(own, ('h', 'b'), axis=0, tiled=False)  35.9 us
    pallas_call x2, Pallas kernels, mlp_fwd(): pl.pallas_call(mlp_fwd_kernel, name='mlp_fwd', out_shape=(jax.ShapeDtypeS...  34.6 us
    pallas_call x2, Pallas kernels, mlp_bwd(): pl.pallas_call(mlp_bwd_kernel, name='mlp_bwd', out_shape=(jax.ShapeDtypeS...  32.3 us
    ppermute x6, starting transfers between devices, swap(): return lax.ppermute(v, AXES, perm)  14.6 us
  transfers between devices with their start and end apart: 8, of which 0 were waited for; matrix products, arithmetic and copies ran while one was open for 4% of the time, Pallas kernels for 26%

profile of v2, /device:TPU:0, one launch (start us, length us, event | category | flops | bytes accessed | tf_op | source)
XLA Modules:
  0.0 465.5 jit_solution(4136088266442124294)
XLA Ops:
  9.0 1.3 fusion.5
  12.1 19.6 %all-gather = bf16[640,512]{1,0:T(8,128)(2,1)S(1)} all-gather(bf16[160,512]{1,0:T(8,128)(2,1)S(1)} %pad_maximum_fusion.2), channel_id=2, replica_groups=mesh['o'=1,'k'=4,'c'=2,'h'=2,'b'=2] {'h','b'}, dimensions={0}, use_global_device_ids=true | all-gather | bytes 819200 | tf_op jit(solution)/shard_map/all_gather | solution.py:1022
  32.7 16.3 %all-gather.2 = bf16[640,512]{1,0:T(8,128)(2,1)S(1)} all-gather(bf16[160,512]{1,0:T(8,128)(2,1)S(1)} %pad_maximum_fusion.3), channel_id=4, replica_groups=mesh['o'=1,'k'=4,'c'=2,'h'=2,'b'=2] {'h','b'}, dimensions={0}, use_global_device_ids=true | all-gather | bytes 819200 | tf_op jit(solution)/shard_map/all_gather | solution.py:1022
  51.4 5.4 %collective-permute-start = (bf16[512,512]{1,0:T(8,128)(2,1)}, bf16[512,512]{1,0:T(8,128)(2,1)}, u32[]{:S(2)}, u32[]{:S(2)}) collective-permute-start(bf16[512,512]{1,0:T(8,128)(2,1)} %param.13), channel_id=1, source_target_pairs={{0,0},{1,1},{2,4},{3,5},{4,2},{5,3},{6,6},{7,7},{8,8},{9,9},{10,12... | collective-permute-start | bytes 1572872 | tf_op jit(solution)/shard_map/ppermute | solution.py:1011
  56.8 1.7 collective-permute-start.5
  63.2 2.1 convert_element_type.77.x_ref
  65.4 1.1 convert_element_type.87.g_ref
  68.0 69.2 %attn_fwd.2 = (bf16[4,512,512]{2,1,0:T(8,128)(2,1)}, bf16[4,512,384]{2,1,0:T(8,128)(2,1)}, f32[4,128,512]{2,1,0:T(8,128)}, f32[4,8,1024]{2,1,0:T(8,128)}, bf16[512,512]{1,0:T(8,128)(2,1)}) custom-call(f32[512,512]{1,0:T(8,128)} %convert_element_type.77.x_ref, f32[1,512]{1,0:T(1,128)} %get-tuple-element.139.gain_ref, f32[1,512]{1,0:T(1,128)} %get-tuple-element.135.shift_ref, ...), custom_call_target="tpu_custom_call" | custom-call | tf_op jit(solution)/shard_map/attn_fwd/pallas_call | solution.py:225
  137.9 17.4 %mlp_fwd.2 = (f32[512,512]{1,0:T(8,128)}, bf16[4,512,512]{2,1,0:T(8,128)(2,1)}, bf16[4,512,512]{2,1,0:T(8,128)(2,1)}, f32[512,512]{1,0:T(8,128)}) custom-call(bf16[512,512]{1,0:T(8,128)(2,1)} %get-tuple-element.51.att_ref, f32[512,512]{1,0:T(8,128)} %convert_element_type.77.x_ref, bf16[8,4,144,512]{3,2,1,0:T(8,128)(2,1)} %bitcast.81, ...), custom_call_target="tpu_custom_call" | custom-call | tf_op jit(solution)/shard_map/mlp_fwd/pallas_call | solution.py:580
  155.3 35.9 %attn_fwd.3 = (bf16[4,512,512]{2,1,0:T(8,128)(2,1)}, bf16[4,512,384]{2,1,0:T(8,128)(2,1)}, f32[4,128,512]{2,1,0:T(8,128)}, f32[4,8,1024]{2,1,0:T(8,128)}, bf16[512,512]{1,0:T(8,128)(2,1)}) custom-call(f32[512,512]{1,0:T(8,128)} %get-tuple-element.52.x_ref, f32[1,512]{1,0:T(1,128)} %get-tuple-element.137.gain_ref, f32[1,512]{1,0:T(1,128)} %get-tuple-element.133.shift_ref, ...), custom_call_target="tpu_custom_call" | custom-call | tf_op jit(solution)/shard_map/attn_fwd/pallas_call | solution.py:225
  191.9 17.3 %mlp_fwd.3 = (f32[512,512]{1,0:T(8,128)}, bf16[4,512,512]{2,1,0:T(8,128)(2,1)}, bf16[4,512,512]{2,1,0:T(8,128)(2,1)}, f32[512,512]{1,0:T(8,128)}) custom-call(bf16[512,512]{1,0:T(8,128)(2,1)} %get-tuple-element.53.att_ref, f32[512,512]{1,0:T(8,128)} %get-tuple-element.52.x_ref, bf16[8,4,144,512]{3,2,1,0:T(8,128)(2,1)} %bitcast.83, ...), custom_call_target="tpu_custom_call" | custom-call | tf_op jit(solution)/shard_map/mlp_fwd/pallas_call | solution.py:580
  209.2 16.2 %mlp_bwd.2 = (bf16[8,4,144,512]{3,2,1,0:T(8,128)(2,1)}, f32[512,512]{1,0:T(8,128)}, bf16[512,512]{1,0:T(8,128)(2,1)}, f32[8,512]{1,0:T(8,128)}) custom-call(f32[512,512]{1,0:T(8,128)} %convert_element_type.87.g_ref, f32[512,512]{1,0:T(8,128)} %get-tuple-element.55.mid_ref, bf16[512,512]{1,0:T(8,128)(2,1)} %get-tuple-element.53.att_ref, ...), custom_call_target="tpu_custom_call" | custom-call | tf_op jit(solution)/shard_map/mlp_bwd/pallas_call | solution.py:684
  225.4 69.4 %attn_bwd.2 = (f32[512,512]{1,0:T(8,128)}, f32[384,512]{1,0:T(8,128)}, f32[8,384]{1,0:T(8,128)}, f32[8,512]{1,0:T(8,128)}, bf16[8,144,512]{2,1,0:T(8,128)(2,1)}) custom-call(bf16[512,512]{1,0:T(8,128)(2,1)} %get-tuple-element.58.ga_ref, f32[512,512]{1,0:T(8,128)} %get-tuple-element.52.x_ref, f32[1,512]{1,0:T(1,128)} %get-tuple-element.137.gain_ref, ...), custom_call_target="tpu_custom_call" | custom-call | tf_op jit(solution)/shard_map/attn_bwd/pallas_call | solution.py:477
  294.8 16.2 %mlp_bwd.3 = (bf16[8,4,144,512]{3,2,1,0:T(8,128)(2,1)}, f32[512,512]{1,0:T(8,128)}, bf16[512,512]{1,0:T(8,128)(2,1)}, f32[8,512]{1,0:T(8,128)}) custom-call(f32[512,512]{1,0:T(8,128)} %get-tuple-element.65.g_ref, f32[512,512]{1,0:T(8,128)} %get-tuple-element.66.mid_ref, bf16[512,512]{1,0:T(8,128)(2,1)} %get-tuple-element.51.att_ref, ...), custom_call_target="tpu_custom_call" | custom-call | tf_op jit(solution)/shard_map/mlp_bwd/pallas_call | solution.py:684
  310.9 66.8 %attn_bwd.3 = (f32[512,512]{1,0:T(8,128)}, f32[384,512]{1,0:T(8,128)}, f32[8,384]{1,0:T(8,128)}, f32[8,512]{1,0:T(8,128)}, bf16[8,144,512]{2,1,0:T(8,128)(2,1)}) custom-call(bf16[512,512]{1,0:T(8,128)(2,1)} %get-tuple-element.69.ga_ref, f32[512,512]{1,0:T(8,128)} %convert_element_type.77.x_ref, f32[1,512]{1,0:T(1,128)} %get-tuple-element.139.gain_ref, ...), custom_call_target="tpu_custom_call" | custom-call | tf_op jit(solution)/shard_map/attn_bwd/pallas_call | solution.py:477
  381.7 2.1 convert_element_type.88.gt_ref
  383.8 1.3 pad_maximum_fusion.gw_ref
  385.1 50.7 %tail_sums.1 = (bf16[8,2,48,512]{3,2,1,0:T(8,128)(2,1)}, f32[32,512]{1,0:T(8,128)}, bf16[512,512]{1,0:T(8,128)(2,1)}) custom-call(f32[2,384,512]{2,1,0:T(8,128)} %pad_maximum_fusion.gw_ref, f32[32,512]{1,0:T(8,128)} %pad.9.small_ref, bf16[512,512]{1,0:T(8,128)(2,1)} %convert_element_type.88.gt_ref), custom_call_target="tpu_custom_call" | custom-call | tf_op jit(solution)/shard_map/tail_sums/pallas_call | solution.py:957
  440.8 5.3 %collective-permute-start.4 = (bf16[512,512]{1,0:T(8,128)(2,1)}, bf16[512,512]{1,0:T(8,128)(2,1)}, u32[]{:S(2)}, u32[]{:S(2)}) collective-permute-start(bf16[512,512]{1,0:T(8,128)(2,1)} %convert_element_type.86), channel_id=1, source_target_pairs={{0,0},{1,1},{2,4},{3,5},{4,2},{5,3},{6,6},{7,7},{8,8},{9,9},{10,12... | collective-permute-start | bytes 1572872 | tf_op jit(solution)/shard_map/ppermute | solution.py:1011
  446.5 1.6 copy.36
  448.1 3.1 fusion
  451.2 1.8 copy.35
  454.3 1.8 maximum_convert_fusion.1
  456.0 1.9 copy.54
  (115 shorter events, 25.6 us)
Async XLA Ops:
  7.2 3.1 copy-start.2
  7.2 130.1 %all-gather.7.cloned.1.call-start = ((), (), s32[]{:S(2)}) async-start(), calls=%async_computation | async-start | bytes 5308416 | tf_op jit(solution)/shard_map/all_gather | solution.py:1023
  32.6 17.3 %copy-start.15 = (s32[1,4]{1,0:T(1,128)S(1)}, s32[1,4]{1,0:T(1,128)}, u32[]{:S(2)}) copy-start(s32[1,4]{1,0:T(1,128)} %param.15) | copy-start | bytes 52
  32.6 18.1 %copy-start.14 = (bf16[2,2,128]{2,1,0:T(2,128)(2,1)S(1)}, bf16[2,2,128]{2,1,0:T(2,128)(2,1)}, u32[]{:S(2)}) copy-start(bf16[2,2,128]{2,1,0:T(2,128)(2,1)} %param.17) | copy-start | bytes 3076
  32.6 25.9 %copy-start.3 = (bf16[2,3,512,128]{3,2,1,0:T(8,128)(2,1)S(1)}, bf16[2,3,512,128]{3,2,1,0:T(8,128)(2,1)}, u32[]{:S(2)}) copy-start(bf16[2,3,512,128]{3,2,1,0:T(8,128)(2,1)} %param.16) | copy-start | bytes 2359300
  32.6 158.7 %all-gather.9.cloned.1.call-start = ((), (), s32[]{:S(2)}) async-start(), calls=%async_computation.1 | async-start | bytes 5308416 | tf_op jit(solution)/shard_map/all_gather | solution.py:1023
  49.9 10.2 %copy-start.12 = (bf16[2,2,512]{2,1,0:T(2,128)(2,1)S(1)}, bf16[2,2,512]{2,1,0:T(2,128)(2,1)}, u32[]{:S(2)}) copy-start(bf16[2,2,512]{2,1,0:T(2,128)(2,1)} %param.24) | copy-start | bytes 12292
  49.9 10.2 %copy-start.13 = (bf16[2,2,512]{2,1,0:T(2,128)(2,1)S(1)}, bf16[2,2,512]{2,1,0:T(2,128)(2,1)}, u32[]{:S(2)}) copy-start(bf16[2,2,512]{2,1,0:T(2,128)(2,1)} %param.25) | copy-start | bytes 12292
  49.9 11.4 %copy-start.10 = (bf16[2,512]{1,0:T(2,128)(2,1)S(1)}, bf16[2,512]{1,0:T(2,128)(2,1)}, u32[]{:S(2)}) copy-start(bf16[2,512]{1,0:T(2,128)(2,1)} %param.23) | copy-start | bytes 6148
  49.9 11.4 %copy-start.11 = (bf16[2,512]{1,0:T(2,128)(2,1)S(1)}, bf16[2,512]{1,0:T(2,128)(2,1)}, u32[]{:S(2)}) copy-start(bf16[2,512]{1,0:T(2,128)(2,1)} %param.19) | copy-start | bytes 6148
  49.9 12.7 %collective-permute-start.3 = (s32[1,4]{1,0:T(1,128)S(1)}, s32[1,4]{1,0:T(1,128)S(1)}, u32[]{:S(2)}, u32[]{:S(2)}) collective-permute-start(s32[1,4]{1,0:T(1,128)S(1)} %copy-done.15), channel_id=1, source_target_pairs={{0,0},{1,1},{2,4},{3,5},{4,2},{5,3},{6,6},{7,7},{8,8},{9,9},{10,12... | collective-permute-start | bytes 56 | tf_op jit(solution)/shard_map/ppermute | solution.py:1011
  50.7 11.9 %collective-permute-start.2 = (bf16[2,2,128]{2,1,0:T(2,128)(2,1)S(1)}, bf16[2,2,128]{2,1,0:T(2,128)(2,1)S(1)}, u32[]{:S(2)}, u32[]{:S(2)}) collective-permute-start(bf16[2,2,128]{2,1,0:T(2,128)(2,1)S(1)} %copy-done.14), channel_id=1, source_target_pairs={{0,0},{1,1},{2,4},{3,5},{4,2},{5,3},{6,6},{7,7},{8,8},{9,9},{10,12... | collective-permute-start | bytes 3080 | tf_op jit(solution)/shard_map/ppermute | solution.py:1011
  51.4 11.9 %collective-permute-start = (bf16[512,512]{1,0:T(8,128)(2,1)}, bf16[512,512]{1,0:T(8,128)(2,1)}, u32[]{:S(2)}, u32[]{:S(2)}) collective-permute-start(bf16[512,512]{1,0:T(8,128)(2,1)} %param.13), channel_id=1, source_target_pairs={{0,0},{1,1},{2,4},{3,5},{4,2},{5,3},{6,6},{7,7},{8,8},{9,9},{10,12... | collective-permute-start | bytes 1572872 | tf_op jit(solution)/shard_map/ppermute | solution.py:1011
  56.8 8.6 %collective-permute-start.5 = (bf16[512,512]{1,0:T(8,128)(2,1)}, bf16[512,512]{1,0:T(8,128)(2,1)S(1)}, u32[]{:S(2)}, u32[]{:S(2)}) collective-permute-start(bf16[512,512]{1,0:T(8,128)(2,1)} %param.14), channel_id=1, source_target_pairs={{0,0},{1,1},{2,4},{3,5},{4,2},{5,3},{6,6},{7,7},{8,8},{9,9},{10,12... | collective-permute-start | bytes 1572872 | tf_op jit(solution)/shard_map/ppermute | solution.py:1011
  59.1 7.4 %collective-permute-start.1 = (bf16[2,512,384]{2,1,0:T(8,128)(2,1)S(1)}, bf16[2,512,384]{2,1,0:T(8,128)(2,1)S(1)}, u32[]{:S(2)}, u32[]{:S(2)}) collective-permute-start(bf16[2,512,384]{2,1,0:T(8,128)(2,1)S(1)} %copy.33), channel_id=1, source_target_pairs={{0,0},{1,1},{2,4},{3,5},{4,2},{5,3},{6,6},{7,7},{8,8},{9,9},{10,12... | collective-permute-start | bytes 2359304 | tf_op jit(solution)/shard_map/ppermute | solution.py:1011
  310.9 69.9 %copy-start.8 = (f32[8,512]{1,0:T(8,128)S(1)}, f32[8,512]{1,0:T(8,128)}, u32[]{:S(2)}) copy-start(f32[8,512]{1,0:T(8,128)} %get-tuple-element.80) | copy-start | bytes 49156
  310.9 69.9 %copy-start.9 = (f32[8,512]{1,0:T(8,128)S(1)}, f32[8,512]{1,0:T(8,128)}, u32[]{:S(2)}) copy-start(f32[8,512]{1,0:T(8,128)} %get-tuple-element.78) | copy-start | bytes 49156
  377.7 6.1 %copy-start.4 = (f32[384,512]{1,0:T(8,128)S(1)}, f32[384,512]{1,0:T(8,128)}, u32[]{:S(2)}) copy-start(f32[384,512]{1,0:T(8,128)} %get-tuple-element.77) | copy-start | bytes 2359300
  377.7 6.0 %copy-start.5 = (f32[384,512]{1,0:T(8,128)S(1)}, f32[384,512]{1,0:T(8,128)}, u32[]{:S(2)}) copy-start(f32[384,512]{1,0:T(8,128)} %get-tuple-element.76) | copy-start | bytes 2359300
  383.8 53.7 %copy-start.1 = (f32[512,512]{1,0:T(8,128)S(1)}, f32[512,512]{1,0:T(8,128)}, u32[]{:S(2)}) copy-start(f32[512,512]{1,0:T(8,128)} %get-tuple-element.54) | copy-start | bytes 3145732
  435.8 10.4 %copy-start.6 = (bf16[8,2,48,512]{3,2,1,0:T(8,128)(2,1)S(1)}, bf16[8,2,48,512]{3,2,1,0:T(8,128)(2,1)}, u32[]{:S(2)}) copy-start(bf16[8,2,48,512]{3,2,1,0:T(8,128)(2,1)} %get-tuple-element.86) | copy-start | bytes 2359300
  440.8 15.2 %collective-permute-start.4 = (bf16[512,512]{1,0:T(8,128)(2,1)}, bf16[512,512]{1,0:T(8,128)(2,1)}, u32[]{:S(2)}, u32[]{:S(2)}) collective-permute-start(bf16[512,512]{1,0:T(8,128)(2,1)} %convert_element_type.86), channel_id=1, source_target_pairs={{0,0},{1,1},{2,4},{3,5},{4,2},{5,3},{6,6},{7,7},{8,8},{9,9},{10,12... | collective-permute-start | bytes 1572872 | tf_op jit(solution)/shard_map/ppermute | solution.py:1011
  446.5 1.6 copy-start
  453.0 4.9 %copy-start.7 = (bf16[512,512]{1,0:T(8,128)(2,1)S(1)}, bf16[512,512]{1,0:T(8,128)(2,1)}, u32[]{:S(2)}) copy-start(bf16[512,512]{1,0:T(8,128)(2,1)} %get-tuple-element.169) | copy-start | bytes 1572868
Sparse Core Ops, SparseCore 0:
  32.7 39.2 all-gather.6
  73.9 38.8 all-gather.8

commit v3 on v2

--- a/solution.py
+++ b/solution.py
@@ -250,57 +250,54 @@
     )(x, gain, shift, w, bias, neg)
 
 
-def attn_bwd_kernel(
-    ga_ref,
-    x_ref,
-    gain_ref,
-    gmid_ref,
-    ag_ref,
-    qkv_ref,
-    ot_ref,
-    lse_ref,
-    w_ref,
-    neg_ref,
-    p_ref,
-    gx_ref,
-    gwt_ref,
-    gb_ref,
-    gln_ref,
-    e_ref,
-    do_s,
-    qt_s,
-    qp_s,
-    dot_s,
-    dop_s,
-    kt_s,
-    delta_s,
-    dk_s,
-    dv_s,
-    dqt_s,
-    part_s,
-    core_in,
-    zsend_s,
-    z_in,
-    own_s,
-    a2a_send,
-    a2a_recv,
-    cs_sem,
-    cr_sem,
-    zs_sem,
-    zr_sem,
-    *red_refs,
-):
+BWD_IN = (
+    "ga_ref", "x_ref", "gain_ref", "gmid_ref", "ag_ref", "qkv_ref", "ot_ref", "lse_ref", "w_ref",
+    "neg_ref", "p_ref",
+)
+BWD_OUT = (
+    "gx_ref", "gw_ref", "gb_ref", "gln_ref", "rc_ref",
+)
+BWD_SCRATCH = (
+    "do_s", "qt_s", "qp_s", "dot_s", "dop_s", "kt_s", "delta_s", "dk_s", "dv_s", "dqt_s", "part_s",
+    "core_in", "zsend_s", "z_in", "own_s", "gwt_s", "a2a_send", "a2a_recv", "cs_sem", "cr_sem",
+    "zs_sem", "zr_sem", "ra", "rb1", "rb2", "rs", "rr",
+)
+CLOSE_IN = ("crc", "cgw")
+CLOSE_OUT = ("ce", "cgwo")
+CLOSE_SCRATCH = ("crd", "crt", "ccs", "ccr")
+
+
+def attn_bwd_kernel(closing, *refs):
+    names = BWD_IN + (CLOSE_IN if closing else ("sw_in",))
+    names += BWD_OUT + (CLOSE_OUT if closing else ("sw_out",))
+    names += BWD_SCRATCH + (CLOSE_SCRATCH if closing else ("sw_sem",))
+    r = Refs(names, refs)
+    ga_ref, x_ref, gain_ref, gmid_ref, ag_ref, qkv_ref = (
+        r.ga_ref, r.x_ref, r.gain_ref, r.gmid_ref, r.ag_ref, r.qkv_ref
+    )
+    ot_ref, lse_ref, w_ref, neg_ref = r.ot_ref, r.lse_ref, r.w_ref, r.neg_ref
+    gx_ref, gb_ref, gln_ref = r.gx_ref, r.gb_ref, r.gln_ref
+    do_s, qt_s, qp_s, dot_s, dop_s, kt_s = r.do_s, r.qt_s, r.qp_s, r.dot_s, r.dop_s, r.kt_s
+    delta_s, dk_s, dv_s, dqt_s, part_s = r.delta_s, r.dk_s, r.dv_s, r.dqt_s, r.part_s
+    core_in, zsend_s, z_in, own_s, gwt_ref = r.core_in, r.zsend_s, r.z_in, r.own_s, r.gwt_s
+    a2a_send, a2a_recv, cs_sem, cr_sem, zs_sem, zr_sem = (
+        r.a2a_send, r.a2a_recv, r.cs_sem, r.cr_sem, r.zs_sem, r.zr_sem
+    )
     py, px, c, h, b = place()
     me = 2 * c + b
     rows = x_ref.shape[0]
     group = ag_ref.shape[0]
     ld = w_ref.shape[1] // 3
-    red = Reducer(p_ref, e_ref, *red_refs)
-    meet(
-        [dev for _, dev in plane_peers(py, px, c)]
-        + [{"h": hh, "b": bb} for _, hh, bb in depth_peers(h, b)]
-        + [{"c": 1 - c, "b": 1 - b}]
-    )
+    red = Reducer(r.p_ref, r.rc_ref, r.ra, r.rb1, r.rb2, r.rs, r.rr)
+    if closing:
+        close = Closer(r.crc, r.cgw, r.ce, r.cgwo, r.crd, r.crt, r.ccs, r.ccr)
+        meet(all_near(py, px, c, h, b))
+    else:
+        swap = Swap(r.sw_in, r.sw_out, r.sw_sem)
+        meet(
+            [dev for _, dev in plane_peers(py, px, c)]
+            + [{"b": 1 - b}, {"c": 1 - c, "b": 1 - b}, {"c": 1 - c, "h": 1 - h}]
+        )
     peers = [(1, c, 1 - b), (2, 1 - c, b), (3, 1 - c, 1 - b)]
     sends = []
     for slot, cc, bb in peers:
@@ -343,6 +340,10 @@
 
     lax.fori_loop(0, group, prep_do, 0)
     red.stage_b()
+    if closing:
+        close.stage_1()
+    else:
+        swap.start()
     neg = neg_ref[0:1, 0:1]
     gwt_ref[...] = jnp.zeros(gwt_ref.shape, F32)
     gb_ref[...] = jnp.zeros(gb_ref.shape, F32)
@@ -435,8 +436,9 @@
         def _():
             relay(i + 1)
 
-        for n, stage in ((0, red.stage_c), (1, red.stage_d), (2, red.stage_e)):
-            pl.when(it == n)(stage)
+        pl.when(it == 0)(red.stage_c)
+        if closing:
+            pl.when(it == 1)(close.stage_2)
 
         return carry
 
@@ -455,7 +457,7 @@
         u = g * gain_ref[...]
         mu = jnp.mean(u, axis=-1, keepdims=True)
         mun = jnp.mean(u * n, axis=-1, keepdims=True)
-        gx_ref[at, :] = gmid_ref[at, :] + rstd * (u - mu - n * mun)
+        gx_ref[at, :] = (gmid_ref[at, :] + rstd * (u - mu - n * mun)).astype(gx_ref.dtype)
         gln_ref[0:1, :] += jnp.sum(g * n, axis=0, keepdims=True)
         gln_ref[1:2, :] += jnp.sum(g, axis=0, keepdims=True)
         return carry
@@ -466,26 +468,46 @@
     core_copy(0, 0).wait_send()
     core_copy(0, 1).wait_send()
     z_copy.wait_send()
+    n = r.gw_ref.shape[1]
+    for i in range(8):
+        r.gw_ref[i] = gwt_ref[i * n : (i + 1) * n, :].astype(BF)
     red.finish()
-
-
-def attn_bwd(ga, x, gain, gmid, ag, qkv, ot, lse, w, neg, p, cid):
+    if closing:
+        close.finish()
+        close.drain()
+    else:
+        swap.wait()
+
+
+def attn_bwd(ga, x, gain, gmid, ag, qkv, ot, lse, w, neg, p, extra, out_kind, cid):
     rows, width = x.shape
-    p = p.reshape((2, 2, 2) + p.shape[1:])
     ld = w.shape[1] // 3
     g = 4
+    p = p.reshape((2, 2, 2) + p.shape[1:])
+    closing = len(extra) == 2
+    piece = p.shape[4:]
+    out = [
+        jax.ShapeDtypeStruct((rows, width), out_kind),
+        jax.ShapeDtypeStruct((8, 3 * ld // 8, width), BF),
+        jax.ShapeDtypeStruct((8, 3 * ld), F32),
+        jax.ShapeDtypeStruct((8, width), F32),
+        jax.ShapeDtypeStruct((4,) + piece, BF),
+    ]
+    if closing:
+        out += [
+            jax.ShapeDtypeStruct((8,) + piece, BF),
+            jax.ShapeDtypeStruct((8, 3 * ld // 8, width), BF),
+        ]
+        more = closer_scratch(*piece, 3 * ld // 8)
+    else:
+        out += [jax.ShapeDtypeStruct(extra[0].shape, BF)]
+        more = [pltpu.SemaphoreType.DMA((3,))]
     return pl.pallas_call(
-        attn_bwd_kernel,
+        functools.partial(attn_bwd_kernel, closing),
         name="attn_bwd",
-        out_shape=(
-            jax.ShapeDtypeStruct((rows, width), F32),
-            jax.ShapeDtypeStruct((3 * ld, width), F32),
-            jax.ShapeDtypeStruct((8, 3 * ld), F32),
-            jax.ShapeDtypeStruct((8, width), F32),
-            jax.ShapeDtypeStruct((8,) + p.shape[4:], BF),
-        ),
-        in_specs=vm(11),
-        out_specs=tuple(vm(5)),
+        out_shape=tuple(out),
+        in_specs=vm(11 + len(extra)),
+        out_specs=tuple(vm(len(out))),
         scratch_shapes=[
             pltpu.VMEM((g, rows, ld), BF),
             pltpu.VMEM((g, ld, 2 * rows), BF),
@@ -502,6 +524,7 @@
             pltpu.VMEM((rows, width), BF),
             pltpu.VMEM((rows, width), BF),
             pltpu.VMEM((rows, width), F32),
+            pltpu.VMEM((3 * ld, width), F32),
             pltpu.SemaphoreType.DMA((4,)),
             pltpu.SemaphoreType.DMA((4,)),
             pltpu.SemaphoreType.DMA((2,)),
@@ -509,11 +532,12 @@
             pltpu.SemaphoreType.DMA,
             pltpu.SemaphoreType.DMA,
         ]
-        + reducer_scratch(*p.shape[4:]),
+        + reducer_scratch(*piece)
+        + more,
         compiler_params=pltpu.CompilerParams(
             collective_id=cid, has_side_effects=True, vmem_limit_bytes=VMEM_LIMIT
         ),
-    )(ga, x, gain, gmid, ag, qkv, ot, lse, w, neg, p)
+    )(ga, x, gain, gmid, ag, qkv, ot, lse, w, neg, p, *extra)
 
 
 def gelu_both(x):
@@ -530,7 +554,7 @@
 
 
 def mlp_fwd_kernel(
-    att_ref, x_ref, w_ref, bu_ref, vec_ref, mid_ref, hid_ref, dg_ref, out_ref, in_s
+    att_ref, x_ref, w_ref, bu_ref, vec_ref, mid_ref, hid_ref, dg_ref, out_ref, in_s, out_s
 ):
     n_out = att_ref.shape[1] // 32
     n_up = (w_ref.shape[2] - n_out) // 2
@@ -551,7 +575,7 @@
         return carry
 
     lax.fori_loop(0, x_ref.shape[0] // step, norm, 0)
-    out_ref[...] = mid_ref[...] + vec_ref[1:2, :]
+    out_s[...] = mid_ref[...] + vec_ref[1:2, :]
 
     def part(q, carry):
         wu = w_ref[:, q, n_out : n_out + n_up, :].reshape(8 * n_up, quarter)
@@ -565,16 +589,17 @@
             act = act.astype(BF)
             hid_ref[q, at, :] = act
             dg_ref[q, at, :] = der.astype(BF)
-            out_ref[at, :] += nn(act, wd)
+            out_s[at, :] += nn(act, wd)
             return cc
 
         lax.fori_loop(0, x_ref.shape[0] // half, chunk, 0)
         return carry
 
     lax.fori_loop(0, 4, part, 0)
-
-
-def mlp_fwd(att, x, w, bu, vec):
+    out_ref[...] = out_s[...].astype(out_ref.dtype)
+
+
+def mlp_fwd(att, x, w, bu, vec, out_kind):
     rows, width = x.shape
     quarter = w.shape[3]
     return pl.pallas_call(
@@ -584,11 +609,11 @@
             jax.ShapeDtypeStruct((rows, width), F32),
             jax.ShapeDtypeStruct((4, rows, quarter), BF),
             jax.ShapeDtypeStruct((4, rows, quarter), BF),
-            jax.ShapeDtypeStruct((rows, width), F32),
+            jax.ShapeDtypeStruct((rows, width), out_kind),
         ),
         in_specs=vm(5),
         out_specs=tuple(vm(4)),
-        scratch_shapes=[pltpu.VMEM((rows, width), BF)],
+        scratch_shapes=[pltpu.VMEM((rows, width), BF), pltpu.VMEM((rows, width), F32)],
         compiler_params=pltpu.CompilerParams(vmem_limit_bytes=VMEM_LIMIT),
     )(att, x, w, bu, vec)
 
@@ -737,12 +762,37 @@
     )
 
 
+class Refs:
+    def __init__(self, names, refs):
+        assert len(names) == len(refs)
+        for name, ref in zip(names, refs):
+            setattr(self, name, ref)
+
+
+def begin(copies):
+    for one in copies:
+        one.start()
+
+
+def landed(copies):
+    for one in copies:
+        one.wait_recv()
+
+
+def sent(copies):
+    for one in copies:
+        one.wait_send()
+
+
+def add_low(a, b):
+    return (a.astype(F32) + b.astype(F32)).astype(BF)
+
+
 class Reducer:
-    def __init__(self, p_ref, e_ref, ra, rb1, rb2, rc, rd, s_sem, r_sem):
-        y, x, c, h, b = place()
-        self.at = (y, x, c, h, b)
-        self.bufs = (p_ref, e_ref, ra, rb1, rb2, rc, rd)
-        self.piece = c * 4 + y * 2 + x
+    def __init__(self, p_ref, rc, ra, rb1, rb2, s_sem, r_sem):
+        y, x, c, _, _ = place()
+        self.at = (y, x, c)
+        self.bufs = (p_ref, rc, ra, rb1, rb2)
         core = {"c": 1 - c}
         xp = {"k": 2 * y + 1 - x}
         yp = {"k": 2 * (1 - y) + x}
@@ -756,71 +806,42 @@
         self.b = [cp(ra.at[j, 1 - x, 0:2], rb1.at[j], xp) for j in range(2)]
         self.b += [cp(ra.at[1 - y, j, 2:4], rb2.at[j], yp) for j in range(2)]
         self.c = [cp(rb1.at[1 - y], rc.at[0:2], yp), cp(rb2.at[1 - x], rc.at[2:4], xp)]
-        self.d = [
-            cp(rc.at[2 * hh + bb], rd.at[i - 1], {"h": hh, "b": bb})
-            for i, hh, bb in depth_peers(h, b)
-        ]
-        self.e = [cp(e_ref.at[self.piece], e_ref.at[self.piece], dev) for _, dev in plane_peers(y, x, c)]
-
-    @staticmethod
-    def start(copies):
-        for one in copies:
-            one.start()
-
-    @staticmethod
-    def landed(copies):
-        for one in copies:
-            one.wait_recv()
 
     def stage_a(self):
-        self.start(self.a)
+        begin(self.a)
 
     def stage_b(self):
-        p_ref, e_ref, ra, rb1, rb2, rc, rd = self.bufs
+        p_ref, rc, ra, rb1, rb2 = self.bufs
         c = self.at[2]
-        self.landed(self.a)
+        landed(self.a)
 
         def add(i, carry):
             yy, xx = lax.div(i, 2), lax.rem(i, 2)
             for q in range(4):
-                ra[yy, xx, q] = (ra[yy, xx, q].astype(F32) + p_ref[c, yy, xx, q].astype(F32)).astype(BF)
+                ra[yy, xx, q] = add_low(ra[yy, xx, q], p_ref[c, yy, xx, q])
             return carry
 
         lax.fori_loop(0, 4, add, 0)
-        self.start(self.b)
+        begin(self.b)
 
     def stage_c(self):
-        p_ref, e_ref, ra, rb1, rb2, rc, rd = self.bufs
+        p_ref, rc, ra, rb1, rb2 = self.bufs
         y, x = self.at[0], self.at[1]
-        self.landed(self.b)
+        landed(self.b)
         for j in range(2):
             for q in range(2):
-                rb1[j, q] = (rb1[j, q].astype(F32) + ra[j, x, q].astype(F32)).astype(BF)
-                rb2[j, q] = (rb2[j, q].astype(F32) + ra[y, j, 2 + q].astype(F32)).astype(BF)
-        self.start(self.c)
-
-    def stage_d(self):
-        p_ref, e_ref, ra, rb1, rb2, rc, rd = self.bufs
+                rb1[j, q] = add_low(rb1[j, q], ra[j, x, q])
+                rb2[j, q] = add_low(rb2[j, q], ra[y, j, 2 + q])
+        begin(self.c)
+
+    def finish(self):
+        p_ref, rc, ra, rb1, rb2 = self.bufs
         y, x = self.at[0], self.at[1]
-        self.landed(self.c)
+        landed(self.c)
         for q in range(2):
-            rc[q] = (rc[q].astype(F32) + rb1[y, q].astype(F32)).astype(BF)
-            rc[2 + q] = (rc[2 + q].astype(F32) + rb2[x, q].astype(F32)).astype(BF)
-        self.start(self.d)
-
-    def stage_e(self):
-        p_ref, e_ref, ra, rb1, rb2, rc, rd = self.bufs
-        h, b = self.at[3], self.at[4]
-        self.landed(self.d)
-        tot = rc[2 * h + b].astype(F32) + rd[0].astype(F32) + rd[1].astype(F32) + rd[2].astype(F32)
-        e_ref[self.piece] = tot.astype(BF)
-        self.start(self.e)
-
-    def finish(self):
-        self.landed(self.e)
-        for group in (self.a, self.b, self.c, self.d, self.e):
-            for one in group:
-                one.wait_send()
+            rc[q] = add_low(rc[q], rb1[y, q])
+            rc[2 + q] = add_low(rc[2 + q], rb2[x, q])
+        sent(self.a + self.b + self.c)
 
 
 def reducer_scratch(rows, width):
@@ -828,19 +849,127 @@
         pltpu.VMEM((2, 2, 4, rows, width), BF),
         pltpu.VMEM((2, 2, rows, width), BF),
         pltpu.VMEM((2, 2, rows, width), BF),
-        pltpu.VMEM((4, rows, width), BF),
+        pltpu.SemaphoreType.DMA((7,)),
+        pltpu.SemaphoreType.DMA((7,)),
+    ]
+
+
+class Closer:
+    def __init__(self, rc, gw, e_ref, gwo, rd, rt, s_sem, r_sem):
+        y, x, c, h, b = place()
+        k = 2 * y + x
+        self.refs = (rc, gw, e_ref, gwo, rd, rt)
+        self.at = (k, c, h, b)
+        self.sems = (s_sem, r_sem)
+        self.piece = c * 4 + y * 2 + x
+        self.me = 2 * k + c
+        self.stays = c == h
+        self.d = [
+            remote(
+                rc.at[2 * hh + bb],
+                rd.at[i - 1],
+                s_sem.at[i - 1],
+                r_sem.at[i - 1],
+                {"h": hh, "b": bb},
+            )
+            for i, hh, bb in depth_peers(h, b)
+        ]
+        peers = plane_peers(y, x, c)
+        self.e = [
+            remote(e_ref.at[self.piece], e_ref.at[self.piece], s_sem.at[2 + i], r_sem.at[2 + i], dev)
+            for i, dev in peers
+        ]
+        self.f = [
+            remote(gwo.at[self.me], gwo.at[self.me], s_sem.at[9 + i], r_sem.at[9 + i], dev)
+            for i, dev in peers
+        ]
+
+    def part(self, p):
+        rc, gw, e_ref, gwo, rd, rt = self.refs
+        k, c, h, b = self.at
+        s_sem, r_sem = self.sems
+        slot = 2 * k + h
+        dev = {"k": p // 2, "c": p % 2, "h": c}
+        return remote(gw.at[p], rt.at[slot], s_sem.at[17 + p], r_sem.at[17 + slot], dev)
+
+    def home(self, p):
+        k, c, h, b = self.at
+        return (k == p // 2) & (c == p % 2) & self.stays
+
+    def stage_1(self):
+        rc, gw, e_ref, gwo, rd, rt = self.refs
+        h = self.at[2]
+        begin(self.d)
+        for p in range(8):
+
+            @pl.when(jnp.logical_not(self.home(p)))
+            def _():
+                self.part(p).start()
+
+            @pl.when(self.home(p))
+            def _():
+                rt[p // 2 * 2 + h] = gw[p]
+
+    def stage_2(self):
+        rc, gw, e_ref, gwo, rd, rt = self.refs
+        k, c, h, b = self.at
+        s_sem, r_sem = self.sems
+        landed(self.d)
+        tot = rc[2 * h + b].astype(F32) + rd[0].astype(F32) + rd[1].astype(F32) + rd[2].astype(F32)
+        e_ref[self.piece] = tot.astype(BF)
+        begin(self.e)
+        for j in range(8):
+
+            @pl.when(jnp.logical_not(self.stays & (k == j // 2) & (h == j % 2)))
+            def _():
+                one = remote(gw.at[0], rt.at[j], s_sem.at[17], r_sem.at[17 + j], {"c": 1 - c})
+                one.wait_recv()
+
+        tot = rt[0].astype(F32)
+        for j in range(1, 8):
+            tot = tot + rt[j].astype(F32)
+        gwo[self.me] = tot.astype(BF)
+        begin(self.f)
+
+    def finish(self):
+        landed(self.e)
+        landed(self.f)
+
+    def drain(self):
+        sent(self.d + self.e + self.f)
+        for p in range(8):
+
+            @pl.when(jnp.logical_not(self.home(p)))
+            def _():
+                self.part(p).wait_send()
+
+
+def closer_scratch(rows, width, parts):
+    return [
         pltpu.VMEM((3, rows, width), BF),
-        pltpu.SemaphoreType.DMA((17,)),
-        pltpu.SemaphoreType.DMA((17,)),
+        pltpu.VMEM((8, parts, width), BF),
+        pltpu.SemaphoreType.DMA((25,)),
+        pltpu.SemaphoreType.DMA((25,)),
     ]
 
 
-def tail_kernel(
-    gw_ref, small_ref, gt_ref, gwo_ref, tot_ref, gto_ref, gw_s, rt, sm_in, sz, s_sem, r_sem, own_sem
-):
-    y, x, c, h, b = place()
-    k = 2 * y + x
-    pieces = gwo_ref.shape[0]
+class Swap:
+    def __init__(self, src, dst, sems):
+        _, _, c, h, _ = place()
+        self.stays = c == h
+        self.out = remote(src, dst, sems.at[0], sems.at[1], {"c": 1 - c, "h": 1 - h})
+        self.own = pltpu.make_async_copy(src, dst, sems.at[2])
+
+    def start(self):
+        pl.when(jnp.logical_not(self.stays))(self.out.start)
+        pl.when(self.stays)(self.own.start)
+
+    def wait(self):
+        pl.when(jnp.logical_not(self.stays))(self.out.wait)
+        pl.when(self.stays)(self.own.wait)
+
+
+def all_near(y, x, c, h, b):
     devs = [dev for _, dev in plane_peers(y, x, c)]
     for dy in range(2):
         for dx in range(2):
@@ -848,135 +977,125 @@
                 yy = 1 - y if dy else y
                 xx = 1 - x if dx else x
                 devs.append({"k": 2 * yy + xx, "c": 1 - c if dc else c, "h": 1 - h})
-    devs += [{"h": h, "b": 1 - b}, {"h": 1 - h, "b": 1 - b}]
-    meet(devs)
-    gt_copy = remote(
-        gt_ref, gto_ref, s_sem.at[0], r_sem.at[0], {"c": 1 - c, "h": 1 - h}
-    )
-    gt_own = pltpu.make_async_copy(gt_ref, gto_ref, own_sem)
-    stays = c == h
-
-    small_copies = []
+    devs += [{"h": h, "b": 1 - b}, {"h": 1 - h, "b": 1 - b}, {"c": 1 - c, "b": 1 - b}]
+    return devs
+
+
+TAIL_NAMES = (
+    "rc", "gw", "gt", "e1", "gwo1", "small0", "small1", "gln0", "gln1", "gb0", "gb1", "gq", "gbq",
+    "wout", "bout", "wup", "bup", "wdown", "bdown", "gain", "shift", "gto", "e0", "gwo0", "sm",
+    "sm_in", "sz", "tot", "sm_s", "sm_r", "sw", "rd", "rt", "cs", "cr",
+)
+
+
+def tail_kernel(*refs):
+    r = Refs(TAIL_NAMES, refs)
+    y, x, c, h, b = place()
+    home = 2 * h + b
+    width = r.tot.shape[1]
+    ld = r.gq.shape[3]
+    meet(all_near(y, x, c, h, b)[:-1])
+    close = Closer(r.rc, r.gw, r.e0, r.gwo0, r.rd, r.rt, r.cs, r.cr)
+    swap = Swap(r.gt, r.gto, r.sw)
+    close.stage_1()
+    swap.start()
+    r.sm[...] = jnp.zeros(r.sm.shape, F32)
+    for l, (small, gln, gb) in enumerate(((r.small0, r.gln0, r.gb0), (r.small1, r.gln1, r.gb1))):
+        r.sm[10 * l : 10 * l + 8, :] = small[...]
+        r.sm[10 * l + 8 : 10 * l + 10, :] = gln[0:2, :]
+        r.sm[pl.ds(20 + 2 * (2 * c + b) + l, 1), 0 : 3 * ld] = gb[0:1, :]
+    plane = []
     for i, dev in plane_peers(y, x, c):
-        one = remote(small_ref, sm_in.at[i - 1], s_sem.at[i], r_sem.at[i], dev)
-        one.start()
-        small_copies.append(one)
-
-    def pack(l, carry):
-        for p in range(8):
-            rows = gw_s.shape[2]
-            gw_s[p, l] = gw_ref[l, p * rows : (p + 1) * rows, :].astype(BF)
-        return carry
-
-    lax.fori_loop(0, gw_ref.shape[0], pack, 0)
-
-    def gw_copy(p):
-        dev = {"k": p // 2, "c": p % 2, "h": c}
-        return remote(
-            gw_s.at[p], rt.at[2 * k + h], s_sem.at[8 + p], r_sem.at[8 + 2 * k + h], dev
-        )
-
-    def at_home(p):
-        return (k == p // 2) & (c == p % 2) & stays
-
-    for p in range(8):
-        @pl.when(jnp.logical_not(at_home(p)))
-        def _():
-            gw_copy(p).start()
-
-        @pl.when(at_home(p))
-        def _():
-            rt[p // 2 * 2 + h] = gw_s[p]
-
-    @pl.when(jnp.logical_not(stays))
-    def _():
-        gt_copy.start()
-
-    @pl.when(stays)
-    def _():
-        gt_own.start()
-
-    acc = small_ref[...]
-    for i, one in enumerate(small_copies):
+        plane.append(remote(r.sm, r.sm_in.at[i - 1], r.sm_s.at[i - 1], r.sm_r.at[i - 1], dev))
+    begin(plane)
+
+    def lay_big(l, e):
+        n_out = ld // 8
+        n_up = (e.shape[1] - n_out) // 2
+        r.wout[l] = e[:, :n_out, :].reshape(8 * n_out, width).astype(F32)
+        r.wup[l] = e[:, n_out : n_out + n_up, :].reshape(8 * n_up, width).astype(F32)
+        r.wdown[l] = e[:, n_out + n_up :, :].reshape(8 * n_up, width).astype(F32).T
+
+    def lay_qkv(l, gwo):
+        full = gwo[...].reshape(3 * ld, width).astype(F32)
+        for i in range(3):
+            r.gq[l, i] = full[i * ld : (i + 1) * ld].T
+
+    lay_big(1, r.e1)
+    lay_qkv(1, r.gwo1)
+    acc = r.sm[...]
+    for i, one in enumerate(plane):
         one.wait_recv()
-        acc = acc + sm_in[i]
-    sz[0] = acc
+        acc = acc + r.sm_in[i]
+    r.sz[0] = acc
     depth = []
     for i, hh, bb in depth_peers(h, b):
-        one = remote(sz.at[0], sz.at[i], s_sem.at[15 + i], r_sem.at[15 + i], {"h": hh, "b": bb})
-        one.start()
-        depth.append(one)
-
-    def gw_landed(j):
-        one = remote(gw_s.at[0], rt.at[j], s_sem.at[8], r_sem.at[8 + j], {"c": 1 - c})
-        one.wait_recv()
-
-    for j in range(8):
-        @pl.when(jnp.logical_not(stays & (k == j // 2) & (h == j % 2)))
-        def _():
-            gw_landed(j)
-
-    me = 2 * k + c
-    for l in range(gw_ref.shape[0]):
-        tot = rt[0, l].astype(F32)
-        for j in range(1, 8):
-            tot = tot + rt[j, l].astype(F32)
-        gwo_ref[me, l] = tot.astype(BF)
-    plane = []
-    for i, dev in plane_peers(y, x, c):
-        one = remote(gwo_ref.at[me], gwo_ref.at[me], s_sem.at[18 + i], r_sem.at[18 + i], dev)
-        one.start()
-        plane.append(one)
-    acc = sz[0]
-    for i, one in enumerate(depth):
-        one.wait_recv()
-        acc = acc + sz[i + 1]
-    tot_ref[...] = acc
-    for one in plane:
-        one.wait_recv()
-
-    @pl.when(jnp.logical_not(stays))
-    def _():
-        gt_copy.wait()
-
-    @pl.when(stays)
-    def _():
-        gt_own.wait()
-
-    for one in small_copies + depth + plane:
-        one.wait_send()
-    for p in range(8):
-        @pl.when(jnp.logical_not(at_home(p)))
-        def _():
-            gw_copy(p).wait_send()
-
-
-def tail(gw, small, gt, cid):
-    layers, rows3, width = gw.shape
-    n = rows3 // 8
+        depth.append(
+            remote(r.sz.at[0], r.sz.at[i], r.sm_s.at[6 + i], r.sm_r.at[6 + i], {"h": hh, "b": bb})
+        )
+    begin(depth)
+    close.stage_2()
+    landed(depth)
+    r.tot[...] = r.sz[0] + r.sz[1] + r.sz[2] + r.sz[3]
+    for l in range(2):
+        at = 10 * l
+        r.bdown[l : l + 1, :] = r.tot[at : at + 1, :]
+        r.bout[l : l + 1, :] = r.tot[at + 1 : at + 2, :]
+        r.gain[l, 1:2, :] = r.tot[at + 2 : at + 3, :]
+        r.shift[l, 1:2, :] = r.tot[at + 3 : at + 4, :]
+        r.gain[l, 0:1, :] = r.tot[at + 8 : at + 9, :]
+        r.shift[l, 0:1, :] = r.tot[at + 9 : at + 10, :]
+        r.bup[l : l + 1, :] = r.tot[pl.ds(at + 4 + home, 1), :]
+        row = r.tot[pl.ds(20 + 2 * home + l, 1), :]
+        r.gbq[l, 0:1, :] = row[:, :ld]
+        r.gbq[l, 1:2, :] = row[:, 2 * ld : 3 * ld]
+    close.finish()
+    lay_big(0, r.e0)
+    lay_qkv(0, r.gwo0)
+    swap.wait()
+    close.drain()
+    sent(plane + depth)
+
+
+def tail(rc, gw, gt, e1, gwo1, small, gln, gb, cid):
+    ld = gw.shape[0] * gw.shape[1] // 3
+    _, rows, width = rc.shape
+    sm = (32, width)
+    f32 = [
+        (2, 3, width, ld),
+        (2, 2, ld),
+        (2, ld, width),
+        (2, width),
+        (2, width, width),
+        (2, width),
+        (2, width, width),
+        (2, width),
+        (2, 2, width),
+        (2, 2, width),
+    ]
     return pl.pallas_call(
         tail_kernel,
         name="tail_sums",
-        out_shape=(
-            jax.ShapeDtypeStruct((8, layers, n, width), BF),
-            jax.ShapeDtypeStruct(small.shape, F32),
-            jax.ShapeDtypeStruct(gt.shape, BF),
-        ),
-        in_specs=vm(3),
-        out_specs=tuple(vm(3)),
+        out_shape=tuple(jax.ShapeDtypeStruct(s, F32) for s in f32)
+        + (jax.ShapeDtypeStruct(gt.shape, BF),),
+        in_specs=vm(11),
+        out_specs=tuple(vm(11)),
         scratch_shapes=[
-            pltpu.VMEM((8, layers, n, width), BF),
-            pltpu.VMEM((8, layers, n, width), BF),
-            pltpu.VMEM((7,) + small.shape, F32),
-            pltpu.VMEM((4,) + small.shape, F32),
-            pltpu.SemaphoreType.DMA((26,)),
-            pltpu.SemaphoreType.DMA((26,)),
-            pltpu.SemaphoreType.DMA,
-        ],
+            pltpu.VMEM(e1.shape, BF),
+            pltpu.VMEM(gwo1.shape, BF),
+            pltpu.VMEM(sm, F32),
+            pltpu.VMEM((7,) + sm, F32),
+            pltpu.VMEM((4,) + sm, F32),
+            pltpu.VMEM(sm, F32),
+            pltpu.SemaphoreType.DMA((10,)),
+            pltpu.SemaphoreType.DMA((10,)),
+            pltpu.SemaphoreType.DMA((3,)),
+        ]
+        + closer_scratch(rows, width, gw.shape[1]),
         compiler_params=pltpu.CompilerParams(
             collective_id=cid, has_side_effects=True, vmem_limit_bytes=VMEM_LIMIT
         ),
-    )(gw, small, gt)
+    )(rc, gw, gt, e1, gwo1, *small, *gln, *gb)
 
 
 def shards(
@@ -1054,61 +1173,41 @@
         w, bu = weights[l]
         bu = jnp.broadcast_to(bu.astype(F32)[:, None], (4, 8, quarter))
         vec = vectors(l)
-        mid, hid, dg, nxt = mlp_fwd(att, stream, w, bu, vec)
+        mid, hid, dg, nxt = mlp_fwd(att, stream, w, bu, vec, BF if l == layers - 1 else F32)
         stored.append((stream, ag, qkv, ot, lse, att, mid, hid, dg, w, vec))
         stream = nxt
-    output = swap(stream.astype(BF))
-
     grad = g_in.astype(F32)
-    keys = ("wqkv", "bqv", "small", "big")
-    outs = {k: [None] * layers for k in keys}
+    small, gln, gb = [None] * layers, [None] * layers, [None] * layers
+    output = rc = gw = None
     for l in reversed(range(layers)):
         stream_in, ag, qkv, ot, lse, att, mid, hid, dg, w, vec = stored[l]
-        p, g_mid, ga, small_l = mlp_bwd(grad, mid, att, hid, dg, w, vec)
-        grad, gwt, gb, gln, big = attn_bwd(
-            ga, stream_in, gains[l, 0][None], g_mid, ag, qkv, ot, lse, wq[l], neg, p, 2 * l + 1
+        p, g_mid, ga, small[l] = mlp_bwd(grad, mid, att, hid, dg, w, vec)
+        top = l == layers - 1
+        extra = (stream,) if top else (rc, gw)
+        grad, gw, gb[l], gln[l], rc, *rest = attn_bwd(
+            ga,
+            stream_in,
+            gains[l, 0][None],
+            g_mid,
+            ag,
+            qkv,
+            ot,
+            lse,
+            wq[l],
+            neg,
+            p,
+            extra,
+            F32 if l else BF,
+            2 * l + 1,
         )
-        outs["wqkv"][l] = gwt
-        outs["bqv"][l] = gb[0:1]
-        outs["small"][l] = jnp.concatenate([small_l, gln[:2]])
-        outs["big"][l] = big
-    group_at = lax.axis_index("c") * 2 + lax.axis_index("b")
-    home = lax.axis_index("h") * 2 + lax.axis_index("b")
-    gbq = jnp.pad(jnp.concatenate(outs["bqv"]), ((0, 0), (0, width - 3 * ld)))
-    gbq = jnp.where(jnp.arange(4)[:, None, None] == group_at, gbq[None], 0.0)
-    flat = jnp.concatenate(outs["small"] + [gbq.reshape(4 * layers, width)])
-    n_small = flat.shape[0]
-    flat = jnp.pad(flat, ((0, -n_small % 8), (0, 0)))
-    gq, flat, g_tok = tail(jnp.stack(outs["wqkv"]), flat, grad.astype(BF), 2 * layers)
-    big = jnp.stack(outs["big"])
+        if top:
+            output = rest[0]
+        else:
+            e1, gwo1 = rest
+    *grads, g_tok = tail(rc, gw, grad, e1, gwo1, small, gln, gb, 2 * layers)
     if n_outer > 1:
-        gq, flat, big = lax.psum((gq, flat, big), "o")
-    gq = gq.transpose(1, 0, 2, 3).reshape(layers, 3, ld, width).transpose(0, 1, 3, 2).astype(F32)
-    small = flat[: 10 * layers].reshape(layers, 10, width)
-    gbq = flat[10 * layers : n_small].reshape(4, layers, width)
-    gbq = lax.dynamic_index_in_dim(gbq, home, 0, keepdims=False)[:, : 3 * ld]
-    gbq = gbq.reshape(layers, 3, ld)[:, ::2]
-    n_out = ld // 8
-    n_up = width // 8
-    big = big.astype(F32)
-    g_wout = big[:, :, :n_out].reshape(layers, ld, width)
-    g_wup = big[:, :, n_out : n_out + n_up].reshape(layers, width, quarter)
-    g_wdown = big[:, :, n_out + n_up :].reshape(layers, width, quarter).transpose(0, 2, 1)
-    g_bup = lax.dynamic_index_in_dim(small[:, 4:8], home, 1, keepdims=False)
-    return (
-        output,
-        g_tok,
-        gq,
-        gbq,
-        g_wout,
-        small[:, 1],
-        g_wup,
-        g_bup,
-        g_wdown,
-        small[:, 0],
-        jnp.stack([small[:, 8], small[:, 2]], axis=1),
-        jnp.stack([small[:, 9], small[:, 3]], axis=1),
-    )
+        grads = lax.psum(tuple(grads), "o")
+    return (output, g_tok, *grads)
 
 
 def solution(mesh):

time: 467 us -> 433 us (0.927)
  Pallas kernels: 359 us -> 344 us
  other arithmetic: 14.5 us -> 3.87 us
  starting transfers between devices: 14.7 us -> 9.34 us
    pallas_call x3, Pallas kernels: 187 us -> 171 us  [the longest x2 119 us: attn_bwd(): pl.pallas_call(functools.partial(attn_bwd_kernel, closing), name='attn_bw...]
    convert_element_type x4 -> x0, other arithmetic: 6.25 us -> none  [the longest x1 3.11 us: shards(): big = big.astype(F32)]
    ppermute x6 -> x5, starting transfers between devices: 14.6 us -> 9.26 us  [swap(): return lax.ppermute(v, AXES, perm)]
    slice x10 -> x0, local copies, waits for them, and re-layouts: 5.24 us -> none  [the longest x2 1.53 us: shards(): outs['bqv'][l] = gb[0:1]]
    unnamed x41 -> x53, local copies, waits for them, and re-layouts: 6.41 us -> 11.6 us
  transfers between devices with their start and end apart: 8 -> 7, of which waited for: 0 -> 0; matrix products, arithmetic and copies ran while one was open for 4% -> 2% of each run, Pallas kernels for 26% -> 28%
where the time goes in v3:
time: 433 us; the launch traced here: 431 us
  Pallas kernels  344 us (79%)
  blocking collectives  35.9 us (8%)
  local copies, waits for them, and re-layouts  23.8 us (5%)
  between operations  14.4 us (3%)
  starting transfers between devices  9.34 us (2%)
    pallas_call x2, Pallas kernels, attn_bwd(): pl.pallas_call(functools.partial(attn_bwd_kernel, closing), name='attn_bw...  119 us
    pallas_call x2, Pallas kernels, attn_fwd(): pl.pallas_call(attn_fwd_kernel, name='attn_fwd', out_shape=(jax.ShapeDtyp...  105 us
    pallas_call x1, Pallas kernels, tail(): pl.pallas_call(tail_kernel, name='tail_sums', out_shape=tuple((jax.ShapeD...  52.5 us
    all_gather x2, blocking collectives, gather_weights(): g1 = lax.all_gather(own, ('h', 'b'), axis=0, tiled=False)  35.9 us
    pallas_call x2, Pallas kernels, mlp_fwd(): pl.pallas_call(mlp_fwd_kernel, name='mlp_fwd', out_shape=(jax.ShapeDtypeS...  34.5 us
    pallas_call x2, Pallas kernels, mlp_bwd(): pl.pallas_call(mlp_bwd_kernel, name='mlp_bwd', out_shape=(jax.ShapeDtypeS...  32.3 us
    unnamed x53, local copies, waits for them, and re-layouts  11.6 us
    ppermute x5, starting transfers between devices, swap(): return lax.ppermute(v, AXES, perm)  9.26 us
  transfers between devices with their start and end apart: 7, of which 0 were waited for; matrix products, arithmetic and copies ran while one was open for 2% of the time, Pallas kernels for 28%

profile of v3, /device:TPU:0, one launch (start us, length us, event | category | flops | bytes accessed | tf_op | source)
XLA Modules:
  0.0 431.0 jit_solution(6164417219801726385)
XLA Ops:
  8.0 1.0 fusion.6
  9.0 1.3 fusion.4
  12.1 19.6 %all-gather = bf16[640,512]{1,0:T(8,128)(2,1)S(1)} all-gather(bf16[160,512]{1,0:T(8,128)(2,1)S(1)} %pad_maximum_fusion), channel_id=2, replica_groups=mesh['o'=1,'k'=4,'c'=2,'h'=2,'b'=2] {'h','b'}, dimensions={0}, use_global_device_ids=true | all-gather | bytes 819200 | tf_op jit(solution)/shard_map/all_gather | solution.py:1141
  31.7 0.9 slice.133
  32.7 16.3 %all-gather.2 = bf16[640,512]{1,0:T(8,128)(2,1)S(1)} all-gather(bf16[160,512]{1,0:T(8,128)(2,1)S(1)} %pad_maximum_fusion.1), channel_id=4, replica_groups=mesh['o'=1,'k'=4,'c'=2,'h'=2,'b'=2] {'h','b'}, dimensions={0}, use_global_device_ids=true | all-gather | bytes 819200 | tf_op jit(solution)/shard_map/all_gather | solution.py:1141
  49.0 0.9 slice.142
  51.4 5.4 %collective-permute-start.1 = (bf16[512,512]{1,0:T(8,128)(2,1)}, bf16[512,512]{1,0:T(8,128)(2,1)}, u32[]{:S(2)}, u32[]{:S(2)}) collective-permute-start(bf16[512,512]{1,0:T(8,128)(2,1)} %param.13), channel_id=1, source_target_pairs={{0,0},{1,1},{2,4},{3,5},{4,2},{5,3},{6,6},{7,7},{8,8},{9,9},{10,12... | collective-permute-start | bytes 1572872 | tf_op jit(solution)/shard_map/ppermute | solution.py:1130
  56.8 1.7 collective-permute-start
  63.1 2.1 convert_element_type.53.x_ref.refs_1_
  65.2 1.1 convert_element_type.52.g_ref
  66.3 1.0 slice_bitcast_fusion
  67.9 69.4 %attn_fwd.2 = (bf16[4,512,512]{2,1,0:T(8,128)(2,1)}, bf16[4,512,384]{2,1,0:T(8,128)(2,1)}, f32[4,128,512]{2,1,0:T(8,128)}, f32[4,8,1024]{2,1,0:T(8,128)}, bf16[512,512]{1,0:T(8,128)(2,1)}) custom-call(f32[512,512]{1,0:T(8,128)} %convert_element_type.53.x_ref.refs_1_, f32[1,512]{1,0:T(1,128)} %get-tuple-element.129.gain_ref.refs_2_, ...), custom_call_target="tpu_custom_call" | custom-call | tf_op jit(solution)/shard_map/attn_fwd/pallas_call | solution.py:225
  137.9 17.4 %mlp_fwd.2 = (f32[512,512]{1,0:T(8,128)}, bf16[4,512,512]{2,1,0:T(8,128)(2,1)}, bf16[4,512,512]{2,1,0:T(8,128)(2,1)}, f32[512,512]{1,0:T(8,128)}) custom-call(bf16[512,512]{1,0:T(8,128)(2,1)} %get-tuple-element.62.att_ref, f32[512,512]{1,0:T(8,128)} %convert_element_type.53.x_ref.refs_1_, bf16[8,4,144,512]{3,2,1,0:T(8,128)(2,1)} %bitcast.57, ...), custom_call_target="tpu_custom_call" | custom-call | tf_op jit(solution)/shard_map/mlp_fwd/pallas_call | solution.py:605
  155.3 36.0 %attn_fwd.3 = (bf16[4,512,512]{2,1,0:T(8,128)(2,1)}, bf16[4,512,384]{2,1,0:T(8,128)(2,1)}, f32[4,128,512]{2,1,0:T(8,128)}, f32[4,8,1024]{2,1,0:T(8,128)}, bf16[512,512]{1,0:T(8,128)(2,1)}) custom-call(f32[512,512]{1,0:T(8,128)} %get-tuple-element.63.x_ref.refs_1_, f32[1,512]{1,0:T(1,128)} %get-tuple-element.127.gain_ref.refs_2_, ...), custom_call_target="tpu_custom_call" | custom-call | tf_op jit(solution)/shard_map/attn_fwd/pallas_call | solution.py:225
  192.0 17.1 %mlp_fwd.3 = (f32[512,512]{1,0:T(8,128)}, bf16[4,512,512]{2,1,0:T(8,128)(2,1)}, bf16[4,512,512]{2,1,0:T(8,128)(2,1)}, bf16[512,512]{1,0:T(8,128)(2,1)}) custom-call(bf16[512,512]{1,0:T(8,128)(2,1)} %get-tuple-element.64.att_ref, f32[512,512]{1,0:T(8,128)} %get-tuple-element.63.x_ref.refs_1_, bf16[8,4,144,512]{3,2,1,0:T(8,128)(2,1)} %bitcast.59, ...), custom_call_target="tpu_custom_call" | custom-call | tf_op jit(solution)/shard_map/mlp_fwd/pallas_call | solution.py:605
  209.1 16.2 %mlp_bwd.2 = (bf16[8,4,144,512]{3,2,1,0:T(8,128)(2,1)}, f32[512,512]{1,0:T(8,128)}, bf16[512,512]{1,0:T(8,128)(2,1)}, f32[8,512]{1,0:T(8,128)}) custom-call(f32[512,512]{1,0:T(8,128)} %convert_element_type.52.g_ref, f32[512,512]{1,0:T(8,128)} %get-tuple-element.65.mid_ref, bf16[512,512]{1,0:T(8,128)(2,1)} %get-tuple-element.64.att_ref, ...), custom_call_target="tpu_custom_call" | custom-call | tf_op jit(solution)/shard_map/mlp_bwd/pallas_call | solution.py:709
  225.3 53.4 %attn_bwd.2 = (f32[512,512]{1,0:T(8,128)}, bf16[8,48,512]{2,1,0:T(8,128)(2,1)}, f32[8,384]{1,0:T(8,128)}, f32[8,512]{1,0:T(8,128)}, bf16[4,144,512]{2,1,0:T(8,128)(2,1)}, /*index=5*/bf16[512,512]{1,0:T(8,128)(2,1)}) custom-call(bf16[512,512]{1,0:T(8,128)(2,1)} %get-tuple-element.68.refs_0_, f32[512,512]{1,0:T(8,128)} %get-tuple-element.63.x_ref.refs_1_, ...), custom_call_target="tpu_custom_call" | custom-call | tf_op jit(solution)/shard_map/attn_bwd/pallas_call | solution.py:505
  278.8 16.2 %mlp_bwd.3 = (bf16[8,4,144,512]{3,2,1,0:T(8,128)(2,1)}, f32[512,512]{1,0:T(8,128)}, bf16[512,512]{1,0:T(8,128)(2,1)}, f32[8,512]{1,0:T(8,128)}) custom-call(f32[512,512]{1,0:T(8,128)} %get-tuple-element.77.g_ref, f32[512,512]{1,0:T(8,128)} %get-tuple-element.78.mid_ref, bf16[512,512]{1,0:T(8,128)(2,1)} %get-tuple-element.62.att_ref, ...), custom_call_target="tpu_custom_call" | custom-call | tf_op jit(solution)/shard_map/mlp_bwd/pallas_call | solution.py:709
  294.9 65.3 %attn_bwd.3 = (bf16[512,512]{1,0:T(8,128)(2,1)}, bf16[8,48,512]{2,1,0:T(8,128)(2,1)}, f32[8,384]{1,0:T(8,128)}, f32[8,512]{1,0:T(8,128)}, bf16[4,144,512]{2,1,0:...) custom-call(bf16[512,512]{1,0:T(8,128)(2,1)} %get-tuple-element.81.refs_0_, ...), custom_call_target="tpu_custom_call" | custom-call | tf_op jit(solution)/shard_map/attn_bwd/pallas_call | solution.py:505
  360.3 52.5 %tail_sums.1 = (f32[2,3,512,128]{3,2,1,0:T(8,128)}, f32[2,2,128]{2,1,0:T(2,128)}, f32[2,128,512]{2,1,0:T(8,128)}, f32[2,512]{1,0:T(2,128)}, f32[2,512,512]{2,1,0...) custom-call(bf16[4,144,512]{2,1,0:T(8,128)(2,1)} %get-tuple-element., ...), custom_call_target="tpu_custom_call" | custom-call | tf_op jit(solution)/shard_map/tail_sums/pallas_call | solution.py:1076
  413.6 1.9 copy.49
  415.6 1.1 copy.50
  418.7 1.3 copy.54
  421.1 1.3 copy.56
  (91 shorter events, 16.1 us)
Async XLA Ops:
  7.2 3.1 copy-start.3
  7.2 130.1 %all-gather.7.cloned.1.call-start = ((), (), s32[]{:S(2)}) async-start(), calls=%async_computation | async-start | bytes 5308416 | tf_op jit(solution)/shard_map/all_gather | solution.py:1142
  32.6 17.3 %copy-start.18 = (s32[1,4]{1,0:T(1,128)S(1)}, s32[1,4]{1,0:T(1,128)}, u32[]{:S(2)}) copy-start(s32[1,4]{1,0:T(1,128)} %param.15) | copy-start | bytes 52
  32.6 18.2 %copy-start.17 = (bf16[2,2,128]{2,1,0:T(2,128)(2,1)S(1)}, bf16[2,2,128]{2,1,0:T(2,128)(2,1)}, u32[]{:S(2)}) copy-start(bf16[2,2,128]{2,1,0:T(2,128)(2,1)} %param.17) | copy-start | bytes 3076
  32.6 25.9 %copy-start.4 = (bf16[2,3,512,128]{3,2,1,0:T(8,128)(2,1)S(1)}, bf16[2,3,512,128]{3,2,1,0:T(8,128)(2,1)}, u32[]{:S(2)}) copy-start(bf16[2,3,512,128]{3,2,1,0:T(8,128)(2,1)} %param.16) | copy-start | bytes 2359300
  32.6 158.8 %all-gather.9.cloned.1.call-start = ((), (), s32[]{:S(2)}) async-start(), calls=%async_computation.1 | async-start | bytes 5308416 | tf_op jit(solution)/shard_map/all_gather | solution.py:1142
  49.9 10.0 %copy-start.11 = (bf16[2,2,512]{2,1,0:T(2,128)(2,1)S(1)}, bf16[2,2,512]{2,1,0:T(2,128)(2,1)}, u32[]{:S(2)}) copy-start(bf16[2,2,512]{2,1,0:T(2,128)(2,1)} %param.24) | copy-start | bytes 12292
  49.9 10.0 %copy-start.12 = (bf16[2,2,512]{2,1,0:T(2,128)(2,1)S(1)}, bf16[2,2,512]{2,1,0:T(2,128)(2,1)}, u32[]{:S(2)}) copy-start(bf16[2,2,512]{2,1,0:T(2,128)(2,1)} %param.25) | copy-start | bytes 12292
  49.9 11.3 %copy-start.9 = (bf16[2,512]{1,0:T(2,128)(2,1)S(1)}, bf16[2,512]{1,0:T(2,128)(2,1)}, u32[]{:S(2)}) copy-start(bf16[2,512]{1,0:T(2,128)(2,1)} %param.23) | copy-start | bytes 6148
  49.9 11.3 %copy-start.10 = (bf16[2,512]{1,0:T(2,128)(2,1)S(1)}, bf16[2,512]{1,0:T(2,128)(2,1)}, u32[]{:S(2)}) copy-start(bf16[2,512]{1,0:T(2,128)(2,1)} %param.19) | copy-start | bytes 6148
  49.9 12.5 %collective-permute-start.4 = (s32[1,4]{1,0:T(1,128)S(1)}, s32[1,4]{1,0:T(1,128)S(1)}, u32[]{:S(2)}, u32[]{:S(2)}) collective-permute-start(s32[1,4]{1,0:T(1,128)S(1)} %copy-done.18), channel_id=1, source_target_pairs={{0,0},{1,1},{2,4},{3,5},{4,2},{5,3},{6,6},{7,7},{8,8},{9,9},{10,12... | collective-permute-start | bytes 56 | tf_op jit(solution)/shard_map/ppermute | solution.py:1130
  50.7 11.8 %collective-permute-start.3 = (bf16[2,2,128]{2,1,0:T(2,128)(2,1)S(1)}, bf16[2,2,128]{2,1,0:T(2,128)(2,1)S(1)}, u32[]{:S(2)}, u32[]{:S(2)}) collective-permute-start(bf16[2,2,128]{2,1,0:T(2,128)(2,1)S(1)} %copy-done.17), channel_id=1, source_target_pairs={{0,0},{1,1},{2,4},{3,5},{4,2},{5,3},{6,6},{7,7},{8,8},{9,9},{10,12... | collective-permute-start | bytes 3080 | tf_op jit(solution)/shard_map/ppermute | solution.py:1130
  51.4 11.7 %collective-permute-start.1 = (bf16[512,512]{1,0:T(8,128)(2,1)}, bf16[512,512]{1,0:T(8,128)(2,1)}, u32[]{:S(2)}, u32[]{:S(2)}) collective-permute-start(bf16[512,512]{1,0:T(8,128)(2,1)} %param.13), channel_id=1, source_target_pairs={{0,0},{1,1},{2,4},{3,5},{4,2},{5,3},{6,6},{7,7},{8,8},{9,9},{10,12... | collective-permute-start | bytes 1572872 | tf_op jit(solution)/shard_map/ppermute | solution.py:1130
  56.8 8.4 %collective-permute-start = (bf16[512,512]{1,0:T(8,128)(2,1)}, bf16[512,512]{1,0:T(8,128)(2,1)S(1)}, u32[]{:S(2)}, u32[]{:S(2)}) collective-permute-start(bf16[512,512]{1,0:T(8,128)(2,1)} %param.14), channel_id=1, source_target_pairs={{0,0},{1,1},{2,4},{3,5},{4,2},{5,3},{6,6},{7,7},{8,8},{9,9},{10,12... | collective-permute-start | bytes 1572872 | tf_op jit(solution)/shard_map/ppermute | solution.py:1130
  59.1 7.2 %collective-permute-start.2 = (bf16[2,512,384]{2,1,0:T(8,128)(2,1)S(1)}, bf16[2,512,384]{2,1,0:T(8,128)(2,1)S(1)}, u32[]{:S(2)}, u32[]{:S(2)}) collective-permute-start(bf16[2,512,384]{2,1,0:T(8,128)(2,1)S(1)} %copy.29), channel_id=1, source_target_pairs={{0,0},{1,1},{2,4},{3,5},{4,2},{5,3},{6,6},{7,7},{8,8},{9,9},{10,12... | collective-permute-start | bytes 2359304 | tf_op jit(solution)/shard_map/ppermute | solution.py:1130
  360.3 52.6 %copy-start.5 = (bf16[512,512]{1,0:T(8,128)(2,1)S(1)}, bf16[512,512]{1,0:T(8,128)(2,1)}, u32[]{:S(2)}) copy-start(bf16[512,512]{1,0:T(8,128)(2,1)} %get-tuple-element.158) | copy-start | bytes 1572868
  412.8 2.7 copy-start.2
  413.6 3.1 copy-start.16
  413.6 3.7 copy-start.6
  415.6 2.5 copy-start.15
  415.6 3.1 copy-start.1
  418.7 2.4 copy-start
  421.1 1.9 copy-start.8
  421.1 2.5 copy-start.7
  (2 other events, 2.7 us)
Sparse Core Ops, SparseCore 0:
  32.7 39.1 all-gather.6
  73.8 38.9 all-gather.8

commit v4 on v3

--- a/solution.py
+++ b/solution.py
@@ -36,13 +36,6 @@
     return cen * rstd, rstd
 
 
-def group_barrier(c, b):
-    bar = pltpu.get_barrier_semaphore()
-    for cc, bb in ((c, 1 - b), (1 - c, b), (1 - c, 1 - b)):
-        pl.semaphore_signal(bar, inc=1, device_id={"c": cc, "b": bb}, device_id_type=MESH)
-    pl.semaphore_wait(bar, 3)
-
-
 def pad_heads_lanes(t):
     row = lax.broadcasted_iota(jnp.int32, t.shape, 0)
     low = jnp.where(row < HEAD_DIM, t, 0.0)
@@ -64,83 +57,218 @@
     return key <= qry
 
 
-def attn_fwd_kernel(
-    x_ref,
-    gain_ref,
-    shift_ref,
-    w_ref,
-    bias_ref,
-    neg_ref,
-    ag_ref,
-    qkv_ref,
-    ot_ref,
-    lse_ref,
-    att_ref,
-    qt_s,
-    vt_s,
-    ob_s,
-    acc_s,
-    ag_send,
-    ag_recv,
-    a2a_send,
-    a2a_recv,
-):
-    c = lax.axis_index("c")
-    b = lax.axis_index("b")
-    me = 2 * c + b
-    core_peer = 2 * (1 - c) + b
-    z_peer = 2 * c + 1 - b
-    far_peer = 2 * (1 - c) + 1 - b
-    rows = x_ref.shape[0]
-    width = x_ref.shape[1]
-    group = ag_ref.shape[0]
-    ld = w_ref.shape[1] // 3
-    step = 64
-
-    def norm(it, carry):
-        at = pl.ds(pl.multiple_of(it * step, step), step)
-        n, _ = ln_parts(x_ref[at, :].astype(F32))
-        ag_ref[me, at, :] = (n * gain_ref[...] + shift_ref[...]).astype(BF)
-        return carry
-
-    lax.fori_loop(0, rows // step, norm, 0)
-    group_barrier(c, b)
-
-    def send(src_slot, dev, slot):
-        return pltpu.make_async_remote_copy(
-            src_ref=ag_ref.at[src_slot],
-            dst_ref=ag_ref.at[src_slot],
-            send_sem=ag_send.at[slot],
-            recv_sem=ag_recv.at[slot],
-            device_id=dev,
-            device_id_type=MESH,
-        )
-
-    to_z = send(me, {"c": c, "b": 1 - b}, 0)
-    to_core = send(me, {"c": 1 - c, "b": b}, 1)
-    fwd = send(z_peer, {"c": 1 - c, "b": b}, 2)
-    to_z.start()
-    to_core.start()
-
-    def project(slot):
-        r = nn(ag_ref[slot], w_ref[...]) + bias_ref[...]
-        qkv_ref[slot] = r.astype(BF)
-        qt_s[slot] = pad_heads_lanes(r[:, :ld].T).astype(BF)
-        vt_s[slot] = r[:, 2 * ld :].T.astype(BF)
-
-    project(me)
-    to_core.wait_recv()
-    project(core_peer)
-    to_z.wait_recv()
-    fwd.start()
-    project(z_peer)
-    fwd.wait_recv()
-    project(far_peer)
-
-    neg = neg_ref[0:1, 0:1]
-
-    def block(i, j, m, l, diag):
-        s = nn(qkv_ref[j, :, ld : 2 * ld], qt_s[i])
+def meet(devices):
+    bar = pltpu.get_barrier_semaphore()
+    for dev in devices:
+        pl.semaphore_signal(bar, inc=1, device_id=dev, device_id_type=MESH)
+    pl.semaphore_wait(bar, len(devices))
+
+
+def remote(src, dst, send, recv, dev):
+    return pltpu.make_async_remote_copy(
+        src_ref=src, dst_ref=dst, send_sem=send, recv_sem=recv, device_id=dev, device_id_type=MESH
+    )
+
+
+def place():
+    k = lax.axis_index("k")
+    return lax.div(k, 2), lax.rem(k, 2), lax.axis_index("c"), lax.axis_index("h"), lax.axis_index("b")
+
+
+def plane_peers(y, x, c):
+    found = []
+    for dy in range(2):
+        for dx in range(2):
+            for dc in range(2):
+                if dy + dx + dc:
+                    yy = 1 - y if dy else y
+                    xx = 1 - x if dx else x
+                    cc = 1 - c if dc else c
+                    found.append((dy * 4 + dx * 2 + dc, {"k": 2 * yy + xx, "c": cc}))
+    return found
+
+
+def depth_peers(h, b):
+    return [(1, h, 1 - b), (2, 1 - h, b), (3, 1 - h, 1 - b)]
+
+
+class Refs:
+    def __init__(self, names, refs):
+        assert len(names) == len(refs)
+        for name, ref in zip(names, refs):
+            setattr(self, name, ref)
+
+
+def begin(copies):
+    for one in copies:
+        one.start()
+
+
+def landed(copies):
+    for one in copies:
+        one.wait_recv()
+
+
+def sent(copies):
+    for one in copies:
+        one.wait_send()
+
+
+def row_of(ref, *at):
+    full = ref[...].astype(F32)
+    for i in at[:-1]:
+        full = full[i]
+    return full[at[-1] : at[-1] + 1]
+
+
+class Swap:
+    def __init__(self, src, dst, sems):
+        _, _, c, h, _ = place()
+        self.stays = c == h
+        self.out = remote(src, dst, sems.at[0], sems.at[1], {"c": 1 - c, "h": 1 - h})
+        self.own = pltpu.make_async_copy(src, dst, sems.at[2])
+
+    def start(self):
+        pl.when(jnp.logical_not(self.stays))(self.out.start)
+        pl.when(self.stays)(self.own.start)
+
+    def wait(self):
+        pl.when(jnp.logical_not(self.stays))(self.out.wait)
+        pl.when(self.stays)(self.own.wait)
+
+
+class DepthGather:
+    def __init__(self, l, weights, put, s_sem, r_sem):
+        y, x, c, h, b = place()
+        piece = c * 4 + 2 * y + x
+        mine = put(2 * h + b)
+        self.copies = []
+        for r, hh, bb in depth_peers(h, b):
+            low = 0
+            for j, ref in enumerate(weights):
+                n = ref.shape[2]
+                i = 3 * (r - 1) + j
+                self.copies.append(
+                    remote(
+                        ref.at[l, piece],
+                        mine.at[low : low + n],
+                        s_sem.at[i],
+                        r_sem.at[i],
+                        {"h": hh, "b": bb},
+                    )
+                )
+                low += n
+
+
+class PlaneGather:
+    def __init__(self, l, weights, full, eighth, own_sem, s_sem, r_sem):
+        y, x, c, h, b = place()
+        me = c * 4 + 2 * y + x
+        px = c * 4 + 2 * y + 1 - x
+        py = c * 4 + 2 * (1 - y) + x
+        xp = {"k": 2 * y + 1 - x}
+        yp = {"k": 2 * (1 - y) + x}
+        core = {"c": 1 - c}
+        t = 2 * h + b
+        q1, q2, q3 = [2 * hh + bb for _, hh, bb in depth_peers(h, b)]
+        rows = full.shape[2]
+        cut = (rows // 2 + 15) // 16 * 16
+        n = iter(range(32))
+
+        def cp(src, dst, dev):
+            i = next(n)
+            return remote(src, dst, s_sem.at[i], r_sem.at[i], dev)
+
+        first = [(q1, slice(0, rows)), (q3, slice(0, cut))]
+        second = [(q2, slice(0, rows)), (q3, slice(cut, rows))]
+        self.a = [cp(eighth(q).at[s], full.at[me, q, s], xp) for q, s in first]
+        self.a += [cp(eighth(q).at[s], full.at[me, q, s], yp) for q, s in second]
+        self.b = [cp(full.at[p, q, s], full.at[p, q, s], yp) for p in (me, px) for q, s in first]
+        self.b += [cp(full.at[p, q, s], full.at[p, q, s], xp) for p in (me, py) for q, s in second]
+        four = pl.ds(4 * c, 4)
+        self.c = [cp(full.at[four, q], full.at[four, q], core) for q in (q1, q2, q3)]
+        self.own = []
+        low = 0
+        for j, ref in enumerate(weights):
+            m = ref.shape[2]
+            self.own.append(
+                pltpu.make_async_copy(ref.at[l], full.at[:, t, low : low + m], own_sem.at[j])
+            )
+            low += m
+
+    def drain(self):
+        sent(self.a + self.b + self.c)
+        for one in self.own:
+            one.wait()
+
+
+class Attention:
+    def __init__(self, r, parts):
+        self.r = r
+        self.parts = parts
+        _, _, c, _, b = place()
+        self.c, self.b = c, b
+        self.me = 2 * c + b
+        self.core_peer = 2 * (1 - c) + b
+        self.z_peer = 2 * c + 1 - b
+        self.far_peer = 2 * (1 - c) + 1 - b
+        rows = r.ag.shape[1] // parts
+        core = {"c": 1 - c}
+        deep = {"b": 1 - b}
+        self.to_z, self.to_core, self.fwd = [], [], []
+        for i in range(parts):
+            at = slice(i * rows, (i + 1) * rows)
+            for kind, (slot, dev, out) in enumerate(
+                (
+                    (self.me, deep, self.to_z),
+                    (self.me, core, self.to_core),
+                    (self.z_peer, core, self.fwd),
+                )
+            ):
+                n = kind * parts + i
+                ref = r.ag.at[slot, at]
+                out.append(remote(ref, ref, r.ag_s.at[n], r.ag_r.at[n], dev))
+
+    def norm_send(self, i, x_ref, gain, shift):
+        r = self.r
+        rows = r.ag.shape[1] // self.parts
+        step = 64
+
+        def norm(it, carry):
+            at = pl.ds(pl.multiple_of(i * rows + it * step, step), step)
+            n, _ = ln_parts(x_ref[at, :].astype(F32))
+            r.ag[self.me, at, :] = (n * gain + shift).astype(BF)
+            return carry
+
+        lax.fori_loop(0, rows // step, norm, 0)
+        self.to_z[i].start()
+        self.to_core[i].start()
+
+    def forward(self):
+        for i in range(self.parts):
+            self.to_z[i].wait_recv()
+            self.fwd[i].start()
+
+    def project(self, slot, w, bias):
+        r = self.r
+        ld = r.vt.shape[1]
+        v = nn(r.ag[slot], w) + bias
+        r.qkv[slot] = v.astype(BF)
+        r.qt[slot] = pad_heads_lanes(v[:, :ld].T).astype(BF)
+        r.vt[slot] = v[:, 2 * ld :].T.astype(BF)
+
+    def project_all(self, w, bias):
+        self.project(self.me, w, bias)
+        self.project(self.z_peer, w, bias)
+        landed(self.to_core)
+        self.project(self.core_peer, w, bias)
+        landed(self.fwd)
+        self.project(self.far_peer, w, bias)
+
+    def block(self, i, j, m, l, neg, diag):
+        r = self.r
+        ld, rows = r.vt.shape[1], r.vt.shape[2]
+        s = nn(r.qkv[j, :, ld : 2 * ld], r.qt[i])
         if diag:
             s = jnp.where(causal_mask(rows), s, -1e30)
             m_new = jnp.max(s, axis=0, keepdims=True)
@@ -151,103 +279,345 @@
         p = jnp.exp2(s * SCALE2 - base)
         l_new = jnp.sum(p, axis=0, keepdims=True)
         pb = p.astype(BF)
-        o0 = nn(vt_s[j, :HEAD_DIM, :], pb[:, :rows])
-        o1 = nn(vt_s[j, HEAD_DIM:, :], pb[:, rows:])
+        o0 = nn(r.vt[j, :HEAD_DIM, :], pb[:, :rows])
+        o1 = nn(r.vt[j, HEAD_DIM:, :], pb[:, rows:])
         if diag:
-            acc_s[:HEAD_DIM, :] = o0
-            acc_s[HEAD_DIM:, :] = o1
+            r.acc[:HEAD_DIM, :] = o0
+            r.acc[HEAD_DIM:, :] = o1
         else:
             alpha = jnp.exp2((m - m_new) * SCALE2)
             l_new = l * alpha + l_new
-            acc_s[:HEAD_DIM, :] = acc_s[:HEAD_DIM, :] * alpha[:, :rows] + o0
-            acc_s[HEAD_DIM:, :] = acc_s[HEAD_DIM:, :] * alpha[:, rows:] + o1
+            r.acc[:HEAD_DIM, :] = r.acc[:HEAD_DIM, :] * alpha[:, :rows] + o0
+            r.acc[HEAD_DIM:, :] = r.acc[HEAD_DIM:, :] * alpha[:, rows:] + o1
         return m_new, l_new
 
-    def a2a(i):
-        ic, ib = i // 2, i % 2
-        slot = 2 * (ic - c) * (ic - c) + (ib - b) * (ib - b)
-        return pltpu.make_async_remote_copy(
-            src_ref=ob_s.at[i],
-            dst_ref=att_ref.at[:, pl.ds(pl.multiple_of(me * ld, ld), ld)],
-            send_sem=a2a_send.at[slot],
-            recv_sem=a2a_recv.at[slot],
-            device_id={"c": ic, "b": ib},
-            device_id_type=MESH,
+    def attend(self, neg, hooks):
+        r, c, b, me = self.r, self.c, self.b, self.me
+        ld, rows = r.vt.shape[1], r.vt.shape[2]
+        group = r.ag.shape[0]
+        mine = r.att.at[:, pl.ds(pl.multiple_of(me * ld, ld), ld)]
+
+        def row(it, carry):
+            i = group - 1 - it
+            m, l = self.block(i, i, None, None, neg, True)
+            m, l = lax.fori_loop(
+                0, i, lambda j, ml: self.block(i, j, ml[0], ml[1], neg, False), (m, l)
+            )
+            inv = 1.0 / l
+            ot = jnp.concatenate(
+                [r.acc[:HEAD_DIM, :] * inv[:, :rows], r.acc[HEAD_DIM:, :] * inv[:, rows:]], axis=0
+            )
+            r.ot[i] = ot
+            r.lse[i] = jnp.broadcast_to(m * SCALE2 + jnp.log(l) * LOG2E, r.lse.shape[1:])
+            r.ob[i] = ot.T.astype(BF)
+            ic, ib = i // 2, i % 2
+            slot = 2 * (ic - c) * (ic - c) + (ib - b) * (ib - b)
+
+            @pl.when(i == me)
+            def _():
+                mine[...] = r.ob[i]
+
+            @pl.when(i != me)
+            def _():
+                dev = {"c": ic, "b": ib}
+                remote(r.ob.at[i], mine, r.x_s.at[slot], r.x_r.at[slot], dev).start()
+
+            for n, hook in hooks:
+                pl.when(it == n)(hook)
+            return carry
+
+        lax.fori_loop(0, group, row, 0)
+
+    def finish(self):
+        r = self.r
+        for slot in range(1, r.ag.shape[0]):
+            one = remote(
+                r.ob.at[0], r.ob.at[0], r.x_s.at[slot], r.x_r.at[slot], {"c": 1 - self.c}
+            )
+            one.wait_send()
+            one.wait_recv()
+        sent(self.to_z + self.to_core + self.fwd)
+
+
+ATT_OUT = ("ag", "qkv", "ot", "lse", "att")
+ATT_SCRATCH = ("qt", "vt", "ob", "acc", "ag_s", "ag_r", "x_s", "x_r")
+PARTS = 4
+
+
+def att_out(rows, width, ld):
+    g = 4
+    return [
+        jax.ShapeDtypeStruct((g, rows, width), BF),
+        jax.ShapeDtypeStruct((g, rows, 3 * ld), BF),
+        jax.ShapeDtypeStruct((g, ld, rows), F32),
+        jax.ShapeDtypeStruct((g, 8, 2 * rows), F32),
+        jax.ShapeDtypeStruct((rows, width), BF),
+    ]
+
+
+def att_scratch(rows, ld):
+    g = 4
+    return [
+        pltpu.VMEM((g, ld, 2 * rows), BF),
+        pltpu.VMEM((g, ld, rows), BF),
+        pltpu.VMEM((g, rows, ld), BF),
+        pltpu.VMEM((ld, rows), F32),
+        pltpu.SemaphoreType.DMA((3 * PARTS,)),
+        pltpu.SemaphoreType.DMA((3 * PARTS,)),
+        pltpu.SemaphoreType.DMA((4,)),
+        pltpu.SemaphoreType.DMA((4,)),
+    ]
+
+
+FIRST_IN = ("tok", "wqkv", "bqv", "clips", "bup", "gain", "shift", "wo", "wu", "wd")
+FIRST_OUT = ("xo", "wj", "smo", "full", "next", "bu")
+FIRST_SCRATCH = (
+    "wq_in", "sm", "bu_s", "t_s", "t_r", "wq_s", "wq_r", "sm_s", "sm_r", "bu_ss", "bu_rs",
+    "d0_s", "d0_r", "d1_s", "d1_r", "own_sem", "p_s", "p_r",
+)
+
+
+def attn_first_kernel(*refs):
+    r = Refs(FIRST_IN + ATT_OUT + FIRST_OUT + ATT_SCRATCH + FIRST_SCRATCH, refs)
+    y, x, c, h, b = place()
+    t = 2 * h + b
+    piece = c * 4 + 2 * y + x
+    stays = c == h
+    moves = jnp.logical_not(stays)
+    rows, width = r.tok.shape
+    ld = r.vt.shape[1]
+    partner = {"c": 1 - c, "h": 1 - h}
+    r.sm[...] = jnp.zeros(r.sm.shape, F32)
+    for l in range(2):
+        r.sm[l : l + 1, 0:ld] = row_of(r.bqv, l, 0)
+        r.sm[l : l + 1, 2 * ld : 3 * ld] = row_of(r.bqv, l, 1)
+    whole = r.clips[0:1, 0:1] == 4 * rows
+    r.sm[2:3, :] = jnp.broadcast_to(jnp.where(whole, 0.0, -1e30), (1, r.sm.shape[1]))
+    r.bu_s[...] = jnp.zeros(r.bu_s.shape, F32)
+    r.bu_s[0:2, :] = r.bup[...].astype(F32)
+    r.bu[t] = r.bu_s[...]
+    meet(
+        [{"b": 1 - b}, {"c": 1 - c}, {"c": 1 - c, "b": 1 - b}, partner]
+        + [{"h": 1 - h}, {"h": 1 - h, "b": 1 - b}]
+        + [{"k": 2 * y + 1 - x}, {"k": 2 * (1 - y) + x}]
+    )
+    n = rows // PARTS
+    tok = [
+        remote(
+            r.tok.at[i * n : (i + 1) * n],
+            r.xo.at[i * n : (i + 1) * n],
+            r.t_s.at[i],
+            r.t_r.at[i],
+            partner,
         )
-
-    def row(it, carry):
-        i = group - 1 - it
-        m, l = block(i, i, None, None, True)
-        m, l = lax.fori_loop(0, i, lambda j, ml: block(i, j, ml[0], ml[1], False), (m, l))
-        inv = 1.0 / l
-        ot = jnp.concatenate(
-            [acc_s[:HEAD_DIM, :] * inv[:, :rows], acc_s[HEAD_DIM:, :] * inv[:, rows:]], axis=0
-        )
-        ot_ref[i] = ot
-        lse_ref[i] = jnp.broadcast_to(m * SCALE2 + jnp.log(l) * LOG2E, lse_ref.shape[1:])
-        ob_s[i] = ot.T.astype(BF)
-
-        @pl.when(i == me)
+        for i in range(PARTS)
+    ]
+    small = remote(r.sm, r.smo, r.sm_s, r.sm_r, partner)
+    wq = [
+        remote(r.wqkv.at[l], r.wq_in.at[l], r.wq_s.at[l], r.wq_r.at[l], partner) for l in range(2)
+    ]
+    weights = (r.wo, r.wu, r.wd)
+    deep0 = DepthGather(0, weights, lambda q: r.full.at[piece, q], r.d0_s, r.d0_r)
+    deep1 = DepthGather(1, weights, lambda q: r.next.at[q], r.d1_s, r.d1_r)
+    plane = PlaneGather(
+        0, weights, r.full, lambda q: r.full.at[piece, q], r.own_sem, r.p_s, r.p_r
+    )
+    ups = [
+        remote(r.bu_s, r.bu.at[t], r.bu_ss.at[i - 1], r.bu_rs.at[i - 1], {"h": hh, "b": bb})
+        for i, hh, bb in depth_peers(h, b)
+    ]
+
+    @pl.when(moves)
+    def _():
+        begin(tok + [small, wq[0]])
+
+    @pl.when(stays)
+    def _():
+        r.smo[...] = r.sm[...]
+
+    begin(deep0.copies + plane.own + ups)
+    att = Attention(r, PARTS)
+    gain, shift = row_of(r.gain, 0, 0), row_of(r.shift, 0, 0)
+    for i in range(PARTS):
+
+        @pl.when(stays)
         def _():
-            att_ref[:, pl.ds(pl.multiple_of(me * ld, ld), ld)] = ob_s[i]
-
-        @pl.when(i != me)
+            r.xo[i * n : (i + 1) * n, :] = r.tok[i * n : (i + 1) * n, :]
+
+        pl.when(moves)(tok[i].wait_recv)
+        att.norm_send(i, r.xo, gain, shift)
+    att.forward()
+
+    def join(l):
+        @pl.when(moves)
         def _():
-            a2a(i).start()
-
-        return carry
-
-    lax.fori_loop(0, group, row, 0)
-    to_z.wait_send()
-    to_core.wait_send()
-    fwd.wait_send()
-    for slot in range(1, group):
-        cp = pltpu.make_async_remote_copy(
-            src_ref=ob_s.at[0],
-            dst_ref=ob_s.at[0],
-            send_sem=a2a_send.at[slot],
-            recv_sem=a2a_recv.at[slot],
-            device_id={"c": 1 - c, "b": b},
-            device_id_type=MESH,
-        )
-        cp.wait_send()
-        cp.wait_recv()
+            wq[l].wait_recv()
+            for i in range(3):
+                r.wj[l, :, i * ld : (i + 1) * ld] = r.wq_in[l, i]
+
+        @pl.when(stays)
+        def _():
+            for i in range(3):
+                r.wj[l, :, i * ld : (i + 1) * ld] = r.wqkv[l, i]
+
+    join(0)
+    pl.when(moves)(small.wait_recv)
+    att.project_all(r.wj[0], r.smo[0:1, : 3 * ld])
+    landed(deep0.copies)
+    begin(plane.a)
+
+    def hook_0():
+        landed(plane.a)
+        begin(plane.b)
+        pl.when(moves)(wq[1].start)
+        begin(deep1.copies)
+
+    def hook_1():
+        landed(plane.b)
+        begin(plane.c)
+
+    att.attend(r.smo[2:3, 0:1], ((0, hook_0), (1, hook_1)))
+    join(1)
+    landed(deep1.copies + ups)
+    att.finish()
+    landed(plane.c)
+    plane.drain()
+    sent(deep0.copies + deep1.copies + ups)
+    pl.when(moves)(lambda: sent(tok + wq + [small]))
+
+
+def anywhere(n):
+    return [pl.BlockSpec(memory_space=pl.ANY)] * n
 
 
 def vm(n):
     return [pl.BlockSpec(memory_space=pltpu.VMEM)] * n
 
 
-def attn_fwd(x, gain, shift, w, bias, neg, cid):
-    rows, width = x.shape
-    ld = w.shape[1] // 3
-    g = 4
+def gather_sems():
+    return [
+        pltpu.SemaphoreType.DMA((3,)),
+        pltpu.SemaphoreType.DMA((15,)),
+        pltpu.SemaphoreType.DMA((15,)),
+    ]
+
+
+def attn_first(tok, wqkv, bqv, clips, bup, gain, shift, wo, wu, wd, cid):
+    rows, width = tok.shape
+    layers, _, _, ld = wqkv.shape
+    piece = wo.shape[2] + wu.shape[2] + wd.shape[2]
+    quarter = wu.shape[3]
+    dma = pltpu.SemaphoreType.DMA
     return pl.pallas_call(
-        attn_fwd_kernel,
-        name="attn_fwd",
-        out_shape=(
-            jax.ShapeDtypeStruct((g, rows, width), BF),
-            jax.ShapeDtypeStruct((g, rows, 3 * ld), BF),
-            jax.ShapeDtypeStruct((g, ld, rows), F32),
-            jax.ShapeDtypeStruct((g, 8, 2 * rows), F32),
-            jax.ShapeDtypeStruct((rows, width), BF),
+        attn_first_kernel,
+        name="attn_first",
+        out_shape=tuple(
+            att_out(rows, width, ld)
+            + [
+                jax.ShapeDtypeStruct((rows, width), BF),
+                jax.ShapeDtypeStruct((layers, width, 3 * ld), BF),
+                jax.ShapeDtypeStruct((8, width), F32),
+                jax.ShapeDtypeStruct((8, 4, piece, width), BF),
+                jax.ShapeDtypeStruct((4, piece, width), BF),
+                jax.ShapeDtypeStruct((4, 8, quarter), F32),
+            ]
         ),
-        in_specs=vm(6),
-        out_specs=tuple(vm(5)),
-        scratch_shapes=[
-            pltpu.VMEM((g, ld, 2 * rows), BF),
-            pltpu.VMEM((g, ld, rows), BF),
-            pltpu.VMEM((g, rows, ld), BF),
-            pltpu.VMEM((ld, rows), F32),
-            pltpu.SemaphoreType.DMA((3,)),
-            pltpu.SemaphoreType.DMA((3,)),
-            pltpu.SemaphoreType.DMA((4,)),
-            pltpu.SemaphoreType.DMA((4,)),
-        ],
+        in_specs=vm(7) + anywhere(3),
+        out_specs=tuple(vm(11)),
+        scratch_shapes=att_scratch(rows, ld)
+        + [
+            pltpu.VMEM(wqkv.shape, BF),
+            pltpu.VMEM((8, width), F32),
+            pltpu.VMEM((8, quarter), F32),
+            dma((PARTS,)),
+            dma((PARTS,)),
+            dma((2,)),
+            dma((2,)),
+            dma,
+            dma,
+            dma((3,)),
+            dma((3,)),
+            dma((9,)),
+            dma((9,)),
+            dma((9,)),
+            dma((9,)),
+        ]
+        + gather_sems(),
         compiler_params=pltpu.CompilerParams(
             collective_id=cid, has_side_effects=True, vmem_limit_bytes=VMEM_LIMIT
         ),
-    )(x, gain, shift, w, bias, neg)
+    )(tok, wqkv, bqv, clips, bup, gain, shift, wo, wu, wd)
+
+
+NEXT_IN = ("x", "wj", "smo", "gain", "shift", "eighth", "cot", "wo", "wu", "wd")
+NEXT_OUT = ("full", "coto")
+NEXT_SCRATCH = ("own_sem", "p_s", "p_r", "e_sem", "sw")
+
+
+def attn_next_kernel(*refs):
+    r = Refs(NEXT_IN + ATT_OUT + NEXT_OUT + ATT_SCRATCH + NEXT_SCRATCH, refs)
+    y, x, c, h, b = place()
+    piece = c * 4 + 2 * y + x
+    ld = r.vt.shape[1]
+    meet(
+        [{"b": 1 - b}, {"c": 1 - c}, {"c": 1 - c, "b": 1 - b}, {"c": 1 - c, "h": 1 - h}]
+        + [{"k": 2 * y + 1 - x}, {"k": 2 * (1 - y) + x}]
+    )
+    att = Attention(r, PARTS)
+    plane = PlaneGather(
+        1, (r.wo, r.wu, r.wd), r.full, lambda q: r.eighth.at[q], r.own_sem, r.p_s, r.p_r
+    )
+    swap = Swap(r.cot, r.coto, r.sw)
+    gain, shift = row_of(r.gain, 1, 0), row_of(r.shift, 1, 0)
+    for i in range(PARTS):
+        att.norm_send(i, r.x, gain, shift)
+    begin(plane.a + plane.own)
+    mine = [
+        pltpu.make_async_copy(r.eighth.at[q], r.full.at[piece, q], r.e_sem.at[i - 1])
+        for i, q in ((i, 2 * hh + bb) for i, hh, bb in depth_peers(h, b))
+    ]
+    begin(mine)
+    att.forward()
+    att.project_all(r.wj[1], r.smo[1:2, : 3 * ld])
+    for one in mine:
+        one.wait()
+    landed(plane.a)
+    begin(plane.b)
+    swap.start()
+
+    def hook_0():
+        landed(plane.b)
+        begin(plane.c)
+
+    att.attend(r.smo[2:3, 0:1], ((0, hook_0),))
+    att.finish()
+    landed(plane.c)
+    plane.drain()
+    swap.wait()
+
+
+def attn_next(x, wj, smo, gain, shift, eighth, cot, wo, wu, wd, cid):
+    rows, width = x.shape
+    ld = wj.shape[2] // 3
+    return pl.pallas_call(
+        attn_next_kernel,
+        name="attn_next",
+        out_shape=tuple(
+            att_out(rows, width, ld)
+            + [
+                jax.ShapeDtypeStruct((8,) + eighth.shape, BF),
+                jax.ShapeDtypeStruct(cot.shape, BF),
+            ]
+        ),
+        in_specs=vm(7) + anywhere(3),
+        out_specs=tuple(vm(7)),
+        scratch_shapes=att_scratch(rows, ld)
+        + gather_sems()
+        + [pltpu.SemaphoreType.DMA((3,)), pltpu.SemaphoreType.DMA((3,))],
+        compiler_params=pltpu.CompilerParams(
+            collective_id=cid, has_side_effects=True, vmem_limit_bytes=VMEM_LIMIT
+        ),
+    )(x, wj, smo, gain, shift, eighth, cot, wo, wu, wd)
 
 
 BWD_IN = (
@@ -267,7 +637,7 @@
 CLOSE_SCRATCH = ("crd", "crt", "ccs", "ccr")
 
 
-def attn_bwd_kernel(closing, *refs):
+def attn_bwd_kernel(layer, closing, *refs):
     names = BWD_IN + (CLOSE_IN if closing else ("sw_in",))
     names += BWD_OUT + (CLOSE_OUT if closing else ("sw_out",))
     names += BWD_SCRATCH + (CLOSE_SCRATCH if closing else ("sw_sem",))
@@ -275,7 +645,8 @@
     ga_ref, x_ref, gain_ref, gmid_ref, ag_ref, qkv_ref = (
         r.ga_ref, r.x_ref, r.gain_ref, r.gmid_ref, r.ag_ref, r.qkv_ref
     )
-    ot_ref, lse_ref, w_ref, neg_ref = r.ot_ref, r.lse_ref, r.w_ref, r.neg_ref
+    ot_ref, lse_ref, w_ref, neg_ref = r.ot_ref, r.lse_ref, r.w_ref.at[layer], r.neg_ref
+    gain = row_of(gain_ref, layer, 0)
     gx_ref, gb_ref, gln_ref = r.gx_ref, r.gb_ref, r.gln_ref
     do_s, qt_s, qp_s, dot_s, dop_s, kt_s = r.do_s, r.qt_s, r.qp_s, r.dot_s, r.dop_s, r.kt_s
     delta_s, dk_s, dv_s, dqt_s, part_s = r.delta_s, r.dk_s, r.dv_s, r.dqt_s, r.part_s
@@ -344,7 +715,7 @@
         close.stage_1()
     else:
         swap.start()
-    neg = neg_ref[0:1, 0:1]
+    neg = neg_ref[2:3, 0:1]
     gwt_ref[...] = jnp.zeros(gwt_ref.shape, F32)
     gb_ref[...] = jnp.zeros(gb_ref.shape, F32)
 
@@ -454,7 +825,7 @@
         at = pl.ds(pl.multiple_of(it * step, step), step)
         g = own_s[at, :] + core_in[0, at, :].astype(F32) + z_in[at, :].astype(F32)
         n, rstd = ln_parts(x_ref[at, :].astype(F32))
-        u = g * gain_ref[...]
+        u = g * gain
         mu = jnp.mean(u, axis=-1, keepdims=True)
         mun = jnp.mean(u * n, axis=-1, keepdims=True)
         gx_ref[at, :] = (gmid_ref[at, :] + rstd * (u - mu - n * mun)).astype(gx_ref.dtype)
@@ -479,9 +850,9 @@
         swap.wait()
 
 
-def attn_bwd(ga, x, gain, gmid, ag, qkv, ot, lse, w, neg, p, extra, out_kind, cid):
+def attn_bwd(layer, ga, x, gain, gmid, ag, qkv, ot, lse, w, neg, p, extra, out_kind, cid):
     rows, width = x.shape
-    ld = w.shape[1] // 3
+    ld = w.shape[2] // 3
     g = 4
     p = p.reshape((2, 2, 2) + p.shape[1:])
     closing = len(extra) == 2
@@ -503,7 +874,7 @@
         out += [jax.ShapeDtypeStruct(extra[0].shape, BF)]
         more = [pltpu.SemaphoreType.DMA((3,))]
     return pl.pallas_call(
-        functools.partial(attn_bwd_kernel, closing),
+        functools.partial(attn_bwd_kernel, layer, closing),
         name="attn_bwd",
         out_shape=tuple(out),
         in_specs=vm(11 + len(extra)),
@@ -554,14 +925,29 @@
 
 
 def mlp_fwd_kernel(
-    att_ref, x_ref, w_ref, bu_ref, vec_ref, mid_ref, hid_ref, dg_ref, out_ref, in_s, out_s
+    layer,
+    att_ref,
+    x_ref,
+    w_ref,
+    bu_ref,
+    bo_ref,
+    bd_ref,
+    gain_ref,
+    shift_ref,
+    mid_ref,
+    hid_ref,
+    dg_ref,
+    out_ref,
+    in_s,
+    out_s,
 ):
     n_out = att_ref.shape[1] // 32
     n_up = (w_ref.shape[2] - n_out) // 2
     quarter = w_ref.shape[3]
     att_w = 8 * n_out
     width = x_ref.shape[1]
-    acc = x_ref[...].astype(F32) + vec_ref[0:1, :]
+    gain, shift = row_of(gain_ref, layer, 1), row_of(shift_ref, layer, 1)
+    acc = x_ref[...].astype(F32) + row_of(bo_ref, layer)
     for q in range(4):
         wo = w_ref[:, q, :n_out, :].reshape(att_w, width)
         acc = acc + nn(att_ref[:, q * att_w : (q + 1) * att_w], wo)
@@ -571,11 +957,11 @@
     def norm(it, carry):
         at = pl.ds(pl.multiple_of(it * step, step), step)
         n, _ = ln_parts(mid_ref[at, :])
-        in_s[at, :] = (n * vec_ref[2:3, :] + vec_ref[3:4, :]).astype(BF)
+        in_s[at, :] = (n * gain + shift).astype(BF)
         return carry
 
     lax.fori_loop(0, x_ref.shape[0] // step, norm, 0)
-    out_s[...] = mid_ref[...] + vec_ref[1:2, :]
+    out_s[...] = mid_ref[...] + row_of(bd_ref, layer)
 
     def part(q, carry):
         wu = w_ref[:, q, n_out : n_out + n_up, :].reshape(8 * n_up, quarter)
@@ -584,7 +970,7 @@
 
         def chunk(r, cc):
             at = pl.ds(pl.multiple_of(r * half, half), half)
-            pre = nn(in_s[at, :], wu) + bu_ref[q, 0:1, :]
+            pre = nn(in_s[at, :], wu) + bu_ref[q, layer : layer + 1, :]
             act, der = gelu_both(pre)
             act = act.astype(BF)
             hid_ref[q, at, :] = act
@@ -599,11 +985,11 @@
     out_ref[...] = out_s[...].astype(out_ref.dtype)
 
 
-def mlp_fwd(att, x, w, bu, vec, out_kind):
+def mlp_fwd(layer, att, x, w, bu, vecs, out_kind):
     rows, width = x.shape
     quarter = w.shape[3]
     return pl.pallas_call(
-        mlp_fwd_kernel,
+        functools.partial(mlp_fwd_kernel, layer),
         name="mlp_fwd",
         out_shape=(
             jax.ShapeDtypeStruct((rows, width), F32),
@@ -611,21 +997,23 @@
             jax.ShapeDtypeStruct((4, rows, quarter), BF),
             jax.ShapeDtypeStruct((rows, width), out_kind),
         ),
-        in_specs=vm(5),
+        in_specs=vm(8),
         out_specs=tuple(vm(4)),
         scratch_shapes=[pltpu.VMEM((rows, width), BF), pltpu.VMEM((rows, width), F32)],
         compiler_params=pltpu.CompilerParams(vmem_limit_bytes=VMEM_LIMIT),
-    )(att, x, w, bu, vec)
+    )(att, x, w, bu, *vecs)
 
 
 def mlp_bwd_kernel(
+    layer,
     g_ref,
     mid_ref,
     att_ref,
     hid_ref,
     dg_ref,
     w_ref,
-    vec_ref,
+    gain_ref,
+    shift_ref,
     p_ref,
     gmid_ref,
     ga_ref,
@@ -642,10 +1030,11 @@
     rows, width = g_ref.shape
     step = 64
     small_ref[...] = jnp.zeros(small_ref.shape, F32)
+    gain, shift = row_of(gain_ref, layer, 1), row_of(shift_ref, layer, 1)
 
     def prep(it, carry):
         at = pl.ds(pl.multiple_of(it * step, step), step)
-        g = g_ref[at, :]
+        g = g_ref[at, :].astype(F32)
         low_s[at, :] = g.astype(BF)
         small_ref[0:1, :] += jnp.sum(g, axis=0, keepdims=True)
         return carry
@@ -654,9 +1043,9 @@
 
     def flip(it, carry):
         at = pl.ds(pl.multiple_of(it * 128, 128), 128)
-        lowt_s[:, at] = g_ref[at, :].T.astype(BF)
+        lowt_s[:, at] = g_ref[at, :].astype(F32).T.astype(BF)
         n, _ = ln_parts(mid_ref[at, :])
-        int_s[:, at] = (n * vec_ref[2:3, :] + vec_ref[3:4, :]).astype(BF).astype(F32).T.astype(BF)
+        int_s[:, at] = (n * gain + shift).astype(BF).astype(F32).T.astype(BF)
         return carry
 
     for it in range(rows // 128):
@@ -684,10 +1073,10 @@
         at = pl.ds(pl.multiple_of(it * step, step), step)
         gm = gm_s[at, :]
         n, rstd = ln_parts(mid_ref[at, :])
-        u = gm * vec_ref[2:3, :]
+        u = gm * gain
         mu = jnp.mean(u, axis=-1, keepdims=True)
         mun = jnp.mean(u * n, axis=-1, keepdims=True)
-        g = g_ref[at, :] + rstd * (u - mu - n * mun)
+        g = g_ref[at, :].astype(F32) + rstd * (u - mu - n * mun)
         gmid_ref[at, :] = g
         low_s[at, :] = g.astype(BF)
         small_ref[1:2, :] += jnp.sum(g, axis=0, keepdims=True)
@@ -704,10 +1093,10 @@
         put(q, 0, n_out, nn(att_t, low_s[...]).astype(BF))
 
 
-def mlp_bwd(g, mid, att, hid, dg, w, vec):
+def mlp_bwd(layer, g, mid, att, hid, dg, w, gain, shift):
     rows, width = g.shape
     return pl.pallas_call(
-        mlp_bwd_kernel,
+        functools.partial(mlp_bwd_kernel, layer),
         name="mlp_bwd",
         out_shape=(
             jax.ShapeDtypeStruct(w.shape, BF),
@@ -715,7 +1104,7 @@
             jax.ShapeDtypeStruct((rows, width), BF),
             jax.ShapeDtypeStruct((8, width), F32),
         ),
-        in_specs=vm(7),
+        in_specs=vm(8),
         out_specs=tuple(vm(4)),
         scratch_shapes=[
             pltpu.VMEM((rows, width), BF),
@@ -724,64 +1113,7 @@
             pltpu.VMEM((rows, width), F32),
         ],
         compiler_params=pltpu.CompilerParams(vmem_limit_bytes=VMEM_LIMIT),
-    )(g, mid, att, hid, dg, w, vec)
-
-
-def place():
-    k = lax.axis_index("k")
-    return lax.div(k, 2), lax.rem(k, 2), lax.axis_index("c"), lax.axis_index("h"), lax.axis_index("b")
-
-
-def plane_peers(y, x, c):
-    found = []
-    for dy in range(2):
-        for dx in range(2):
-            for dc in range(2):
-                if dy + dx + dc:
-                    yy = 1 - y if dy else y
-                    xx = 1 - x if dx else x
-                    cc = 1 - c if dc else c
-                    found.append((dy * 4 + dx * 2 + dc, {"k": 2 * yy + xx, "c": cc}))
-    return found
-
-
-def depth_peers(h, b):
-    return [(1, h, 1 - b), (2, 1 - h, b), (3, 1 - h, 1 - b)]
-
-
-def meet(devices):
-    bar = pltpu.get_barrier_semaphore()
-    for dev in devices:
-        pl.semaphore_signal(bar, inc=1, device_id=dev, device_id_type=MESH)
-    pl.semaphore_wait(bar, len(devices))
-
-
-def remote(src, dst, send, recv, dev):
-    return pltpu.make_async_remote_copy(
-        src_ref=src, dst_ref=dst, send_sem=send, recv_sem=recv, device_id=dev, device_id_type=MESH
-    )
-
-
-class Refs:
-    def __init__(self, names, refs):
-        assert len(names) == len(refs)
-        for name, ref in zip(names, refs):
-            setattr(self, name, ref)
-
-
-def begin(copies):
-    for one in copies:
-        one.start()
-
-
-def landed(copies):
-    for one in copies:
-        one.wait_recv()
-
-
-def sent(copies):
-    for one in copies:
-        one.wait_send()
+    )(g, mid, att, hid, dg, w, gain, shift)
 
 
 def add_low(a, b):
@@ -951,22 +1283,6 @@
         pltpu.SemaphoreType.DMA((25,)),
         pltpu.SemaphoreType.DMA((25,)),
     ]
-
-
-class Swap:
-    def __init__(self, src, dst, sems):
-        _, _, c, h, _ = place()
-        self.stays = c == h
-        self.out = remote(src, dst, sems.at[0], sems.at[1], {"c": 1 - c, "h": 1 - h})
-        self.own = pltpu.make_async_copy(src, dst, sems.at[2])
-
-    def start(self):
-        pl.when(jnp.logical_not(self.stays))(self.out.start)
-        pl.when(self.stays)(self.own.start)
-
-    def wait(self):
-        pl.when(jnp.logical_not(self.stays))(self.out.wait)
-        pl.when(self.stays)(self.own.wait)
 
 
 def all_near(y, x, c, h, b):
@@ -1113,99 +1429,55 @@
     ln_gain,
     ln_bias,
 ):
-    rows, width = tokens.shape
-    layers = w_qkv.shape[0]
-    ld = w_qkv.shape[3]
-    n_outer = lax.axis_size("o")
+    width = tokens.shape[1]
+    layers, local_out = w_out.shape[:2]
     quarter = w_up.shape[2]
-
-    perm = []
-    for lead in range(4 * n_outer):
-        for cc in range(2):
-            for hh in range(2):
-                for bb in range(2):
-                    perm.append((lead * 8 + cc * 4 + hh * 2 + bb, lead * 8 + hh * 4 + cc * 2 + bb))
-
-    def swap(v):
-        return lax.ppermute(v, AXES, perm)
-
-    piece = lax.axis_index("k") * 2 + lax.axis_index("c")
-
-    def gather_weights(l):
-        def cut(v):
-            n = v.shape[0] // 8
-            return lax.dynamic_slice_in_dim(v, piece * n, n, 0)
-
-        rows_b = jnp.broadcast_to(b_up[l][None], (16, quarter))
-        own = jnp.concatenate([cut(w_out[l]), cut(w_up[l]), cut(w_down[l]), rows_b], axis=0)
-        g1 = lax.all_gather(own, ("h", "b"), axis=0, tiled=False)
-        g2 = lax.all_gather(g1[:, :-16], ("k", "c"), axis=0, tiled=False)
-        return g2, g1[:, -16, :]
-
-    weights = [gather_weights(l) for l in range(layers)]
-    n_out = ld // 8
-    n_up = width // 8
-
-    def vectors(l):
-        rows4 = [b_out[l].astype(F32), b_down[l].astype(F32), gains[l, 1], shifts[l, 1]]
-        return jnp.concatenate([jnp.stack(rows4), jnp.zeros((4, width), F32)])
-
-    x = swap(tokens)
-    wq = swap(jnp.transpose(w_qkv, (0, 2, 1, 3)).reshape(layers, width, 3 * ld))
-    small = swap(b_qv)
-    lengths = swap(clip_lengths)
-    slot_len = rows * 4
-    neg = jnp.where(lengths[0, 0] == slot_len, 0.0, -1e30).astype(F32)
-    neg = jnp.broadcast_to(neg, (8, 128))
-    gains = ln_gain.astype(F32)
-    shifts = ln_bias.astype(F32)
-    g_in = swap(cotangent)
-
-    stream = x.astype(F32)
-    stored = []
-    for l in range(layers):
-        bias = jnp.concatenate(
-            [small[l, 0], jnp.zeros((ld,), BF), small[l, 1]]
-        ).astype(F32)[None]
-        ag, qkv, ot, lse, att = attn_fwd(
-            stream, gains[l, 0][None], shifts[l, 0][None], wq[l], bias, neg, 2 * l
-        )
-        w, bu = weights[l]
-        bu = jnp.broadcast_to(bu.astype(F32)[:, None], (4, 8, quarter))
-        vec = vectors(l)
-        mid, hid, dg, nxt = mlp_fwd(att, stream, w, bu, vec, BF if l == layers - 1 else F32)
-        stored.append((stream, ag, qkv, ot, lse, att, mid, hid, dg, w, vec))
-        stream = nxt
-    grad = g_in.astype(F32)
+    eighths = (
+        w_out.reshape(layers, 8, local_out // 8, width),
+        w_up.reshape(layers, 8, width // 8, quarter),
+        w_down.reshape(layers, 8, quarter // 8, width),
+    )
+    vecs = (b_out, b_down, ln_gain, ln_bias)
+    first = attn_first(tokens, w_qkv, b_qv, clip_lengths, b_up, ln_gain, ln_bias, *eighths, 0)
+    saved0, (stream, wj, smo, full0, eighth, bu) = first[:5], first[5:]
+    mid0, hid0, dg0, mid_stream = mlp_fwd(0, saved0[4], stream, full0, bu, vecs, F32)
+    second = attn_next(mid_stream, wj, smo, ln_gain, ln_bias, eighth, cotangent, *eighths, 1)
+    saved1, (full1, grad) = second[:5], second[5:]
+    mid1, hid1, dg1, out = mlp_fwd(1, saved1[4], mid_stream, full1, bu, vecs, BF)
+    stored = (
+        (stream, saved0, mid0, hid0, dg0, full0),
+        (mid_stream, saved1, mid1, hid1, dg1, full1),
+    )
     small, gln, gb = [None] * layers, [None] * layers, [None] * layers
     output = rc = gw = None
     for l in reversed(range(layers)):
-        stream_in, ag, qkv, ot, lse, att, mid, hid, dg, w, vec = stored[l]
-        p, g_mid, ga, small[l] = mlp_bwd(grad, mid, att, hid, dg, w, vec)
+        stream_in, (ag, qkv, ot, lse, att), mid, hid, dg, w = stored[l]
+        p, g_mid, ga, small[l] = mlp_bwd(l, grad, mid, att, hid, dg, w, ln_gain, ln_bias)
         top = l == layers - 1
-        extra = (stream,) if top else (rc, gw)
+        extra = (out,) if top else (rc, gw)
         grad, gw, gb[l], gln[l], rc, *rest = attn_bwd(
+            l,
             ga,
             stream_in,
-            gains[l, 0][None],
+            ln_gain,
             g_mid,
             ag,
             qkv,
             ot,
             lse,
-            wq[l],
-            neg,
+            wj,
+            smo,
             p,
             extra,
             F32 if l else BF,
-            2 * l + 1,
+            2 + l,
         )
         if top:
             output = rest[0]
         else:
             e1, gwo1 = rest
-    *grads, g_tok = tail(rc, gw, grad, e1, gwo1, small, gln, gb, 2 * layers)
-    if n_outer > 1:
+    *grads, g_tok = tail(rc, gw, grad, e1, gwo1, small, gln, gb, 4)
+    if lax.axis_size("o") > 1:
         grads = lax.psum(tuple(grads), "o")
     return (output, g_tok, *grads)
 

time: 433 us -> 371 us (0.86)
  blocking collectives: 35.9 us -> 0 us
  between operations: 14.4 us -> 0.73 us
  local copies, waits for them, and re-layouts: 23.8 us -> 11.3 us
  Pallas kernels: 344 us -> 356 us
  starting transfers between devices: 9.34 us -> 0 us
    all_gather x2 -> x0, blocking collectives: 35.9 us -> none  [gather_weights(): g1 = lax.all_gather(own, ('h', 'b'), axis=0, tiled=False)]
    pallas_call x8, Pallas kernels: 291 us -> 305 us  [the longest x2 115 us: attn_bwd(): pl.pallas_call(functools.partial(attn_bwd_kernel, layer, closing), name='...]
    ppermute x5 -> x0, starting transfers between devices: 9.26 us -> none  [swap(): return lax.ppermute(v, AXES, perm)]
    slice x6 -> x0, local copies, waits for them, and re-layouts: 5.68 us -> none  [the longest x2 1.76 us: gather_weights(): g2 = lax.all_gather(g1[:, :-16], ('k', 'c'), axis=0, tiled=False)]
    unnamed x53 -> x34, local copies, waits for them, and re-layouts: 11.6 us -> 11.3 us
  transfers between devices with their start and end apart: 7 -> 0, of which waited for: 0 -> 0; matrix products, arithmetic and copies ran while one was open for 2% -> 0% of each run, Pallas kernels for 28% -> 0%
where the time goes in v4:
time: 371 us; the launch traced here: 368 us
  Pallas kernels  356 us (96%)
  local copies, waits for them, and re-layouts  11.3 us (3%)
    pallas_call x2, Pallas kernels, attn_bwd(): pl.pallas_call(functools.partial(attn_bwd_kernel, layer, closing), name='...  115 us
    pallas_call x1, Pallas kernels, attn_first(): pl.pallas_call(attn_first_kernel, name='attn_first', out_shape=tuple(att_...  77.7 us
    pallas_call x1, Pallas kernels, tail(): pl.pallas_call(tail_kernel, name='tail_sums', out_shape=tuple((jax.ShapeD...  51.6 us
    pallas_call x1, Pallas kernels, attn_next(): pl.pallas_call(attn_next_kernel, name='attn_next', out_shape=tuple(att_ou...  45 us
    pallas_call x2, Pallas kernels, mlp_fwd(): pl.pallas_call(functools.partial(mlp_fwd_kernel, layer), name='mlp_fwd',...  34.4 us
    pallas_call x2, Pallas kernels, mlp_bwd(): pl.pallas_call(functools.partial(mlp_bwd_kernel, layer), name='mlp_bwd',...  32.3 us
    unnamed x34, local copies, waits for them, and re-layouts  11.3 us

profile of v4, /device:TPU:0, one launch (start us, length us, event | category | flops | bytes accessed | tf_op | source)
XLA Modules:
  0.0 368.3 jit_solution(14154080008570136874)
XLA Ops:
  0.6 77.7 %attn_first.1 = (bf16[4,512,512]{2,1,0:T(8,128)(2,1)}, bf16[4,512,384]{2,1,0:T(8,128)(2,1)}, f32[4,128,512]{2,1,0:T(8,128)}, f32[4,8,1024]{2,1,0:T(8,128)}, bf16...) custom-call(bf16[512,512]{1,0:T(8,128)(2,1)} %refs_0_.1, ...), custom_call_target="tpu_custom_call" | custom-call | tf_op jit(solution)/shard_map/attn_first/pallas_call | solution.py:511
  78.4 17.2 %mlp_fwd.2 = (f32[512,512]{1,0:T(8,128)}, bf16[4,512,512]{2,1,0:T(8,128)(2,1)}, bf16[4,512,512]{2,1,0:T(8,128)(2,1)}, f32[512,512]{1,0:T(8,128)}) custom-call(bf16[512,512]{1,0:T(8,128)(2,1)} %get-tuple-element.70.att_ref, bf16[512,512]{1,0:T(8,128)(2,1)} %get-tuple-element.71.x_ref.refs_1_, bf16[8,4,144,512]{3,2,1,0:T(8,128)(2,1)} %get-tuple-element.72.w_ref, ...), custom_call_target="tpu_custom_call" | custom-call | tf_op jit(solution)/shard_map/mlp_fwd/pallas_call | solution.py:991
  95.6 45.0 %attn_next.1 = (bf16[4,512,512]{2,1,0:T(8,128)(2,1)}, bf16[4,512,384]{2,1,0:T(8,128)(2,1)}, f32[4,128,512]{2,1,0:T(8,128)}, f32[4,8,1024]{2,1,0:T(8,128)}, bf16[...) custom-call(f32[512,512]{1,0:T(8,128)} %get-tuple-element.74.refs_0_.x_ref.refs_1_, ...), custom_call_target="tpu_custom_call" | custom-call | tf_op jit(solution)/shard_map/attn_next/pallas_call | solution.py:602
  140.6 17.2 %mlp_fwd.3 = (f32[512,512]{1,0:T(8,128)}, bf16[4,512,512]{2,1,0:T(8,128)(2,1)}, bf16[4,512,512]{2,1,0:T(8,128)(2,1)}, bf16[512,512]{1,0:T(8,128)(2,1)}) custom-call(bf16[512,512]{1,0:T(8,128)(2,1)} %get-tuple-element.79.att_ref, f32[512,512]{1,0:T(8,128)} %get-tuple-element.74.refs_0_.x_ref.refs_1_, bf16[8,4,144,512]{3,2,1,0:T(8,128)(2,1)} %get-tuple-element.80.w_ref, ...), custom_call_target="tpu_custom_call" | custom-call | tf_op jit(solution)/shard_map/mlp_fwd/pallas_call | solution.py:991
  157.8 16.1 %mlp_bwd.2 = (bf16[8,4,144,512]{3,2,1,0:T(8,128)(2,1)}, f32[512,512]{1,0:T(8,128)}, bf16[512,512]{1,0:T(8,128)(2,1)}, f32[8,512]{1,0:T(8,128)}) custom-call(bf16[512,512]{1,0:T(8,128)(2,1)} %get-tuple-element.78.g_ref, f32[512,512]{1,0:T(8,128)} %get-tuple-element.81.mid_ref, bf16[512,512]{1,0:T(8,128)(2,1)} %get-tuple-element.79.att_ref, ...), custom_call_target="tpu_custom_call" | custom-call | tf_op jit(solution)/shard_map/mlp_bwd/pallas_call | solution.py:1098
  173.8 55.7 %attn_bwd.2 = (f32[512,512]{1,0:T(8,128)}, bf16[8,48,512]{2,1,0:T(8,128)(2,1)}, f32[8,384]{1,0:T(8,128)}, f32[8,512]{1,0:T(8,128)}, bf16[4,144,512]{2,1,0:T(8,128)(2,1)}, /*index=5*/bf16[512,512]{1,0:T(8,128)(2,1)}) custom-call(bf16[512,512]{1,0:T(8,128)(2,1)} %get-tuple-element.84.refs_0_, f32[512,512]{1,0:T(8,128)} %get-tuple-element.74.refs_0_.x_ref.refs_1_, ...), custom_call_target="tpu_custom_call" | custom-call | tf_op jit(solution)/shard_map/attn_bwd/pallas_call | solution.py:876
  229.6 16.2 %mlp_bwd.3 = (bf16[8,4,144,512]{3,2,1,0:T(8,128)(2,1)}, f32[512,512]{1,0:T(8,128)}, bf16[512,512]{1,0:T(8,128)(2,1)}, f32[8,512]{1,0:T(8,128)}) custom-call(f32[512,512]{1,0:T(8,128)} %get-tuple-element.93.g_ref, f32[512,512]{1,0:T(8,128)} %get-tuple-element.94.mid_ref, bf16[512,512]{1,0:T(8,128)(2,1)} %get-tuple-element.70.att_ref, ...), custom_call_target="tpu_custom_call" | custom-call | tf_op jit(solution)/shard_map/mlp_bwd/pallas_call | solution.py:1098
  245.8 59.6 %attn_bwd.3 = (bf16[512,512]{1,0:T(8,128)(2,1)}, bf16[8,48,512]{2,1,0:T(8,128)(2,1)}, f32[8,384]{1,0:T(8,128)}, f32[8,512]{1,0:T(8,128)}, bf16[4,144,512]{2,1,0:...) custom-call(bf16[512,512]{1,0:T(8,128)(2,1)} %get-tuple-element.97.refs_0_, ...), custom_call_target="tpu_custom_call" | custom-call | tf_op jit(solution)/shard_map/attn_bwd/pallas_call | solution.py:876
  305.4 51.6 %tail_sums.1 = (f32[2,3,512,128]{3,2,1,0:T(8,128)}, f32[2,2,128]{2,1,0:T(2,128)}, f32[2,128,512]{2,1,0:T(8,128)}, f32[2,512]{1,0:T(2,128)}, f32[2,512,512]{2,1,0...) custom-call(bf16[4,144,512]{2,1,0:T(8,128)(2,1)} %get-tuple-element., ...), custom_call_target="tpu_custom_call" | custom-call | tf_op jit(solution)/shard_map/tail_sums/pallas_call | solution.py:1392
  357.0 0.0 copy-start.2
  357.0 0.0 copy-done.3
  357.0 0.8 copy.37
  357.8 1.9 copy.38
  359.7 1.1 copy.39
  360.9 0.6 copy.40
  361.4 0.8 copy.41
  362.2 0.6 copy.42
  362.8 1.3 copy.43
  364.2 0.6 copy.44
  364.7 0.4 copy-done
  365.2 1.3 copy.45
  366.5 0.6 copy.46
  367.1 0.6 copy.47
  367.7 0.6 copy.48
  (19 shorter events, 0.0 us)
Async XLA Ops:
  305.4 51.6 %copy-start.3 = (bf16[512,512]{1,0:T(8,128)(2,1)S(1)}, bf16[512,512]{1,0:T(8,128)(2,1)}, u32[]{:S(2)}) copy-start(bf16[512,512]{1,0:T(8,128)(2,1)} %get-tuple-element.140) | copy-start | bytes 1572868
  357.0 2.7 copy-start.2
  357.8 3.1 copy-start.10
  357.8 3.7 copy-start.4
  359.7 2.5 copy-start.9
  359.7 3.1 copy-start.1
  362.8 1.3 copy-start.8
  362.8 2.4 copy-start
  365.2 1.3 copy-start.7
  365.2 1.9 copy-start.6
  365.2 2.5 copy-start.5
